TPU v7x, 32 devices: a whole 2x2x4 slice. The times are simulated.
32 devices in a mesh: gx: 2 (over x), gy: 4 (over y, core), mode: 4 (over z).
Axes of the slice: x: 2, y: 2, z: 4, core: 2. Of those that a mesh axis runs over, the one named last changes fastest.
Arguments:
- e_init: float32 [3, 24, 32, 128], P(None, 'gx', 'gy'), may hold values from -6 to 6
- h_init: float32 [3, 24, 32, 128], P(None, 'gx', 'gy'), may hold values from -6 to 6
- eps_levels: float32 [3], replicated, may hold values from 1 to 4
- region_gain: float32 [3], replicated, may hold values from 0.5 to 2
- region_labels: int32 [24, 32, 128], P('gx', 'gy'), may hold values from 0 to 2
- kl_blocks: bfloat16 [16, 24, 32, 128], P('mode', 'gx', 'gy'), may hold values from -1.5 to 1.5
- kl_modes: int32 [16], replicated, may hold values from 0 to 3, as said below
- source_z: int32 [24, 32], P('gx', 'gy'), may hold values from 0 to 127
- source_amp: float32 [24, 32], P('gx', 'gy'), may hold values from -6 to 6
Outputs:
- tangent_e: float32 [4, 3, 24, 32, 128], P('mode', None, 'gx', 'gy')
- tangent_h: float32 [4, 3, 24, 32, 128], P('mode', None, 'gx', 'gy')
Inputs may be any that keep to these rules, and one draw needn't show every extreme that they name: `kl_modes`: each of the 4 modes is named by exactly 4 blocks.
All inputs are finite; a program needn't handle non-finite values.
Results may differ from a plain program's by a relative error of at most 0.00065.
Values may be sent and summed in bfloat16 or wider, within the bound.
No kernel may reach another device: no remote copies, remote signals or barrier semaphores. Data moves between devices by JAX's collectives and lax.ppermute only.
A program may use at most 64 MiB of HBM per device.

v0:
```python
import math

import jax
import jax.numpy as jnp
from jax import lax
from jax.sharding import PartitionSpec as P

STEPS = 10


DT_STEP = 0.99 / math.sqrt(3.0)
OMEGA_FREQ = 0.7


def shifted(block, axis, distance):
    devices = range(lax.axis_size(axis))
    route = [((i - distance) % len(devices), i) for i in devices]
    return lax.ppermute(block, axis, route)


def curl_forward(padded):
    center = padded[..., 1:-1, 1:-1, :]

    def along_x(component):
        return padded[..., component, 2:, 1:-1, :] - center[..., component, :, :, :]

    def along_y(component):
        return padded[..., component, 1:-1, 2:, :] - center[..., component, :, :, :]

    def along_z(component):
        values = center[..., component, :, :, :]
        return jnp.concatenate([values[..., 1:], jnp.zeros_like(values[..., :1])], -1) - values

    return jnp.stack(
        [along_y(2) - along_z(1), along_z(0) - along_x(2), along_x(1) - along_y(0)], -4
    )


def curl_backward(padded):
    center = padded[..., 1:-1, 1:-1, :]

    def along_x(component):
        return center[..., component, :, :, :] - padded[..., component, :-2, 1:-1, :]

    def along_y(component):
        return center[..., component, :, :, :] - padded[..., component, 1:-1, :-2, :]

    def along_z(component):
        values = center[..., component, :, :, :]
        return values - jnp.concatenate([jnp.zeros_like(values[..., :1]), values[..., :-1]], -1)

    return jnp.stack(
        [along_y(2) - along_z(1), along_z(0) - along_x(2), along_x(1) - along_y(0)], -4
    )


def advance(state, inv_eps, deps, profile, number, pad_electric, pad_magnetic):
    size_x, size_y, size_z = (state.shape[2], state.shape[3], state.shape[4])
    wave = math.cos(OMEGA_FREQ * (number + 0.5) * DT_STEP)
    electric = state[0:2]
    magnetic = state[2:4]
    padded_e = pad_electric(electric.reshape(6, size_x, size_y, size_z)).reshape(
        2, 3, size_x + 2, size_y + 2, size_z
    )
    magnetic = magnetic - DT_STEP * curl_forward(padded_e)
    padded_h = pad_magnetic(magnetic.reshape(6, size_x, size_y, size_z)).reshape(
        2, 3, size_x + 2, size_y + 2, size_z
    )
    curls = curl_backward(padded_h)
    zeros_field = jnp.zeros_like(profile)
    current = jnp.stack([zeros_field, zeros_field, profile * wave])
    drive = curls[0] + current
    e_base = electric[0] + DT_STEP * inv_eps * drive
    e_tangent = (
        electric[1] + DT_STEP * inv_eps * curls[1] - DT_STEP * deps * inv_eps * inv_eps * drive
    )
    return jnp.concatenate([jnp.stack([e_base, e_tangent]), magnetic], 0)


def pick_level(labels, table):
    return jnp.where(labels == 0, table[0], jnp.where(labels == 1, table[1], table[2]))


def body(
    e_init,
    h_init,
    eps_levels,
    region_gain,
    region_labels,
    kl_blocks,
    kl_modes,
    source_z,
    source_amp,
):
    my_mode = lax.axis_index("mode")
    inv_eps = 1.0 / pick_level(region_labels, eps_levels)
    gain_field = pick_level(region_labels, region_gain)
    gathered = lax.all_gather(kl_blocks, "mode", axis=0, tiled=True)
    select = (kl_modes == my_mode).astype(jnp.bfloat16)
    summed = jnp.einsum("k,kxyz->xyz", select, gathered, preferred_element_type=jnp.float32)
    deps = gain_field * summed
    heights = jnp.arange(region_labels.shape[2], dtype=jnp.int32)
    profile = jnp.where(heights[None, None, :] == source_z[:, :, None], source_amp[:, :, None], 0.0)
    zeros_tangent = jnp.zeros_like(e_init)
    state = jnp.stack([e_init, zeros_tangent, h_init, zeros_tangent])

    def pad_electric(field):
        upper_x = shifted(field[:, 0:1], "gx", -1)
        upper_y = shifted(field[:, :, 0:1], "gy", -1)
        empty_x = jnp.zeros_like(upper_x)
        wide_x = jnp.concatenate([empty_x, field, upper_x], 1)
        corner = jnp.zeros_like(upper_y[:, 0:1])
        column = jnp.concatenate([corner, upper_y, corner], 1)
        return jnp.concatenate([jnp.zeros_like(column), wide_x, column], 2)

    def pad_magnetic(field):
        lower_x = shifted(field[:, -1:], "gx", 1)
        lower_y = shifted(field[:, :, -1:], "gy", 1)
        empty_x = jnp.zeros_like(lower_x)
        wide_x = jnp.concatenate([lower_x, field, empty_x], 1)
        corner = jnp.zeros_like(lower_y[:, 0:1])
        column = jnp.concatenate([corner, lower_y, corner], 1)
        return jnp.concatenate([column, wide_x, jnp.zeros_like(column)], 2)

    for number in range(STEPS):
        state = advance(state, inv_eps, deps, profile, number, pad_electric, pad_magnetic)
    return (state[1][None], state[3][None])


def solution(mesh):
    placed = (
        P(None, "gx", "gy", None),
        P(None, "gx", "gy", None),
        P(),
        P(),
        P("gx", "gy", None),
        P("mode", "gx", "gy", None),
        P(),
        P("gx", "gy"),
        P("gx", "gy"),
    )
    return jax.shard_map(
        body,
        mesh=mesh,
        in_specs=placed,
        out_specs=(P("mode", None, "gx", "gy", None), P("mode", None, "gx", "gy", None)),
        check_vma=False,
    )
```

profile of v0, /device:TPU:0, one launch (start us, length us, event | category | flops | bytes accessed | tf_op | source)
XLA Modules:
  0.0 126.5 jit_solution(18275925089181558317)
XLA Ops:
  1.6 3.0 %collective-permute-start = (f32[6,1,8,128]{3,1,2,0:T(1,128)S(1)}, f32[6,1,8,128]{3,1,2,0:T(1,128)S(1)}, u32[]{:S(2)}, u32[]{:S(2)}) collective-permute-start(f32[6,1,8,128]{3,1,2,0:T(1,128)S(1)} %slice.1135), channel_id=1, source_target_pairs={{16,0},{0,16},{17,1},{1,17},{18,2},{2,18},{19,3},{3,19},{20,4},{4,... | collective-permute-start | bytes 73736 | tf_op jit(solution)/shard_map/ppermute | solution.py:18
  7.4 14.8 %all_gather.3 = bf16[16,12,8,128]{3,2,1,0:T(8,128)(2,1)S(1)} all-gather(bf16[4,12,8,128]{3,2,1,0:T(8,128)(2,1)S(1)} %copy-done.2), channel_id=1, replica_groups=mesh['gx'=2,'gy'=4,'mode'=4] {'mode'}, dimensions={0}, use_global_device_ids=true | all-gather | bytes 491520 | tf_op jit(solution)/shard_map/all_gather | solution.py:98
  23.6 1.9 %fusion.273 = (f32[12,8,128]{2,1,0:T(8,128)S(1)}, pred[12,8,128]{2,1,0:T(8,128)(4,1)S(1)}, pred[12,8,128]{2,1,0:T(8,128)(4,1)S(1)}) fusion(f32[]{:T(128)} %bitcast.2, f32[]{:T(128)} %bitcast.1, f32[]{:T(128)} %bitcast, s32[12,8,128]{2,1,0:T(8,128)S(1)} %copy-done.3), kind=kLoop, calls=%fused_computation.534 | loop fusion | flops 73728 | bytes 122892 | tf_op jit(solution)/shard_map/mul | solution.py:75
  28.4 3.9 %multiply_multiply_fusion = f32[12,8,128]{2,1,0:T(8,128)S(1)} fusion(f32[12,8,128]{2,1,0:T(8,128)S(1)} %bitcast.1356, pred[12,8,128]{2,1,0:T(8,128)(4,1)S(1)} %get-tuple-element.8, pred[12,8,128]{2,1,0:T(8,128)(4,1)S(1)} %get-tuple-element.7, f32[]{:T(128)} %bitcast.33, f32[]{:T(128)} %bitcast.32, f32[]{:T(128)} %bitcast.31, f32[]{:T(128)} %bitcast.2, ...), kind=kLoop, calls=%fused_computation.531 | loop fusion | flops 110592 | bytes 122904 | tf_op jit(solution)/shard_map/mul | solution.py:75
  33.8 1.8 %collective-permute-start.5 = (f32[6,12,1,128]{3,1,2,0:T(8,128)S(1)}, f32[6,12,1,128]{3,1,2,0:T(8,128)S(1)}, u32[]{:S(2)}, u32[]{:S(2)}) collective-permute-start(f32[6,12,1,128]{3,1,2,0:T(8,128)S(1)} %slice.1160), channel_id=1, source_target_pairs={{4,0},{8,4},{12,8},{0,12},{5,1},{9,5},{13,9},{1,13},{6,2},{10,6},{... | collective-permute-start | bytes 110600 | tf_op jit(solution)/shard_map/ppermute | solution.py:18
  37.1 2.3 %collective-permute-done.4 = f32[6,1,8,128]{3,1,2,0:T(1,128)S(1)} collective-permute-done((f32[6,1,8,128]{3,1,2,0:T(1,128)S(1)}, f32[6,1,8,128]{3,1,2,0:T(1,128)S(1)}, u32[]{:S(2)}, u32[]{:S(2)}) %collective-permute-start.4) | collective-permute-done | bytes 24608 | tf_op jit(solution)/shard_map/ppermute | solution.py:18
  40.4 1.6 %collective-permute-start.7 = (f32[6,1,8,128]{3,2,1,0:T(8,128)S(1)}, f32[6,1,8,128]{3,2,1,0:T(8,128)S(1)}, u32[]{:S(2)}, u32[]{:S(2)}) collective-permute-start(f32[6,1,8,128]{3,2,1,0:T(8,128)S(1)} %slice.1171), channel_id=1, source_target_pairs={{16,0},{0,16},{17,1},{1,17},{18,2},{2,18},{19,3},{3,19},{20,4},{4,... | collective-permute-start | bytes 73736 | tf_op jit(solution)/shard_map/ppermute | solution.py:18
  42.0 2.4 %collective-permute-done.7 = f32[6,1,8,128]{3,2,1,0:T(8,128)S(1)} collective-permute-done((f32[6,1,8,128]{3,2,1,0:T(8,128)S(1)}, f32[6,1,8,128]{3,2,1,0:T(8,128)S(1)}, u32[]{:S(2)}, u32[]{:S(2)}) %collective-permute-start.7) | collective-permute-done | bytes 24608 | tf_op jit(solution)/shard_map/ppermute | solution.py:18
  47.5 2.3 %collective-permute-done.8 = f32[6,1,8,128]{3,1,2,0:T(1,128)S(1)} collective-permute-done((f32[6,1,8,128]{3,1,2,0:T(1,128)S(1)}, f32[6,1,8,128]{3,1,2,0:T(1,128)S(1)}, u32[]{:S(2)}, u32[]{:S(2)}) %collective-permute-start.8) | collective-permute-done | bytes 24608 | tf_op jit(solution)/shard_map/ppermute | solution.py:18
  52.3 2.5 %collective-permute-done.11 = f32[6,1,8,128]{3,2,1,0:T(8,128)S(1)} collective-permute-done((f32[6,1,8,128]{3,2,1,0:T(8,128)S(1)}, f32[6,1,8,128]{3,2,1,0:T(8,128)S(1)}, u32[]{:S(2)}, u32[]{:S(2)}) %collective-permute-start.11) | collective-permute-done | bytes 24608 | tf_op jit(solution)/shard_map/ppermute | solution.py:18
  57.3 2.3 %collective-permute-done.12 = f32[6,1,8,128]{3,1,2,0:T(1,128)S(1)} collective-permute-done((f32[6,1,8,128]{3,1,2,0:T(1,128)S(1)}, f32[6,1,8,128]{3,1,2,0:T(1,128)S(1)}, u32[]{:S(2)}, u32[]{:S(2)}) %collective-permute-start.12) | collective-permute-done | bytes 24608 | tf_op jit(solution)/shard_map/ppermute | solution.py:18
  62.1 2.3 %collective-permute-done.15 = f32[6,1,8,128]{3,2,1,0:T(8,128)S(1)} collective-permute-done((f32[6,1,8,128]{3,2,1,0:T(8,128)S(1)}, f32[6,1,8,128]{3,2,1,0:T(8,128)S(1)}, u32[]{:S(2)}, u32[]{:S(2)}) %collective-permute-start.15) | collective-permute-done | bytes 24608 | tf_op jit(solution)/shard_map/ppermute | solution.py:18
  67.5 2.3 %collective-permute-done.16 = f32[6,1,8,128]{3,1,2,0:T(1,128)S(1)} collective-permute-done((f32[6,1,8,128]{3,1,2,0:T(1,128)S(1)}, f32[6,1,8,128]{3,1,2,0:T(1,128)S(1)}, u32[]{:S(2)}, u32[]{:S(2)}) %collective-permute-start.16) | collective-permute-done | bytes 24608 | tf_op jit(solution)/shard_map/ppermute | solution.py:18
  72.4 2.5 %collective-permute-done.19 = f32[6,1,8,128]{3,2,1,0:T(8,128)S(1)} collective-permute-done((f32[6,1,8,128]{3,2,1,0:T(8,128)S(1)}, f32[6,1,8,128]{3,2,1,0:T(8,128)S(1)}, u32[]{:S(2)}, u32[]{:S(2)}) %collective-permute-start.19) | collective-permute-done | bytes 24608 | tf_op jit(solution)/shard_map/ppermute | solution.py:18
  77.4 2.3 %collective-permute-done.20 = f32[6,1,8,128]{3,1,2,0:T(1,128)S(1)} collective-permute-done((f32[6,1,8,128]{3,1,2,0:T(1,128)S(1)}, f32[6,1,8,128]{3,1,2,0:T(1,128)S(1)}, u32[]{:S(2)}, u32[]{:S(2)}) %collective-permute-start.20) | collective-permute-done | bytes 24608 | tf_op jit(solution)/shard_map/ppermute | solution.py:18
  82.3 2.3 %collective-permute-done.23 = f32[6,1,8,128]{3,2,1,0:T(8,128)S(1)} collective-permute-done((f32[6,1,8,128]{3,2,1,0:T(8,128)S(1)}, f32[6,1,8,128]{3,2,1,0:T(8,128)S(1)}, u32[]{:S(2)}, u32[]{:S(2)}) %collective-permute-start.23) | collective-permute-done | bytes 24608 | tf_op jit(solution)/shard_map/ppermute | solution.py:18
  87.7 2.3 %collective-permute-done.24 = f32[6,1,8,128]{3,1,2,0:T(1,128)S(1)} collective-permute-done((f32[6,1,8,128]{3,1,2,0:T(1,128)S(1)}, f32[6,1,8,128]{3,1,2,0:T(1,128)S(1)}, u32[]{:S(2)}, u32[]{:S(2)}) %collective-permute-start.24) | collective-permute-done | bytes 24608 | tf_op jit(solution)/shard_map/ppermute | solution.py:18
  92.6 2.5 %collective-permute-done.27 = f32[6,1,8,128]{3,2,1,0:T(8,128)S(1)} collective-permute-done((f32[6,1,8,128]{3,2,1,0:T(8,128)S(1)}, f32[6,1,8,128]{3,2,1,0:T(8,128)S(1)}, u32[]{:S(2)}, u32[]{:S(2)}) %collective-permute-start.27) | collective-permute-done | bytes 24608 | tf_op jit(solution)/shard_map/ppermute | solution.py:18
  97.8 2.3 %collective-permute-done.28 = f32[6,1,8,128]{3,1,2,0:T(1,128)S(1)} collective-permute-done((f32[6,1,8,128]{3,1,2,0:T(1,128)S(1)}, f32[6,1,8,128]{3,1,2,0:T(1,128)S(1)}, u32[]{:S(2)}, u32[]{:S(2)}) %collective-permute-start.28) | collective-permute-done | bytes 24608 | tf_op jit(solution)/shard_map/ppermute | solution.py:18
  102.7 2.3 %collective-permute-done.31 = f32[6,1,8,128]{3,2,1,0:T(8,128)S(1)} collective-permute-done((f32[6,1,8,128]{3,2,1,0:T(8,128)S(1)}, f32[6,1,8,128]{3,2,1,0:T(8,128)S(1)}, u32[]{:S(2)}, u32[]{:S(2)}) %collective-permute-start.31) | collective-permute-done | bytes 24608 | tf_op jit(solution)/shard_map/ppermute | solution.py:18
  108.1 2.3 %collective-permute-done.32 = f32[6,1,8,128]{3,1,2,0:T(1,128)S(1)} collective-permute-done((f32[6,1,8,128]{3,1,2,0:T(1,128)S(1)}, f32[6,1,8,128]{3,1,2,0:T(1,128)S(1)}, u32[]{:S(2)}, u32[]{:S(2)}) %collective-permute-start.32) | collective-permute-done | bytes 24608 | tf_op jit(solution)/shard_map/ppermute | solution.py:18
  113.1 2.5 %collective-permute-done.35 = f32[6,1,8,128]{3,2,1,0:T(8,128)S(1)} collective-permute-done((f32[6,1,8,128]{3,2,1,0:T(8,128)S(1)}, f32[6,1,8,128]{3,2,1,0:T(8,128)S(1)}, u32[]{:S(2)}, u32[]{:S(2)}) %collective-permute-start.35) | collective-permute-done | bytes 24608 | tf_op jit(solution)/shard_map/ppermute | solution.py:18
  118.1 2.3 %collective-permute-done.36 = f32[6,1,8,128]{3,1,2,0:T(1,128)S(1)} collective-permute-done((f32[6,1,8,128]{3,1,2,0:T(1,128)S(1)}, f32[6,1,8,128]{3,1,2,0:T(1,128)S(1)}, u32[]{:S(2)}, u32[]{:S(2)}) %collective-permute-start.36) | collective-permute-done | bytes 24608 | tf_op jit(solution)/shard_map/ppermute | solution.py:18
  123.8 1.7 %collective-permute-done.39 = f32[6,1,8,128]{3,2,1,0:T(8,128)S(1)} collective-permute-done((f32[6,1,8,128]{3,2,1,0:T(8,128)S(1)}, f32[6,1,8,128]{3,2,1,0:T(8,128)S(1)}, u32[]{:S(2)}, u32[]{:S(2)}) %collective-permute-start.39) | collective-permute-done | bytes 24608 | tf_op jit(solution)/shard_map/ppermute | solution.py:18
  (279 shorter events, 55.6 us)
Async XLA Ops:
  1.6 24.5 %collective-permute-start = (f32[6,1,8,128]{3,1,2,0:T(1,128)S(1)}, f32[6,1,8,128]{3,1,2,0:T(1,128)S(1)}, u32[]{:S(2)}, u32[]{:S(2)}) collective-permute-start(f32[6,1,8,128]{3,1,2,0:T(1,128)S(1)} %slice.1135), channel_id=1, source_target_pairs={{16,0},{0,16},{17,1},{1,17},{18,2},{2,18},{19,3},{3,19},{20,4},{4,... | collective-permute-start | bytes 73736 | tf_op jit(solution)/shard_map/ppermute | solution.py:18
  4.7 21.5 %collective-permute-start.1 = (f32[6,12,1,128]{3,1,2,0:T(8,128)S(1)}, f32[6,12,1,128]{3,1,2,0:T(8,128)S(1)}, u32[]{:S(2)}, u32[]{:S(2)}) collective-permute-start(f32[6,12,1,128]{3,1,2,0:T(8,128)S(1)} %slice.1136), channel_id=1, source_target_pairs={{4,0},{8,4},{12,8},{0,12},{5,1},{9,5},{13,9},{1,13},{6,2},{10,6},{... | collective-permute-start | bytes 110600 | tf_op jit(solution)/shard_map/ppermute | solution.py:18
  27.8 4.6 %collective-permute-start.3 = (f32[6,1,8,128]{3,2,1,0:T(8,128)S(1)}, f32[6,1,8,128]{3,2,1,0:T(8,128)S(1)}, u32[]{:S(2)}, u32[]{:S(2)}) collective-permute-start(f32[6,1,8,128]{3,2,1,0:T(8,128)S(1)} %slice.1147), channel_id=1, source_target_pairs={{16,0},{0,16},{17,1},{1,17},{18,2},{2,18},{19,3},{3,19},{20,4},{4,... | collective-permute-start | bytes 73736 | tf_op jit(solution)/shard_map/ppermute | solution.py:18
  28.4 4.0 %collective-permute-start.2 = (f32[6,12,1,128]{3,2,1,0:T(1,128)S(1)}, f32[6,12,1,128]{3,2,1,0:T(1,128)S(1)}, u32[]{:S(2)}, u32[]{:S(2)}) collective-permute-start(f32[6,12,1,128]{3,2,1,0:T(1,128)S(1)} %slice.1146), channel_id=1, source_target_pairs={{12,0},{0,4},{4,8},{8,12},{13,1},{1,5},{5,9},{9,13},{14,2},{2,6},{... | collective-permute-start | bytes 110600 | tf_op jit(solution)/shard_map/ppermute | solution.py:18
  33.8 5.7 %collective-permute-start.5 = (f32[6,12,1,128]{3,1,2,0:T(8,128)S(1)}, f32[6,12,1,128]{3,1,2,0:T(8,128)S(1)}, u32[]{:S(2)}, u32[]{:S(2)}) collective-permute-start(f32[6,12,1,128]{3,1,2,0:T(8,128)S(1)} %slice.1160), channel_id=1, source_target_pairs={{4,0},{8,4},{12,8},{0,12},{5,1},{9,5},{13,9},{1,13},{6,2},{10,6},{... | collective-permute-start | bytes 110600 | tf_op jit(solution)/shard_map/ppermute | solution.py:18
  40.3 4.1 %collective-permute-start.6 = (f32[6,12,1,128]{3,2,1,0:T(1,128)S(1)}, f32[6,12,1,128]{3,2,1,0:T(1,128)S(1)}, u32[]{:S(2)}, u32[]{:S(2)}) collective-permute-start(f32[6,12,1,128]{3,2,1,0:T(1,128)S(1)} %slice.1170), channel_id=1, source_target_pairs={{12,0},{0,4},{4,8},{8,12},{13,1},{1,5},{5,9},{9,13},{14,2},{2,6},{... | collective-permute-start | bytes 110600 | tf_op jit(solution)/shard_map/ppermute | solution.py:18
  44.9 4.9 %collective-permute-start.9 = (f32[6,12,1,128]{3,1,2,0:T(8,128)S(1)}, f32[6,12,1,128]{3,1,2,0:T(8,128)S(1)}, u32[]{:S(2)}, u32[]{:S(2)}) collective-permute-start(f32[6,12,1,128]{3,1,2,0:T(8,128)S(1)} %slice.1184), channel_id=1, source_target_pairs={{4,0},{8,4},{12,8},{0,12},{5,1},{9,5},{13,9},{1,13},{6,2},{10,6},{... | collective-permute-start | bytes 110600 | tf_op jit(solution)/shard_map/ppermute | solution.py:18
  50.7 4.1 %collective-permute-start.10 = (f32[6,12,1,128]{3,2,1,0:T(1,128)S(1)}, f32[6,12,1,128]{3,2,1,0:T(1,128)S(1)}, u32[]{:S(2)}, u32[]{:S(2)}) collective-permute-start(f32[6,12,1,128]{3,2,1,0:T(1,128)S(1)} %slice.1194), channel_id=1, source_target_pairs={{12,0},{0,4},{4,8},{8,12},{13,1},{1,5},{5,9},{9,13},{14,2},{2,6},{... | collective-permute-start | bytes 110600 | tf_op jit(solution)/shard_map/ppermute | solution.py:18
  50.7 4.0 %collective-permute-start.11 = (f32[6,1,8,128]{3,2,1,0:T(8,128)S(1)}, f32[6,1,8,128]{3,2,1,0:T(8,128)S(1)}, u32[]{:S(2)}, u32[]{:S(2)}) collective-permute-start(f32[6,1,8,128]{3,2,1,0:T(8,128)S(1)} %slice.1195), channel_id=1, source_target_pairs={{16,0},{0,16},{17,1},{1,17},{18,2},{2,18},{19,3},{3,19},{20,4},{4,... | collective-permute-start | bytes 73736 | tf_op jit(solution)/shard_map/ppermute | solution.py:18
  55.2 4.4 %collective-permute-start.13 = (f32[6,12,1,128]{3,1,2,0:T(8,128)S(1)}, f32[6,12,1,128]{3,1,2,0:T(8,128)S(1)}, u32[]{:S(2)}, u32[]{:S(2)}) collective-permute-start(f32[6,12,1,128]{3,1,2,0:T(8,128)S(1)} %slice.1208), channel_id=1, source_target_pairs={{4,0},{8,4},{12,8},{0,12},{5,1},{9,5},{13,9},{1,13},{6,2},{10,6},{... | collective-permute-start | bytes 110600 | tf_op jit(solution)/shard_map/ppermute | solution.py:18
  65.0 4.9 %collective-permute-start.17 = (f32[6,12,1,128]{3,1,2,0:T(8,128)S(1)}, f32[6,12,1,128]{3,1,2,0:T(8,128)S(1)}, u32[]{:S(2)}, u32[]{:S(2)}) collective-permute-start(f32[6,12,1,128]{3,1,2,0:T(8,128)S(1)} %slice.1232), channel_id=1, source_target_pairs={{4,0},{8,4},{12,8},{0,12},{5,1},{9,5},{13,9},{1,13},{6,2},{10,6},{... | collective-permute-start | bytes 110600 | tf_op jit(solution)/shard_map/ppermute | solution.py:18
  70.8 4.1 %collective-permute-start.18 = (f32[6,12,1,128]{3,2,1,0:T(1,128)S(1)}, f32[6,12,1,128]{3,2,1,0:T(1,128)S(1)}, u32[]{:S(2)}, u32[]{:S(2)}) collective-permute-start(f32[6,12,1,128]{3,2,1,0:T(1,128)S(1)} %slice.1242), channel_id=1, source_target_pairs={{12,0},{0,4},{4,8},{8,12},{13,1},{1,5},{5,9},{9,13},{14,2},{2,6},{... | collective-permute-start | bytes 110600 | tf_op jit(solution)/shard_map/ppermute | solution.py:18
  70.8 4.0 %collective-permute-start.19 = (f32[6,1,8,128]{3,2,1,0:T(8,128)S(1)}, f32[6,1,8,128]{3,2,1,0:T(8,128)S(1)}, u32[]{:S(2)}, u32[]{:S(2)}) collective-permute-start(f32[6,1,8,128]{3,2,1,0:T(8,128)S(1)} %slice.1243), channel_id=1, source_target_pairs={{16,0},{0,16},{17,1},{1,17},{18,2},{2,18},{19,3},{3,19},{20,4},{4,... | collective-permute-start | bytes 73736 | tf_op jit(solution)/shard_map/ppermute | solution.py:18
  75.4 4.4 %collective-permute-start.21 = (f32[6,12,1,128]{3,1,2,0:T(8,128)S(1)}, f32[6,12,1,128]{3,1,2,0:T(8,128)S(1)}, u32[]{:S(2)}, u32[]{:S(2)}) collective-permute-start(f32[6,12,1,128]{3,1,2,0:T(8,128)S(1)} %slice.1256), channel_id=1, source_target_pairs={{4,0},{8,4},{12,8},{0,12},{5,1},{9,5},{13,9},{1,13},{6,2},{10,6},{... | collective-permute-start | bytes 110600 | tf_op jit(solution)/shard_map/ppermute | solution.py:18
  85.1 4.9 %collective-permute-start.25 = (f32[6,12,1,128]{3,1,2,0:T(8,128)S(1)}, f32[6,12,1,128]{3,1,2,0:T(8,128)S(1)}, u32[]{:S(2)}, u32[]{:S(2)}) collective-permute-start(f32[6,12,1,128]{3,1,2,0:T(8,128)S(1)} %slice.1280), channel_id=1, source_target_pairs={{4,0},{8,4},{12,8},{0,12},{5,1},{9,5},{13,9},{1,13},{6,2},{10,6},{... | collective-permute-start | bytes 110600 | tf_op jit(solution)/shard_map/ppermute | solution.py:18
  91.0 4.1 %collective-permute-start.26 = (f32[6,12,1,128]{3,2,1,0:T(1,128)S(1)}, f32[6,12,1,128]{3,2,1,0:T(1,128)S(1)}, u32[]{:S(2)}, u32[]{:S(2)}) collective-permute-start(f32[6,12,1,128]{3,2,1,0:T(1,128)S(1)} %slice.1290), channel_id=1, source_target_pairs={{12,0},{0,4},{4,8},{8,12},{13,1},{1,5},{5,9},{9,13},{14,2},{2,6},{... | collective-permute-start | bytes 110600 | tf_op jit(solution)/shard_map/ppermute | solution.py:18
  91.1 4.0 %collective-permute-start.27 = (f32[6,1,8,128]{3,2,1,0:T(8,128)S(1)}, f32[6,1,8,128]{3,2,1,0:T(8,128)S(1)}, u32[]{:S(2)}, u32[]{:S(2)}) collective-permute-start(f32[6,1,8,128]{3,2,1,0:T(8,128)S(1)} %slice.1291), channel_id=1, source_target_pairs={{16,0},{0,16},{17,1},{1,17},{18,2},{2,18},{19,3},{3,19},{20,4},{4,... | collective-permute-start | bytes 73736 | tf_op jit(solution)/shard_map/ppermute | solution.py:18
  95.6 4.5 %collective-permute-start.29 = (f32[6,12,1,128]{3,1,2,0:T(8,128)S(1)}, f32[6,12,1,128]{3,1,2,0:T(8,128)S(1)}, u32[]{:S(2)}, u32[]{:S(2)}) collective-permute-start(f32[6,12,1,128]{3,1,2,0:T(8,128)S(1)} %slice.1304), channel_id=1, source_target_pairs={{4,0},{8,4},{12,8},{0,12},{5,1},{9,5},{13,9},{1,13},{6,2},{10,6},{... | collective-permute-start | bytes 110600 | tf_op jit(solution)/shard_map/ppermute | solution.py:18
  101.1 4.0 %collective-permute-start.30 = (f32[6,12,1,128]{3,2,1,0:T(1,128)S(1)}, f32[6,12,1,128]{3,2,1,0:T(1,128)S(1)}, u32[]{:S(2)}, u32[]{:S(2)}) collective-permute-start(f32[6,12,1,128]{3,2,1,0:T(1,128)S(1)} %slice.1314), channel_id=1, source_target_pairs={{12,0},{0,4},{4,8},{8,12},{13,1},{1,5},{5,9},{9,13},{14,2},{2,6},{... | collective-permute-start | bytes 110600 | tf_op jit(solution)/shard_map/ppermute | solution.py:18
  105.6 4.9 %collective-permute-start.33 = (f32[6,12,1,128]{3,1,2,0:T(8,128)S(1)}, f32[6,12,1,128]{3,1,2,0:T(8,128)S(1)}, u32[]{:S(2)}, u32[]{:S(2)}) collective-permute-start(f32[6,12,1,128]{3,1,2,0:T(8,128)S(1)} %slice.1328), channel_id=1, source_target_pairs={{4,0},{8,4},{12,8},{0,12},{5,1},{9,5},{13,9},{1,13},{6,2},{10,6},{... | collective-permute-start | bytes 110600 | tf_op jit(solution)/shard_map/ppermute | solution.py:18
  111.5 4.1 %collective-permute-start.34 = (f32[6,12,1,128]{3,2,1,0:T(1,128)S(1)}, f32[6,12,1,128]{3,2,1,0:T(1,128)S(1)}, u32[]{:S(2)}, u32[]{:S(2)}) collective-permute-start(f32[6,12,1,128]{3,2,1,0:T(1,128)S(1)} %slice.1338), channel_id=1, source_target_pairs={{12,0},{0,4},{4,8},{8,12},{13,1},{1,5},{5,9},{9,13},{14,2},{2,6},{... | collective-permute-start | bytes 110600 | tf_op jit(solution)/shard_map/ppermute | solution.py:18
  111.6 4.0 %collective-permute-start.35 = (f32[6,1,8,128]{3,2,1,0:T(8,128)S(1)}, f32[6,1,8,128]{3,2,1,0:T(8,128)S(1)}, u32[]{:S(2)}, u32[]{:S(2)}) collective-permute-start(f32[6,1,8,128]{3,2,1,0:T(8,128)S(1)} %slice.1339), channel_id=1, source_target_pairs={{16,0},{0,16},{17,1},{1,17},{18,2},{2,18},{19,3},{3,19},{20,4},{4,... | collective-permute-start | bytes 73736 | tf_op jit(solution)/shard_map/ppermute | solution.py:18
  116.1 4.4 %collective-permute-start.37 = (f32[6,12,1,128]{3,1,2,0:T(8,128)S(1)}, f32[6,12,1,128]{3,1,2,0:T(8,128)S(1)}, u32[]{:S(2)}, u32[]{:S(2)}) collective-permute-start(f32[6,12,1,128]{3,1,2,0:T(8,128)S(1)} %slice.1352), channel_id=1, source_target_pairs={{4,0},{8,4},{12,8},{0,12},{5,1},{9,5},{13,9},{1,13},{6,2},{10,6},{... | collective-permute-start | bytes 110600 | tf_op jit(solution)/shard_map/ppermute | solution.py:18
  121.5 4.0 %collective-permute-start.38 = (f32[6,12,1,128]{3,2,1,0:T(1,128)S(1)}, f32[6,12,1,128]{3,2,1,0:T(1,128)S(1)}, u32[]{:S(2)}, u32[]{:S(2)}) collective-permute-start(f32[6,12,1,128]{3,2,1,0:T(1,128)S(1)} %slice.1362), channel_id=1, source_target_pairs={{12,0},{0,4},{4,8},{8,12},{13,1},{1,5},{5,9},{9,13},{14,2},{2,6},{... | collective-permute-start | bytes 110600 | tf_op jit(solution)/shard_map/ppermute | solution.py:18
  (25 other events, 76.7 us)
where the time goes:
time: 127 us; the launch traced here: 126 us
  waiting for transfers between devices  42 us (33%)
  starting transfers between devices  40.6 us (32%)
  other arithmetic  15.8 us (12%)
  blocking collectives  14.8 us (12%)
  local copies, waits for them, and re-layouts  11.1 us (9%)
  between operations  2.06 us (2%)
    ppermute x40, waiting for transfers between devices, shifted(): return lax.ppermute(block, axis, route)  42 us
    ppermute x40, starting transfers between devices, shifted(): return lax.ppermute(block, axis, route)  40.6 us
    all_gather x1, blocking collectives, body(): gathered = lax.all_gather(kl_blocks, 'mode', axis=0, tiled=True)  14.8 us
    unnamed x30, local copies, waits for them, and re-layouts  5.44 us
    mul x1, other arithmetic, advance(): DT_STEP * deps * inv_eps * inv_eps * drive  3.89 us
  transfers between devices with their start and end apart: 40, of which 18 were waited for; matrix products, arithmetic and copies ran while one was open for 7% of the time, Pallas kernels for 0%

commit v1 on v0

v1 whole, which is shorter than its diff:
```python
import functools
import math

import jax
import jax.numpy as jnp
from jax import lax
from jax.experimental import pallas as pl
from jax.experimental.pallas import tpu as pltpu
from jax.sharding import PartitionSpec as P

STEPS = 10
DT_STEP = 0.99 / math.sqrt(3.0)
OMEGA_FREQ = 0.7

GROUP = 4
TILE = 8
FULL = 32000.0
FINE = 256.0
F32 = jnp.float32
VMEM_LIMIT = 48 * 1024 * 1024


def iota(axis, rows=TILE):
    return lax.broadcasted_iota(jnp.int32, (rows, 128), axis)


def scale_code(largest):
    return jnp.clip(jnp.ceil(jnp.log2(largest) * FINE) + 1.0, -FULL, FULL)


def to_codes(values, code):
    return jnp.round(values * (jnp.exp2(code * (-1.0 / FINE)) * FULL))


def scale_of(code):
    return jnp.exp2(code * (1.0 / FINE)) * (1.0 / FULL)


def narrow(tiles):
    return jnp.concatenate(tiles, 0).astype(jnp.int32).astype(jnp.int16)


def wide(codes):
    return codes.astype(jnp.int32).astype(F32)


def lane(tile, at):
    return jnp.broadcast_to(tile[:, at : at + 1], tile.shape)


def pack_kernel(
    size, me, modes, e, h, labels, kl, source_z, source_amp,
    packed, own, own_part, *rest,
):
    nx, ny = size
    parts, (label_rows, z_rows, amp_rows) = rest[:-3], rest[-3:]
    ratio, plane, stride = nx // GROUP, nx * ny, nx // GROUP * ny
    label_rows[:plane] = labels[...].astype(F32)
    label_rows[plane:] = jnp.zeros((plane, 128), F32)
    z_rows[...] = jnp.zeros(z_rows.shape, F32)
    amp_rows[...] = jnp.zeros(amp_rows.shape, F32)
    z_rows[nx:, :ny] = source_z[...].astype(F32)
    amp_rows[nx:, :ny] = source_amp[...]
    low, lanes = iota(0) < GROUP, iota(1)

    blocks = kl.shape[0] // plane
    rows16 = iota(0, 16)
    weights = [
        [(modes[me[0] * blocks + j] == (me[0] ^ d)).astype(F32) for j in range(blocks)]
        for d in range(len(parts) + 1)
    ]
    codes = [jnp.zeros((16, 128), F32) for _ in parts]
    for k in range(plane // 16):
        tiles = [kl[j * plane + 16 * k : j * plane + 16 * k + 16].astype(F32) for j in range(blocks)]
        for d in range(len(parts) + 1):
            total = sum(weights[d][j] * tiles[j] for j in range(blocks))
            if d == 0:
                own_part[16 * k : 16 * k + 16] = total
                continue
            halves = []
            for i in range(2):
                half = total[TILE * i : TILE * i + TILE]
                code = scale_code(jnp.max(jnp.abs(half), axis=(0, 1), keepdims=True))
                halves.append(to_codes(half, code))
                codes[d - 1] = jnp.where(rows16 == 2 * k + i, code, codes[d - 1])
            parts[d - 1][16 * k : 16 * k + 16] = narrow(halves)
    for d, part in enumerate(parts):
        part[plane:] = narrow([codes[d]])

    for y in range(ny):
        for r in range(ratio):
            at = r * ny + y
            tiles = [e[pl.ds(at, TILE, stride=stride)], h[pl.ds(at, TILE, stride=stride)]]
            e_last = e[pl.ds(at + plane, TILE, stride=stride)]
            h_last = h[pl.ds(at + plane, TILE, stride=stride)]
            tiles.append(jnp.where(low, pltpu.roll(e_last, GROUP, 0), h_last))
            label = label_rows[pl.ds(at, TILE, stride=stride)]
            height = lane(z_rows[pl.ds(r, TILE, stride=ratio)], y)
            amp = lane(amp_rows[pl.ds(r, TILE, stride=ratio)], y)
            coded, meta = [], jnp.zeros((TILE, 128), F32)
            for i, tile in enumerate(tiles):
                code = scale_code(jnp.broadcast_to(jnp.max(jnp.abs(tile), axis=1, keepdims=True), tile.shape))
                coded.append(to_codes(tile, code))
                meta = jnp.where(lanes == 2 * i, pltpu.roll(code, GROUP, 0), meta)
                meta = jnp.where(lanes == 2 * i + 1, code, meta)
            meta = jnp.where(lanes == 6, height, meta)
            amp_code = scale_code(jnp.abs(amp))
            meta = jnp.where(lanes == 7, to_codes(amp, amp_code), meta)
            meta = jnp.where(lanes == 8, amp_code, meta)
            own_meta = jnp.where(lanes == 6, height, jnp.where(lanes == 7, amp, 0.0))
            coded.append(jnp.where(low, label, meta))
            tiles.append(jnp.where(low, label, own_meta))
            base = (y * ratio + r) * 32
            packed[base : base + 16] = narrow(coded[:2])
            packed[base + 16 : base + 32] = narrow(coded[2:])
            for i, tile in enumerate(tiles):
                own[base + TILE * i : base + TILE * i + TILE] = tile


def sum_kernel(size, own_part, *rest):
    nx, ny = size
    parts, (packed, own, total) = rest[:-3], rest[-3:]
    ratio, plane, stride = nx // GROUP, nx * ny, nx // GROUP * ny
    scales = [scale_of(wide(part[plane : plane + 16])) for part in parts]
    total[:plane] = jnp.zeros((plane, 128), F32)
    total[2 * plane :] = jnp.zeros((plane, 128), F32)
    for k in range(plane // 16):
        coded = [wide(part[16 * k : 16 * k + 16]) for part in parts]
        for i in range(2):
            at = 16 * k + TILE * i
            tile = own_part[at : at + TILE]
            for c, s in zip(coded, scales):
                tile = tile + c[TILE * i : TILE * i + TILE] * s[2 * k + i : 2 * k + i + 1]
            total[plane + at : plane + at + TILE] = tile
    low, rows16 = iota(0) < GROUP, iota(0, 16)
    codes = jnp.zeros((16, 128), F32)
    held = []
    for pair in range(ny // 2):
        for r in range(ratio):
            at = r * ny + 2 * pair
            even = total[pl.ds(plane + at, TILE, stride=stride)]
            odd = total[pl.ds(at + 1, TILE, stride=stride)]
            tile = jnp.where(low, even, odd)
            unit = pair * ratio + r
            own[TILE * unit : TILE * unit + TILE] = tile
            code = scale_code(jnp.max(jnp.abs(tile), axis=(0, 1), keepdims=True))
            codes = jnp.where(rows16 == unit, code, codes)
            held.append(to_codes(tile, code))
            if len(held) == 2:
                packed[TILE * (unit - 1) : TILE * (unit + 1)] = narrow(held)
                held = []
    packed[plane:] = narrow([codes])


def x_up(tiles):
    rows = tiles[0].shape[0]
    return tiles[1:] + [pltpu.roll(tiles[0], rows - 1, 0)]


def x_down(tiles):
    return [pltpu.roll(tiles[-1], 1, 0)] + tiles[:-1]


def z_up(tiles):
    last = iota(1, tiles[0].shape[0]) == 127
    return [jnp.where(last, 0.0, pltpu.roll(t, 127, 1)) for t in tiles]


def z_down(tiles):
    first = iota(1, tiles[0].shape[0]) == 0
    return [jnp.where(first, 0.0, pltpu.roll(t, 1, 1)) for t in tiles]


def add_curl_forward(magnetic, now, above):
    ex, ey, ez = now
    above_x, _, above_z = above
    ups = (z_up(ex), z_up(ey), x_up(ey), x_up(ez))
    out = [[], [], []]
    for r in range(len(ex)):
        curl = (
            (above_z[r] - ez[r]) - (ups[1][r] - ey[r]),
            (ups[0][r] - ex[r]) - (ups[3][r] - ez[r]),
            (ups[2][r] - ey[r]) - (above_x[r] - ex[r]),
        )
        for c in range(3):
            out[c].append(-curl[c] if magnetic is None else magnetic[c][r] - curl[c])
    return out


def curl_backward(now, below_x, below_z):
    hx, hy, hz = now
    downs = (z_down(hx), z_down(hy), x_down(hy), x_down(hz))
    out = [[], [], []]
    for r in range(len(hx)):
        out[0].append((hz[r] - below_z[r]) - (hy[r] - downs[1][r]))
        out[1].append((hx[r] - downs[0][r]) - (hz[r] - downs[3][r]))
        out[2].append((hy[r] - downs[2][r]) - (hx[r] - below_x[r]))
    return out


def load_row(ref, at, ratio):
    return [[ref[at, c * ratio + r] for r in range(ratio)] for c in range(3)]


def store_row(ref, at, row):
    ratio = len(row[0])
    for c in range(3):
        for r in range(ratio):
            ref[at, c * ratio + r] = row[c][r]


def flat(row):
    return [t for tiles in row for t in tiles]


def rows_of(step, ny):
    return step + 1, ny + 2 * STEPS - 1 - step


def sweep(first, end, carry, body):
    assert (end - first) % 2 == 0

    def two(i, held):
        at = first + 2 * i
        return body(at + 1, body(at, held))

    return lax.fori_loop(0, (end - first) // 2, two, carry)


def places(parity, ny):
    upper, lower = STEPS + ny, STEPS - ny
    one = jnp.where(parity == 0, upper, lower)
    three = jnp.where(parity == 0, lower, upper)
    over = STEPS - ny
    return (
        ((0, ny, STEPS),),
        ((0, ny, one),),
        ((ny - over, over, 0), (0, over, STEPS + 2 * ny)),
        ((0, ny, three),),
    )


def halves(pairs, low):
    one, two = pairs
    return [
        jnp.where(low, one, pltpu.roll(two, GROUP, 0)),
        jnp.where(low, pltpu.roll(one, GROUP, 0), two),
    ]


def base_kernel(size, order, parity, levels, gains, own, *rest):
    nx, ny = size
    ratio = nx // GROUP
    blocks, (coef, gain_out, moves, electric, magnetic, profile) = rest[:-6], rest[-6:]
    blocks = (own,) + blocks
    low, lanes = iota(0) < GROUP, iota(1)

    def pick(label, table):
        return jnp.where(label < 0.5, table[0], jnp.where(label < 1.5, table[1], table[2]))

    def unpack(y_block, y, to):
        for r in range(ratio):
            base = pl.multiple_of((y * ratio + r) * 32, 32)
            outs = []
            for first in range(0, len(order), 2):
                pair, owned = [], []
                for x_block in order[first : first + 2]:
                    ref = blocks[4 * x_block + y_block]
                    owned.append(x_block == 0 and y_block == 0)
                    if owned[-1]:
                        pair.append([ref[pl.ds(base + TILE * i, TILE)] for i in range(4)])
                    else:
                        both = [wide(ref[pl.ds(base + 16 * i, 16)]) for i in range(2)]
                        pair.append([b[TILE * i : TILE * i + TILE] for b in both for i in range(2)])
                planes = [p for i in range(4) for p in halves((pair[0][i], pair[1][i]), low)]
                meta = planes[7]
                scale = scale_of(meta)
                mine = low if owned[0] else jnp.logical_not(low)

                def scaled(value, at):
                    factor = lane(scale, at)
                    return value * (jnp.where(mine, 1.0, factor) if any(owned) else factor)

                fields = [scaled(planes[i], i) for i in range(6)]
                amp = scaled(lane(meta, 7), 8)
                inv_eps = 1.0 / pick(planes[6], levels)
                outs.append(
                    [fields[i] * DT_STEP for i in (0, 1, 4)]
                    + [fields[i] for i in (2, 3, 5)]
                    + [
                        DT_STEP * DT_STEP * inv_eps,
                        pick(planes[6], gains) * inv_eps,
                        jnp.where(lanes.astype(F32) == lane(meta, 6), amp, 0.0),
                    ]
                )
            for i in range(9):
                tile = jnp.concatenate([o[i] for o in outs], 0) if len(outs) > 1 else outs[0][i]
                if i < 3:
                    electric[to, i * ratio + r] = tile
                elif i < 6:
                    magnetic[to, (i - 3) * ratio + r] = tile
                else:
                    (coef, gain_out, profile)[i - 6][to, r] = tile

    for y_block, pieces in enumerate(places(parity[0], ny)):
        for first, count, to in pieces:

            def some(j, _, y_block=y_block, first=first, to=to):
                unpack(y_block, first + j, to + j)
                return 0

            lax.fori_loop(0, count, some, 0)

    moved = 0
    for step in range(STEPS):
        wave = math.cos(OMEGA_FREQ * (step + 0.5) * DT_STEP)
        first, end = rows_of(step, ny)
        now = load_row(electric, first - 1, ratio)
        above = load_row(electric, first, ratio)
        new = add_curl_forward(load_row(magnetic, first - 1, ratio), now, above)

        def row(at, held, step=step, wave=wave, shift=moved - first):
            now, below_x, below_z = held
            above = load_row(electric, at + 1, ratio)
            new = add_curl_forward(load_row(magnetic, at, ratio), now, above)
            if step < STEPS - 1:
                store_row(magnetic, at, new)
            drive = curl_backward(new, below_x, below_z)
            drive[2] = [d + wave * profile[at, r] for r, d in enumerate(drive[2])]
            change = [[coef[at, r] * drive[c][r] for r in range(ratio)] for c in range(3)]
            store_row(moves, at + shift, change)
            if step < STEPS - 1:
                store_row(electric, at, [[a + b for a, b in zip(now[c], change[c])] for c in range(3)])
            return above, new[0], new[2]

        sweep(first, end, (above, new[0], new[2]), row)
        moved += end - first


def tangent_kernel(size, order, parity, coef, gain, moves, own, *rest):
    nx, ny = size
    ratio, plane = nx // GROUP, nx * ny
    n_blocks = 4 * len(set(order)) - 1
    blocks, rest = (own,) + rest[:n_blocks], rest[n_blocks:]
    out_e, out_h, electric, magnetic, weight, moves_in, sems = rest
    low = iota(0) < GROUP

    copies, moved = [], 0
    for step in range(STEPS):
        first, end = rows_of(step, ny)
        there = pl.ds(moved, end - first)
        copies.append(pltpu.make_async_copy(moves.at[there], moves_in.at[there], sems.at[step]))
        moved += end - first
    for copy in copies:
        copy.start()

    scales = [None if i == 0 else scale_of(wide(b[plane : plane + 16])) for i, b in enumerate(blocks)]

    def unpack(y_block, pair, to, wanted):
        loaded = {}
        for x_block in order:
            i = 4 * x_block + y_block
            if x_block in loaded:
                continue
            tiles = []
            for r in range(ratio):
                unit = pair * ratio + r
                if i == 0:
                    tiles.append(own[TILE * unit : TILE * unit + TILE])
                else:
                    at = TILE * unit // 16 * 16
                    both = wide(blocks[i][at : at + 16])
                    half = TILE * unit - at
                    tiles.append(both[half : half + TILE] * scales[i][unit : unit + 1])
            loaded[x_block] = tiles
        for r in range(ratio):
            outs = [
                halves((loaded[order[k]][r], loaded[order[k + 1]][r]), low)
                for k in range(0, len(order), 2)
            ]
            for i in wanted:
                tile = jnp.concatenate([o[i] for o in outs], 0) if len(outs) > 1 else outs[0][i]
                weight[to + i, r] = tile * gain[to + i, r]

    for y_block, pieces in enumerate(places(parity[0], ny)):
        for first, count, to in pieces:
            for j in range(0, count, 2):
                unpack(y_block, (first + j) // 2, to + j, (0, 1))

    moved = 0
    for step in range(STEPS):
        first, end = rows_of(step, ny)
        copies[step].wait()
        shift = moved - first
        if step == 0:

            def start(at, held, shift=shift):
                change = load_row(moves_in, at + shift, ratio)
                store_row(electric, at, [[-(weight[at, r] * change[c][r]) for r in range(ratio)] for c in range(3)])
                return held

            sweep(first, end, 0, start)
        else:

            def old(at, step=step):
                return load_row(magnetic, at, ratio) if step > 1 else None

            now = load_row(electric, first - 1, ratio)
            above = load_row(electric, first, ratio)
            new = add_curl_forward(old(first - 1), now, above)

            def row(at, held, old=old, shift=shift):
                now, below_x, below_z = held
                above = load_row(electric, at + 1, ratio)
                new = add_curl_forward(old(at), now, above)
                store_row(magnetic, at, new)
                curl = curl_backward(new, below_x, below_z)
                change = load_row(moves_in, at + shift, ratio)
                store_row(
                    electric, at,
                    [[now[c][r] + (coef[at, r] * curl[c][r] - weight[at, r] * change[c][r]) for r in range(ratio)] for c in range(3)],
                )
                return above, new[0], new[2]

            sweep(first, end, (above, new[0], new[2]), row)
        moved += end - first

    at_own = GROUP * order.index(0)
    stride = ratio * ny
    for y in range(ny):
        for r in range(ratio):
            for out, ref, factor in ((out_e, electric, 1.0 / DT_STEP), (out_h, magnetic, None)):
                for c in range(3):
                    tile = ref[STEPS + y, c * ratio + r, at_own : at_own + GROUP]
                    out[pl.ds(c * plane + r * ny + y, GROUP, stride=stride)] = tile if factor is None else tile * factor


def call(kernel, name, outs, specs, scratch, flops, args, size_bytes):
    return pl.pallas_call(
        kernel,
        out_shape=outs,
        in_specs=specs,
        out_specs=tuple(pl.BlockSpec(memory_space=pltpu.VMEM) for _ in outs),
        scratch_shapes=scratch,
        compiler_params=pltpu.CompilerParams(vmem_limit_bytes=VMEM_LIMIT),
        cost_estimate=pl.CostEstimate(flops=flops, bytes_accessed=size_bytes, transcendentals=0),
        name=name,
    )(*args)


def body(sizes, e_init, h_init, eps_levels, region_gain, region_labels, kl_blocks, kl_modes, source_z, source_amp):
    n_gx, n_gy, n_mode = sizes
    _, nx, ny, nz = e_init.shape
    assert n_gy == 4 and nx % GROUP == 0 and nx >= STEPS and ny < STEPS < 2 * ny
    ratio, plane = nx // GROUP, nx * ny
    size = (nx, ny)
    vmem, smem, anywhere = (pl.BlockSpec(memory_space=s) for s in (pltpu.VMEM, pltpu.SMEM, pl.ANY))
    f32 = lambda *shape: jax.ShapeDtypeStruct(shape, F32)
    i16 = lambda *shape: jax.ShapeDtypeStruct(shape, jnp.int16)

    def over_xy(block, dx, flip):
        route = [
            (gx * n_gy + gy, (gx + dx) % n_gx * n_gy + (gy ^ flip))
            for gx in range(n_gx)
            for gy in range(n_gy)
        ]
        return lax.ppermute(block, ("gx", "gy"), route)

    def over_mode(block, flip):
        return lax.ppermute(block, "mode", [(i, i ^ flip) for i in range(n_mode)])

    me = lax.axis_index("mode").astype(jnp.int32).reshape(1)
    parity = (lax.axis_index("gy") % 2).astype(jnp.int32).reshape(1)
    packed, own, own_part, *parts = call(
        functools.partial(pack_kernel, size), "pack",
        (i16(ny * ratio * 32, nz), f32(ny * ratio * 32, nz), f32(plane, nz)) + (i16(plane + 16, nz),) * (n_mode - 1),
        [smem, smem] + [vmem] * 6,
        [pltpu.VMEM((2 * plane, nz), F32), pltpu.VMEM((2 * nx, 128), F32), pltpu.VMEM((2 * nx, 128), F32)],
        10**6,
        (
            me, kl_modes, e_init.reshape(-1, nz), h_init.reshape(-1, nz), region_labels.reshape(-1, nz),
            kl_blocks.reshape(-1, nz), source_z, source_amp,
        ),
        10**6,
    )

    moves_x = [0, -1] if n_gx == 2 else [0, -1, 1]
    order = (0, 1) if n_gx == 2 else (2, 0, 1, 1)
    groups = GROUP * len(order)

    def gather(block):
        near = [block] + [over_xy(block, dx, 0) for dx in moves_x[1:]]
        far = [over_xy(block, dx, 2) for dx in moves_x]
        return near, far

    near, far = gather(packed)
    parts = [over_mode(part, d + 1) for d, part in enumerate(parts)]

    def with_core(near, far):
        got = near[1:] + far
        sent = over_xy(jnp.concatenate(got, 0), 0, 1)
        rows = got[0].shape[0]
        first = over_xy(near[0], 0, 1)
        other = [first] + [sent[rows * i : rows * i + rows] for i in range(len(got))]
        other_near, other_far = other[: len(near)], other[len(near) :]
        return [b for four in zip(near, other_near, far, other_far) for b in four]

    deps_packed, deps_own = call(
        functools.partial(sum_kernel, size), "sum",
        (i16(plane + 16, nz), f32(plane, nz)), [vmem] * n_mode, [pltpu.VMEM((3 * plane, nz), F32)],
        10**5, (own_part, *parts), 10**5,
    )
    blocks = with_core(near, far)
    rows = ny + 2 * STEPS
    moved = sum(rows_of(step, ny)[1] - rows_of(step, ny)[0] for step in range(STEPS))
    coef, gain, moves = call(
        functools.partial(base_kernel, size, order), "base",
        (f32(rows, ratio, groups, nz), f32(rows, ratio, groups, nz), f32(moved, 3 * ratio, groups, nz)),
        [smem] * 3 + [vmem] * len(blocks),
        [pltpu.VMEM((rows, 3 * ratio, groups, nz), F32)] * 2 + [pltpu.VMEM((rows, ratio, groups, nz), F32)],
        10**7, (parity, eps_levels, region_gain, own, *blocks[1:]), 10**7,
    )
    deps = with_core(*gather(deps_packed))
    out_e, out_h = call(
        functools.partial(tangent_kernel, size, order), "tangent",
        (f32(3 * plane, nz), f32(3 * plane, nz)),
        [smem, vmem, vmem, anywhere] + [vmem] * len(deps),
        [pltpu.VMEM((rows, 3 * ratio, groups, nz), F32)] * 2
        + [
            pltpu.VMEM((rows, ratio, groups, nz), F32),
            pltpu.VMEM((moved, 3 * ratio, groups, nz), F32),
            pltpu.SemaphoreType.DMA((STEPS,)),
        ],
        10**7, (parity, coef, gain, moves, deps_own, *deps[1:]), 10**7,
    )
    shape = (1, 3, nx, ny, nz)
    return out_e.reshape(shape), out_h.reshape(shape)


def solution(mesh):
    placed = (
        P(None, "gx", "gy", None),
        P(None, "gx", "gy", None),
        P(),
        P(),
        P("gx", "gy", None),
        P("mode", "gx", "gy", None),
        P(),
        P("gx", "gy"),
        P("gx", "gy"),
    )
    return jax.shard_map(
        functools.partial(body, tuple(mesh.shape[a] for a in ("gx", "gy", "mode"))),
        mesh=mesh,
        in_specs=placed,
        out_specs=(P("mode", None, "gx", "gy", None), P("mode", None, "gx", "gy", None)),
        check_vma=False,
    )
```

time: 127 us -> 76.9 us (0.61)
  Pallas kernels: 0 us -> 36.8 us
  starting transfers between devices: 40.6 us -> 13.3 us
  waiting for transfers between devices: 42 us -> 18.7 us
  other arithmetic: 15.8 us -> 0.05 us
  blocking collectives: 14.8 us -> 0 us
  local copies, waits for them, and re-layouts: 11.1 us -> 7.06 us
  between operations: 2.06 us -> 0.7 us
    pallas_call x0 -> x4, Pallas kernels: none -> 36.8 us  [call(): pl.pallas_call(kernel, out_shape=outs, in_specs=specs, out_specs=tuple((p...]
    ppermute x40 -> x13, starting transfers between devices: 40.6 us -> 13.3 us  [the longest x10 8.84 us: over_xy(): return lax.ppermute(block, ('gx', 'gy'), route)]
    ppermute x40 -> x13, waiting for transfers between devices: 42 us -> 18.7 us  [the longest x10 13.1 us: over_xy(): return lax.ppermute(block, ('gx', 'gy'), route)]
    all_gather x1 -> x0, blocking collectives: 14.8 us -> none  [body(): gathered = lax.all_gather(kl_blocks, 'mode', axis=0, tiled=True)]
    mul x3 -> x0, other arithmetic: 5.9 us -> none  [the longest x1 3.89 us: advance(): DT_STEP * deps * inv_eps * inv_eps * drive]
    slice x73 -> x2, local copies, waits for them, and re-layouts: 4.88 us -> 0.05 us  [with_core(): other = [first] + [sent[rows * i:rows * i + rows] for i in range(len(got))]]
    another operation x45 -> x0, other arithmetic: 4.1 us -> none  [the longest x10 1.52 us: curl_forward(): jnp.stack([along_y(2) - along_z(1), along_z(0) - along_x(2), along_x(1) -...]
    concatenate x20 -> x2, other arithmetic: 2.5 us -> 0.05 us  [with_core(): sent = over_xy(jnp.concatenate(got, 0), 0, 1)]
  transfers between devices with their start and end apart: 40 -> 13, of which waited for: 18 -> 10; matrix products, arithmetic and copies ran while one was open for 7% -> 0% of each run, Pallas kernels for 0% -> 27%
where the time goes in v1:
time: 76.9 us; the launch traced here: 76.6 us
  Pallas kernels  36.8 us (48%)
  waiting for transfers between devices  18.7 us (24%)
  starting transfers between devices  13.3 us (17%)
  local copies, waits for them, and re-layouts  7.06 us (9%)
    pallas_call x4, Pallas kernels, call(): pl.pallas_call(kernel, out_shape=outs, in_specs=specs, out_specs=tuple((p...  36.8 us
    ppermute x10, waiting for transfers between devices, over_xy(): return lax.ppermute(block, ('gx', 'gy'), route)  13.1 us
    ppermute x10, starting transfers between devices, over_xy(): return lax.ppermute(block, ('gx', 'gy'), route)  8.84 us
    unnamed x16, local copies, waits for them, and re-layouts  7.01 us
    ppermute x3, waiting for transfers between devices, over_mode(): return lax.ppermute(block, 'mode', [(i, i ^ flip) for i in range(n_mode)])  5.59 us
    ppermute x3, starting transfers between devices, over_mode(): return lax.ppermute(block, 'mode', [(i, i ^ flip) for i in range(n_mode)])  4.45 us
  transfers between devices with their start and end apart: 13, of which 10 were waited for; matrix products, arithmetic and copies ran while one was open for 0% of the time, Pallas kernels for 27%

profile of v1, /device:TPU:0, one launch (start us, length us, event | category | flops | bytes accessed | tf_op | source)
XLA Modules:
  0.0 76.6 jit_solution(10099435295133077508)
XLA Ops:
  0.6 0.8 %copy.11.source_z = s32[12,8]{1,0:T(8,128)S(1)} copy(s32[12,8]{0,1:T(8,128)} %param.16) | data formatting | bytes 768 | tf_op args[7]
  1.4 0.8 %copy.12.source_amp = f32[12,8]{1,0:T(8,128)S(1)} copy(f32[12,8]{0,1:T(8,128)} %param.17) | data formatting | bytes 768 | tf_op args[8]
  2.2 0.9 %copy-done = f32[3,12,8,128]{3,2,1,0:T(8,128)S(1)} copy-done((f32[3,12,8,128]{3,2,1,0:T(8,128)S(1)}, f32[3,12,8,128]{3,2,1,0:T(8,128)}, u32[]{:S(2)}) %copy-start) | copy-done | bytes 147480
  3.1 0.9 %copy-done.1 = f32[3,12,8,128]{3,2,1,0:T(8,128)S(1)} copy-done((f32[3,12,8,128]{3,2,1,0:T(8,128)S(1)}, f32[3,12,8,128]{3,2,1,0:T(8,128)}, u32[]{:S(2)}) %copy-start.1) | copy-done | bytes 147480
  4.0 0.9 %copy-done.2 = bf16[4,12,8,128]{3,2,1,0:T(8,128)(2,1)S(1)} copy-done((bf16[4,12,8,128]{3,2,1,0:T(8,128)(2,1)S(1)}, bf16[4,12,8,128]{3,2,1,0:T(8,128)(2,1)}, u32[]{:S(2)}) %copy-start.2) | copy-done | bytes 98328
  4.9 0.8 %copy-done.3 = s32[12,8,128]{2,1,0:T(8,128)S(1)} copy-done((s32[12,8,128]{2,1,0:T(8,128)S(1)}, s32[12,8,128]{2,1,0:T(8,128)}, u32[]{:S(2)}) %copy-start.3) | copy-done | bytes 49176
  5.7 0.7 copy-done.4
  6.3 1.2 %pack.1 = (s16[768,128]{1,0:T(8,128)(2,1)S(1)}, f32[768,128]{1,0:T(8,128)S(1)}, f32[96,128]{1,0:T(8,128)S(1)}, s16[112,128]{1,0:T(8,128)(2,1)S(1)}, s16[112,128]...) custom-call(s32[1]{0:T(128)} %bitcast.1.me, s32[16]{0:T(128)S(1)} %copy-done.4, f32[288,128]{1,0:T(8,128)S(1)} %bitcast.8, ...), custom_call_target="tpu_custom_call" | custom-call | flops 1000000 | bytes 1000000 | tf_op jit(solution)/shard_map/pack/pallas_call | solution.py:439
  7.5 3.0 %collective-permute-start.1 = (s16[768,128]{1,0:T(8,128)(2,1)S(1)}, s16[768,128]{1,0:T(8,128)(2,1)S(1)}, u32[]{:S(2)}, u32[]{:S(2)}) collective-permute-start(s16[768,128]{1,0:T(8,128)(2,1)S(1)} %get-tuple-element.16), channel_id=1, source_target_pairs={{0,8},{4,12},{8,0},{12,4},{16,24},{20,28},{24,16},{28,20},{1,9},{5... | collective-permute-start | bytes 589832 | tf_op jit(solution)/shard_map/ppermute | solution.py:467
  10.5 1.5 %collective-permute-start.2 = (s16[768,128]{1,0:T(8,128)(2,1)S(1)}, s16[768,128]{1,0:T(8,128)(2,1)S(1)}, u32[]{:S(2)}, u32[]{:S(2)}) collective-permute-start(s16[768,128]{1,0:T(8,128)(2,1)S(1)} %get-tuple-element.16), channel_id=1, source_target_pairs={{0,16},{4,20},{8,24},{12,28},{16,0},{20,4},{24,8},{28,12},{1,17},{... | collective-permute-start | bytes 589832 | tf_op jit(solution)/shard_map/ppermute | solution.py:467
  12.1 3.4 %collective-permute-done.1.rest_1_ = s16[768,128]{1,0:T(8,128)(2,1)S(1)} collective-permute-done((s16[768,128]{1,0:T(8,128)(2,1)S(1)}, s16[768,128]{1,0:T(8,128)(2,1)S(1)}, u32[]{:S(2)}, u32[]{:S(2)}) %collective-permute-start.1) | collective-permute-done | bytes 196640 | tf_op jit(solution)/shard_map/ppermute | solution.py:467
  15.4 2.9 %collective-permute-done.2.rest_3_ = s16[768,128]{1,0:T(8,128)(2,1)S(1)} collective-permute-done((s16[768,128]{1,0:T(8,128)(2,1)S(1)}, s16[768,128]{1,0:T(8,128)(2,1)S(1)}, u32[]{:S(2)}, u32[]{:S(2)}) %collective-permute-start.2) | collective-permute-done | bytes 196640 | tf_op jit(solution)/shard_map/ppermute | solution.py:467
  18.4 2.5 %collective-permute-done.3.rest_5_ = s16[768,128]{1,0:T(8,128)(2,1)S(1)} collective-permute-done((s16[768,128]{1,0:T(8,128)(2,1)S(1)}, s16[768,128]{1,0:T(8,128)(2,1)S(1)}, u32[]{:S(2)}, u32[]{:S(2)}) %collective-permute-start.3) | collective-permute-done | bytes 196640 | tf_op jit(solution)/shard_map/ppermute | solution.py:467
  21.0 1.8 %collective-permute-start.5 = (s16[112,128]{1,0:T(8,128)(2,1)S(1)}, s16[112,128]{1,0:T(8,128)(2,1)S(1)}, u32[]{:S(2)}, u32[]{:S(2)}) collective-permute-start(s16[112,128]{1,0:T(8,128)(2,1)S(1)} %get-tuple-element.21), channel_id=1, source_target_pairs={{0,1},{1,0},{2,3},{3,2},{4,5},{5,4},{6,7},{7,6},{8,9},{9,8},{10,11... | collective-permute-start | bytes 86024 | tf_op jit(solution)/shard_map/ppermute | solution.py:470
  22.8 2.6 %collective-permute-start.6 = (s16[112,128]{1,0:T(8,128)(2,1)S(1)}, s16[112,128]{1,0:T(8,128)(2,1)S(1)}, u32[]{:S(2)}, u32[]{:S(2)}) collective-permute-start(s16[112,128]{1,0:T(8,128)(2,1)S(1)} %get-tuple-element.22), channel_id=1, source_target_pairs={{0,2},{1,3},{2,0},{3,1},{4,6},{5,7},{6,4},{7,5},{8,10},{9,11},{10,... | collective-permute-start | bytes 86024 | tf_op jit(solution)/shard_map/ppermute | solution.py:470
  25.5 2.4 %collective-permute-done.6.rest_1_ = s16[112,128]{1,0:T(8,128)(2,1)S(1)} collective-permute-done((s16[112,128]{1,0:T(8,128)(2,1)S(1)}, s16[112,128]{1,0:T(8,128)(2,1)S(1)}, u32[]{:S(2)}, u32[]{:S(2)}) %collective-permute-start.6) | collective-permute-done | bytes 28704 | tf_op jit(solution)/shard_map/ppermute | solution.py:470
  27.9 3.2 %collective-permute-done.7.rest_2_ = s16[112,128]{1,0:T(8,128)(2,1)S(1)} collective-permute-done((s16[112,128]{1,0:T(8,128)(2,1)S(1)}, s16[112,128]{1,0:T(8,128)(2,1)S(1)}, u32[]{:S(2)}, u32[]{:S(2)}) %collective-permute-start.7) | collective-permute-done | bytes 28704 | tf_op jit(solution)/shard_map/ppermute | solution.py:470
  31.3 1.6 %collective-permute-start.10 = (s16[112,128]{1,0:T(8,128)(2,1)S(1)}, s16[112,128]{1,0:T(8,128)(2,1)S(1)}, u32[]{:S(2)}, u32[]{:S(2)}) collective-permute-start(s16[112,128]{1,0:T(8,128)(2,1)S(1)} %get-tuple-element.25), channel_id=1, source_target_pairs={{0,16},{4,20},{8,24},{12,28},{16,0},{20,4},{24,8},{28,12},{1,17},{... | collective-permute-start | bytes 86024 | tf_op jit(solution)/shard_map/ppermute | solution.py:467
  32.8 1.5 %collective-permute-start.11 = (s16[112,128]{1,0:T(8,128)(2,1)S(1)}, s16[112,128]{1,0:T(8,128)(2,1)S(1)}, u32[]{:S(2)}, u32[]{:S(2)}) collective-permute-start(s16[112,128]{1,0:T(8,128)(2,1)S(1)} %get-tuple-element.25), channel_id=1, source_target_pairs={{0,24},{4,28},{8,16},{12,20},{16,8},{20,12},{24,0},{28,4},{1,25},{... | collective-permute-start | bytes 86024 | tf_op jit(solution)/shard_map/ppermute | solution.py:467
  35.5 2.1 %collective-permute-done.11.rest_5_ = s16[112,128]{1,0:T(8,128)(2,1)S(1)} collective-permute-done((s16[112,128]{1,0:T(8,128)(2,1)S(1)}, s16[112,128]{1,0:T(8,128)(2,1)S(1)}, u32[]{:S(2)}, u32[]{:S(2)}) %collective-permute-start.11) | collective-permute-done | bytes 28704 | tf_op jit(solution)/shard_map/ppermute | solution.py:467
  38.9 0.7 collective-permute-done.12
  39.8 0.7 copy-done.5
  41.2 20.8 %base.1 = (f32[28,3,8,128]{3,2,1,0:T(8,128)S(1)}, f32[28,3,8,128]{3,2,1,0:T(8,128)S(1)}, f32[170,9,8,128]{3,2,1,0:T(8,128)}) custom-call(s32[1]{0:T(128)} %bitcast.parity, f32[3]{0:T(128)S(1)} %copy-done.5, f32[3]{0:T(128)S(1)} %copy-done.6, f32[768,128]{1,0:T(8,128)S(1)} %get-tuple-element.15.own, s16[768,128]{1,0:T(8,128)(2,1)S(1)} %collective-permute-done.rest_0_, ...), custom_call_target="tpu_custom_call" | custom-call | flops 10000000 | bytes 10000000 | tf_op jit(solution)/shard_map/base/pallas_call | solution.py:439
  62.0 14.6 %tangent.1 = (f32[288,128]{1,0:T(8,128)}, f32[288,128]{1,0:T(8,128)}) custom-call(s32[1]{0:T(128)} %bitcast.parity, f32[28,3,8,128]{3,2,1,0:T(8,128)S(1)} %get-tuple-element.17.coef, f32[28,3,8,128]{3,2,1,0:T(8,128)S(1)} %get-tuple-element.18.gain, f32[170,9,8,128]{3,2,1,0:T(8,128)} %get-tuple-element.19.moves, f32[96,128]{1,0:T(8,128)S(1)} %get-tuple-element.24.own, ...), custom_call_target="tpu_custom_call" | custom-call | flops 10000000 | bytes 10000000 | tf_op jit(solution)/shard_map/tangent/pallas_call | solution.py:439
  (26 shorter events, 3.8 us)
Async XLA Ops:
  2.2 0.9 %copy-start = (f32[3,12,8,128]{3,2,1,0:T(8,128)S(1)}, f32[3,12,8,128]{3,2,1,0:T(8,128)}, u32[]{:S(2)}) copy-start(f32[3,12,8,128]{3,2,1,0:T(8,128)} %param.9) | copy-start | bytes 442372
  3.1 0.9 %copy-start.1 = (f32[3,12,8,128]{3,2,1,0:T(8,128)S(1)}, f32[3,12,8,128]{3,2,1,0:T(8,128)}, u32[]{:S(2)}) copy-start(f32[3,12,8,128]{3,2,1,0:T(8,128)} %param.10) | copy-start | bytes 442372
  4.0 0.9 %copy-start.2 = (bf16[4,12,8,128]{3,2,1,0:T(8,128)(2,1)S(1)}, bf16[4,12,8,128]{3,2,1,0:T(8,128)(2,1)}, u32[]{:S(2)}) copy-start(bf16[4,12,8,128]{3,2,1,0:T(8,128)(2,1)} %param.14) | copy-start | bytes 294916
  4.9 0.8 %copy-start.3 = (s32[12,8,128]{2,1,0:T(8,128)S(1)}, s32[12,8,128]{2,1,0:T(8,128)}, u32[]{:S(2)}) copy-start(s32[12,8,128]{2,1,0:T(8,128)} %param.13) | copy-start | bytes 147460
  5.7 0.7 copy-start.4
  7.5 7.9 %collective-permute-start.1 = (s16[768,128]{1,0:T(8,128)(2,1)S(1)}, s16[768,128]{1,0:T(8,128)(2,1)S(1)}, u32[]{:S(2)}, u32[]{:S(2)}) collective-permute-start(s16[768,128]{1,0:T(8,128)(2,1)S(1)} %get-tuple-element.16), channel_id=1, source_target_pairs={{0,8},{4,12},{8,0},{12,4},{16,24},{20,28},{24,16},{28,20},{1,9},{5... | collective-permute-start | bytes 589832 | tf_op jit(solution)/shard_map/ppermute | solution.py:467
  10.5 7.8 %collective-permute-start.2 = (s16[768,128]{1,0:T(8,128)(2,1)S(1)}, s16[768,128]{1,0:T(8,128)(2,1)S(1)}, u32[]{:S(2)}, u32[]{:S(2)}) collective-permute-start(s16[768,128]{1,0:T(8,128)(2,1)S(1)} %get-tuple-element.16), channel_id=1, source_target_pairs={{0,16},{4,20},{8,24},{12,28},{16,0},{20,4},{24,8},{28,12},{1,17},{... | collective-permute-start | bytes 589832 | tf_op jit(solution)/shard_map/ppermute | solution.py:467
  12.0 8.9 %collective-permute-start.3 = (s16[768,128]{1,0:T(8,128)(2,1)S(1)}, s16[768,128]{1,0:T(8,128)(2,1)S(1)}, u32[]{:S(2)}, u32[]{:S(2)}) collective-permute-start(s16[768,128]{1,0:T(8,128)(2,1)S(1)} %get-tuple-element.16), channel_id=1, source_target_pairs={{0,24},{4,28},{8,16},{12,20},{16,8},{20,12},{24,0},{28,4},{1,25},{... | collective-permute-start | bytes 589832 | tf_op jit(solution)/shard_map/ppermute | solution.py:467
  20.9 18.6 %collective-permute-start.4 = (s16[2304,128]{1,0:T(8,128)(2,1)S(1)}, s16[2304,128]{1,0:T(8,128)(2,1)S(1)}, u32[]{:S(2)}, u32[]{:S(2)}) collective-permute-start(s16[2304,128]{1,0:T(8,128)(2,1)S(1)} %pad_add_fusion), channel_id=1, source_target_pairs={{0,4},{4,0},{8,12},{12,8},{16,20},{20,16},{24,28},{28,24},{1,5},{5... | collective-permute-start | bytes 1769480 | tf_op jit(solution)/shard_map/ppermute | solution.py:467
  21.0 4.5 %collective-permute-start.5 = (s16[112,128]{1,0:T(8,128)(2,1)S(1)}, s16[112,128]{1,0:T(8,128)(2,1)S(1)}, u32[]{:S(2)}, u32[]{:S(2)}) collective-permute-start(s16[112,128]{1,0:T(8,128)(2,1)S(1)} %get-tuple-element.21), channel_id=1, source_target_pairs={{0,1},{1,0},{2,3},{3,2},{4,5},{5,4},{6,7},{7,6},{8,9},{9,8},{10,11... | collective-permute-start | bytes 86024 | tf_op jit(solution)/shard_map/ppermute | solution.py:470
  22.8 5.1 %collective-permute-start.6 = (s16[112,128]{1,0:T(8,128)(2,1)S(1)}, s16[112,128]{1,0:T(8,128)(2,1)S(1)}, u32[]{:S(2)}, u32[]{:S(2)}) collective-permute-start(s16[112,128]{1,0:T(8,128)(2,1)S(1)} %get-tuple-element.22), channel_id=1, source_target_pairs={{0,2},{1,3},{2,0},{3,1},{4,6},{5,7},{6,4},{7,5},{8,10},{9,11},{10,... | collective-permute-start | bytes 86024 | tf_op jit(solution)/shard_map/ppermute | solution.py:470
  25.4 5.7 %collective-permute-start.7 = (s16[112,128]{1,0:T(8,128)(2,1)S(1)}, s16[112,128]{1,0:T(8,128)(2,1)S(1)}, u32[]{:S(2)}, u32[]{:S(2)}) collective-permute-start(s16[112,128]{1,0:T(8,128)(2,1)S(1)} %get-tuple-element.23), channel_id=1, source_target_pairs={{0,3},{1,2},{2,1},{3,0},{4,7},{5,6},{6,5},{7,4},{8,11},{9,10},{10,... | collective-permute-start | bytes 86024 | tf_op jit(solution)/shard_map/ppermute | solution.py:470
  31.3 4.2 %collective-permute-start.10 = (s16[112,128]{1,0:T(8,128)(2,1)S(1)}, s16[112,128]{1,0:T(8,128)(2,1)S(1)}, u32[]{:S(2)}, u32[]{:S(2)}) collective-permute-start(s16[112,128]{1,0:T(8,128)(2,1)S(1)} %get-tuple-element.25), channel_id=1, source_target_pairs={{0,16},{4,20},{8,24},{12,28},{16,0},{20,4},{24,8},{28,12},{1,17},{... | collective-permute-start | bytes 86024 | tf_op jit(solution)/shard_map/ppermute | solution.py:467
  32.8 4.8 %collective-permute-start.11 = (s16[112,128]{1,0:T(8,128)(2,1)S(1)}, s16[112,128]{1,0:T(8,128)(2,1)S(1)}, u32[]{:S(2)}, u32[]{:S(2)}) collective-permute-start(s16[112,128]{1,0:T(8,128)(2,1)S(1)} %get-tuple-element.25), channel_id=1, source_target_pairs={{0,24},{4,28},{8,16},{12,20},{16,8},{20,12},{24,0},{28,4},{1,25},{... | collective-permute-start | bytes 86024 | tf_op jit(solution)/shard_map/ppermute | solution.py:467
  34.3 3.9 %collective-permute-start.9 = (s16[112,128]{1,0:T(8,128)(2,1)S(1)}, s16[112,128]{1,0:T(8,128)(2,1)S(1)}, u32[]{:S(2)}, u32[]{:S(2)}) collective-permute-start(s16[112,128]{1,0:T(8,128)(2,1)S(1)} %get-tuple-element.25), channel_id=1, source_target_pairs={{0,8},{4,12},{8,0},{12,4},{16,24},{20,28},{24,16},{28,20},{1,9},{5... | collective-permute-start | bytes 86024 | tf_op jit(solution)/shard_map/ppermute | solution.py:467
  38.2 1.3 %collective-permute-start.12 = (s16[336,128]{1,0:T(8,128)(2,1)S(1)}, s16[336,128]{1,0:T(8,128)(2,1)S(1)}, u32[]{:S(2)}, u32[]{:S(2)}) collective-permute-start(s16[336,128]{1,0:T(8,128)(2,1)S(1)} %pad_add_fusion.1), channel_id=1, source_target_pairs={{0,4},{4,0},{8,12},{12,8},{16,20},{20,16},{24,28},{28,24},{1,5},{5... | collective-permute-start | bytes 258056 | tf_op jit(solution)/shard_map/ppermute | solution.py:467
  38.3 1.6 %collective-permute-start = (s16[768,128]{1,0:T(8,128)(2,1)S(1)}, s16[768,128]{1,0:T(8,128)(2,1)S(1)}, u32[]{:S(2)}, u32[]{:S(2)}) collective-permute-start(s16[768,128]{1,0:T(8,128)(2,1)S(1)} %get-tuple-element.16), channel_id=1, source_target_pairs={{0,4},{4,0},{8,12},{12,8},{16,20},{20,16},{24,28},{28,24},{1,5},{5... | collective-permute-start | bytes 589832 | tf_op jit(solution)/shard_map/ppermute | solution.py:467
  38.8 23.2 %collective-permute-start.8 = (s16[112,128]{1,0:T(8,128)(2,1)S(1)}, s16[112,128]{1,0:T(8,128)(2,1)S(1)}, u32[]{:S(2)}, u32[]{:S(2)}) collective-permute-start(s16[112,128]{1,0:T(8,128)(2,1)S(1)} %get-tuple-element.25), channel_id=1, source_target_pairs={{0,4},{4,0},{8,12},{12,8},{16,20},{20,16},{24,28},{28,24},{1,5},{5... | collective-permute-start | bytes 86024 | tf_op jit(solution)/shard_map/ppermute | solution.py:467
  39.8 0.7 copy-start.5
  40.5 0.7 copy-start.6

commit v2 on v1

--- a/solution.py
+++ b/solution.py
@@ -16,8 +16,9 @@
 TILE = 8
 FULL = 32000.0
 FINE = 256.0
+CHUNK = 13
 F32 = jnp.float32
-VMEM_LIMIT = 48 * 1024 * 1024
+VMEM_LIMIT = 24 * 1024 * 1024
 
 
 def iota(axis, rows=TILE):
@@ -49,18 +50,39 @@
 
 
 def pack_kernel(
-    size, me, modes, e, h, labels, kl, source_z, source_amp,
-    packed, own, own_part, *rest,
+    size, me, modes_at, levels_at, gains_at, e_at, h_at, labels_at, kl_at, z_at, amp_at,
+    packed, own, own_part, tables, *rest,
 ):
     nx, ny = size
-    parts, (label_rows, z_rows, amp_rows) = rest[:-3], rest[-3:]
+    parts, rest = rest[:-11], rest[-11:]
+    modes, levels, gains, e, h, labels, kl, source_z, source_amp, label_rows, sems = rest
     ratio, plane, stride = nx // GROUP, nx * ny, nx // GROUP * ny
+    ends = zip(
+        (modes_at, levels_at, gains_at, kl_at, e_at, h_at, labels_at, z_at, amp_at),
+        (modes, levels, gains, kl, e, h, labels, source_z, source_amp),
+    )
+    copies = [pltpu.make_async_copy(there, here, sems.at[i]) for i, (there, here) in enumerate(ends)]
+    for copy in copies:
+        copy.start()
+    label_rows[plane:] = jnp.zeros((plane, 128), F32)
+    for copy in copies:
+        copy.wait()
     label_rows[:plane] = labels[...].astype(F32)
-    label_rows[plane:] = jnp.zeros((plane, 128), F32)
-    z_rows[...] = jnp.zeros(z_rows.shape, F32)
-    amp_rows[...] = jnp.zeros(amp_rows.shape, F32)
-    z_rows[nx:, :ny] = source_z[...].astype(F32)
-    amp_rows[nx:, :ny] = source_amp[...]
+    for i in range(3):
+        at = slice(i, i + 1)
+        tables[at] = jnp.full((1, 128), DT_STEP * DT_STEP) / jnp.full((1, 128), levels[i])
+        tables[slice(i + 3, i + 4)] = jnp.full((1, 128), gains[i]) / jnp.full((1, 128), levels[i])
+    tables[6:8] = jnp.zeros((2, 128), F32)
+    heights_of = source_z[...].astype(F32)
+    amps_of = source_amp[...]
+    wide_lanes = lax.broadcasted_iota(jnp.int32, (TILE, nx), 1)
+    turned = lax.broadcasted_iota(jnp.int32, (TILE, nx), 0)
+
+    def column(values, y, r):
+        wanted = wide_lanes == (turned - GROUP) * ratio + r
+        picked = jnp.where(wanted, jnp.broadcast_to(values[y : y + 1], wanted.shape), 0.0)
+        return jnp.broadcast_to(jnp.sum(picked, axis=1, keepdims=True), (TILE, 128))
+
     low, lanes = iota(0) < GROUP, iota(1)
 
     blocks = kl.shape[0] // plane
@@ -95,8 +117,7 @@
             h_last = h[pl.ds(at + plane, TILE, stride=stride)]
             tiles.append(jnp.where(low, pltpu.roll(e_last, GROUP, 0), h_last))
             label = label_rows[pl.ds(at, TILE, stride=stride)]
-            height = lane(z_rows[pl.ds(r, TILE, stride=ratio)], y)
-            amp = lane(amp_rows[pl.ds(r, TILE, stride=ratio)], y)
+            height, amp = column(heights_of, y, r), column(amps_of, y, r)
             coded, meta = [], jnp.zeros((TILE, 128), F32)
             for i, tile in enumerate(tiles):
                 code = scale_code(jnp.broadcast_to(jnp.max(jnp.abs(tile), axis=1, keepdims=True), tile.shape))
@@ -217,14 +238,10 @@
     return step + 1, ny + 2 * STEPS - 1 - step
 
 
-def sweep(first, end, carry, body):
-    assert (end - first) % 2 == 0
-
-    def two(i, held):
-        at = first + 2 * i
-        return body(at + 1, body(at, held))
-
-    return lax.fori_loop(0, (end - first) // 2, two, carry)
+def chunks(first, end):
+    count = -(-(end - first) // CHUNK)
+    cuts = [first + (end - first) * i // count for i in range(count + 1)]
+    return [range(*cut) for cut in zip(cuts, cuts[1:])]
 
 
 def places(parity, ny):
@@ -248,15 +265,16 @@
     ]
 
 
-def base_kernel(size, order, parity, levels, gains, own, *rest):
+def base_kernel(size, order, parity, tables, own, *rest):
     nx, ny = size
     ratio = nx // GROUP
     blocks, (coef, gain_out, moves, electric, magnetic, profile) = rest[:-6], rest[-6:]
     blocks = (own,) + blocks
     low, lanes = iota(0) < GROUP, iota(1)
-
-    def pick(label, table):
-        return jnp.where(label < 0.5, table[0], jnp.where(label < 1.5, table[1], table[2]))
+    table = [jnp.broadcast_to(tables[i : i + 1], (TILE, 128)) for i in range(6)]
+
+    def pick(label, first):
+        return jnp.where(label < 0.5, table[first], jnp.where(label < 1.5, table[first + 1], table[first + 2]))
 
     def unpack(y_block, y, to):
         for r in range(ratio):
@@ -283,13 +301,12 @@
 
                 fields = [scaled(planes[i], i) for i in range(6)]
                 amp = scaled(lane(meta, 7), 8)
-                inv_eps = 1.0 / pick(planes[6], levels)
                 outs.append(
                     [fields[i] * DT_STEP for i in (0, 1, 4)]
                     + [fields[i] for i in (2, 3, 5)]
                     + [
-                        DT_STEP * DT_STEP * inv_eps,
-                        pick(planes[6], gains) * inv_eps,
+                        pick(planes[6], 0),
+                        pick(planes[6], 3),
                         jnp.where(lanes.astype(F32) == lane(meta, 6), amp, 0.0),
                     ]
                 )
@@ -305,11 +322,14 @@
     for y_block, pieces in enumerate(places(parity[0], ny)):
         for first, count, to in pieces:
 
-            def some(j, _, y_block=y_block, first=first, to=to):
-                unpack(y_block, first + j, to + j)
+            each = min(count, 4)
+
+            def some(j, _, y_block=y_block, first=first, to=to, each=each):
+                for i in range(each):
+                    unpack(y_block, first + each * j + i, to + each * j + i)
                 return 0
 
-            lax.fori_loop(0, count, some, 0)
+            lax.fori_loop(0, count // each, some, 0)
 
     moved = 0
     for step in range(STEPS):
@@ -319,21 +339,26 @@
         above = load_row(electric, first, ratio)
         new = add_curl_forward(load_row(magnetic, first - 1, ratio), now, above)
 
-        def row(at, held, step=step, wave=wave, shift=moved - first):
-            now, below_x, below_z = held
-            above = load_row(electric, at + 1, ratio)
-            new = add_curl_forward(load_row(magnetic, at, ratio), now, above)
-            if step < STEPS - 1:
-                store_row(magnetic, at, new)
-            drive = curl_backward(new, below_x, below_z)
-            drive[2] = [d + wave * profile[at, r] for r, d in enumerate(drive[2])]
-            change = [[coef[at, r] * drive[c][r] for r in range(ratio)] for c in range(3)]
-            store_row(moves, at + shift, change)
-            if step < STEPS - 1:
-                store_row(electric, at, [[a + b for a, b in zip(now[c], change[c])] for c in range(3)])
-            return above, new[0], new[2]
-
-        sweep(first, end, (above, new[0], new[2]), row)
+        below_x, below_z = new[0], new[2]
+        for run in chunks(first, end):
+            field = [above] + [load_row(electric, at + 1, ratio) for at in run]
+            above = field[-1]
+            new = [
+                add_curl_forward(load_row(magnetic, at, ratio), field[i], field[i + 1])
+                for i, at in enumerate(run)
+            ]
+            for i, at in enumerate(run):
+                drive = curl_backward(new[i], below_x, below_z)
+                below_x, below_z = new[i][0], new[i][2]
+                drive[2] = [d + wave * profile[at, r] for r, d in enumerate(drive[2])]
+                change = [[coef[at, r] * drive[c][r] for r in range(ratio)] for c in range(3)]
+                store_row(moves, at - first + moved, change)
+                if step < STEPS - 1:
+                    store_row(magnetic, at, new[i])
+                    store_row(
+                        electric, at,
+                        [[p + q for p, q in zip(field[i][c], change[c])] for c in range(3)],
+                    )
         moved += end - first
 
 
@@ -342,17 +367,8 @@
     ratio, plane = nx // GROUP, nx * ny
     n_blocks = 4 * len(set(order)) - 1
     blocks, rest = (own,) + rest[:n_blocks], rest[n_blocks:]
-    out_e, out_h, electric, magnetic, weight, moves_in, sems = rest
+    out_e, out_h, electric, magnetic, weight = rest
     low = iota(0) < GROUP
-
-    copies, moved = [], 0
-    for step in range(STEPS):
-        first, end = rows_of(step, ny)
-        there = pl.ds(moved, end - first)
-        copies.append(pltpu.make_async_copy(moves.at[there], moves_in.at[there], sems.at[step]))
-        moved += end - first
-    for copy in copies:
-        copy.start()
 
     scales = [None if i == 0 else scale_of(wide(b[plane : plane + 16])) for i, b in enumerate(blocks)]
 
@@ -390,16 +406,12 @@
     moved = 0
     for step in range(STEPS):
         first, end = rows_of(step, ny)
-        copies[step].wait()
         shift = moved - first
         if step == 0:
 
-            def start(at, held, shift=shift):
-                change = load_row(moves_in, at + shift, ratio)
+            for at in range(first, end):
+                change = load_row(moves, at + shift, ratio)
                 store_row(electric, at, [[-(weight[at, r] * change[c][r]) for r in range(ratio)] for c in range(3)])
-                return held
-
-            sweep(first, end, 0, start)
         else:
 
             def old(at, step=step):
@@ -409,20 +421,26 @@
             above = load_row(electric, first, ratio)
             new = add_curl_forward(old(first - 1), now, above)
 
-            def row(at, held, old=old, shift=shift):
-                now, below_x, below_z = held
-                above = load_row(electric, at + 1, ratio)
-                new = add_curl_forward(old(at), now, above)
-                store_row(magnetic, at, new)
-                curl = curl_backward(new, below_x, below_z)
-                change = load_row(moves_in, at + shift, ratio)
-                store_row(
-                    electric, at,
-                    [[now[c][r] + (coef[at, r] * curl[c][r] - weight[at, r] * change[c][r]) for r in range(ratio)] for c in range(3)],
-                )
-                return above, new[0], new[2]
-
-            sweep(first, end, (above, new[0], new[2]), row)
+            below_x, below_z = new[0], new[2]
+            for run in chunks(first, end):
+                field = [above] + [load_row(electric, at + 1, ratio) for at in run]
+                above = field[-1]
+                new = [add_curl_forward(old(at), field[i], field[i + 1]) for i, at in enumerate(run)]
+                for i, at in enumerate(run):
+                    curl = curl_backward(new[i], below_x, below_z)
+                    below_x, below_z = new[i][0], new[i][2]
+                    change = load_row(moves, at + shift, ratio)
+                    store_row(magnetic, at, new[i])
+                    store_row(
+                        electric, at,
+                        [
+                            [
+                                field[i][c][r] + (coef[at, r] * curl[c][r] - weight[at, r] * change[c][r])
+                                for r in range(ratio)
+                            ]
+                            for c in range(3)
+                        ],
+                    )
         moved += end - first
 
     at_own = GROUP * order.index(0)
@@ -435,15 +453,15 @@
                     out[pl.ds(c * plane + r * ny + y, GROUP, stride=stride)] = tile if factor is None else tile * factor
 
 
-def call(kernel, name, outs, specs, scratch, flops, args, size_bytes):
+def call(kernel, name, outs, specs, scratch, about_us, args, vmem=VMEM_LIMIT):
     return pl.pallas_call(
         kernel,
         out_shape=outs,
         in_specs=specs,
         out_specs=tuple(pl.BlockSpec(memory_space=pltpu.VMEM) for _ in outs),
         scratch_shapes=scratch,
-        compiler_params=pltpu.CompilerParams(vmem_limit_bytes=VMEM_LIMIT),
-        cost_estimate=pl.CostEstimate(flops=flops, bytes_accessed=size_bytes, transcendentals=0),
+        compiler_params=pltpu.CompilerParams(vmem_limit_bytes=vmem),
+        cost_estimate=pl.CostEstimate(flops=0, bytes_accessed=int(about_us * 3.7e6), transcendentals=0),
         name=name,
     )(*args)
 
@@ -454,7 +472,7 @@
     assert n_gy == 4 and nx % GROUP == 0 and nx >= STEPS and ny < STEPS < 2 * ny
     ratio, plane = nx // GROUP, nx * ny
     size = (nx, ny)
-    vmem, smem, anywhere = (pl.BlockSpec(memory_space=s) for s in (pltpu.VMEM, pltpu.SMEM, pl.ANY))
+    vmem, smem, hbm = (pl.BlockSpec(memory_space=s) for s in (pltpu.VMEM, pltpu.SMEM, pltpu.HBM))
     f32 = lambda *shape: jax.ShapeDtypeStruct(shape, F32)
     i16 = lambda *shape: jax.ShapeDtypeStruct(shape, jnp.int16)
 
@@ -471,17 +489,27 @@
 
     me = lax.axis_index("mode").astype(jnp.int32).reshape(1)
     parity = (lax.axis_index("gy") % 2).astype(jnp.int32).reshape(1)
-    packed, own, own_part, *parts = call(
+    packed, own, own_part, tables, *parts = call(
         functools.partial(pack_kernel, size), "pack",
-        (i16(ny * ratio * 32, nz), f32(ny * ratio * 32, nz), f32(plane, nz)) + (i16(plane + 16, nz),) * (n_mode - 1),
-        [smem, smem] + [vmem] * 6,
-        [pltpu.VMEM((2 * plane, nz), F32), pltpu.VMEM((2 * nx, 128), F32), pltpu.VMEM((2 * nx, 128), F32)],
-        10**6,
+        (i16(ny * ratio * 32, nz), f32(ny * ratio * 32, nz), f32(plane, nz), f32(TILE, nz))
+        + (i16(plane + 16, nz),) * (n_mode - 1),
+        [smem] + [hbm] * 9,
+        [pltpu.SMEM(a.shape, a.dtype) for a in (kl_modes, eps_levels, region_gain)]
+        + [pltpu.VMEM((3 * plane, nz), F32)] * 2
+        + [pltpu.VMEM((plane, nz), jnp.int32), pltpu.VMEM((kl_blocks.shape[0] * plane, nz), kl_blocks.dtype)]
+        + [pltpu.VMEM((ny, nx), jnp.int32), pltpu.VMEM((ny, nx), F32), pltpu.VMEM((2 * plane, nz), F32)]
+        + [pltpu.SemaphoreType.DMA((9,))],
+        1.5,
         (
-            me, kl_modes, e_init.reshape(-1, nz), h_init.reshape(-1, nz), region_labels.reshape(-1, nz),
-            kl_blocks.reshape(-1, nz), source_z, source_amp,
+            me,
+            *(
+                pltpu.with_memory_space_constraint(a, pltpu.HBM)
+                for a in (
+                    kl_modes, eps_levels, region_gain, e_init.reshape(-1, nz), h_init.reshape(-1, nz),
+                    region_labels.reshape(-1, nz), kl_blocks.reshape(-1, nz), source_z.T, source_amp.T,
+                )
+            ),
         ),
-        10**6,
     )
 
     moves_x = [0, -1] if n_gx == 2 else [0, -1, 1]
@@ -508,30 +536,26 @@
     deps_packed, deps_own = call(
         functools.partial(sum_kernel, size), "sum",
         (i16(plane + 16, nz), f32(plane, nz)), [vmem] * n_mode, [pltpu.VMEM((3 * plane, nz), F32)],
-        10**5, (own_part, *parts), 10**5,
-    )
+        0.3, (own_part, *parts),
+    )
+    near, far, deps_packed = lax.optimization_barrier((near, far, deps_packed))
     blocks = with_core(near, far)
     rows = ny + 2 * STEPS
     moved = sum(rows_of(step, ny)[1] - rows_of(step, ny)[0] for step in range(STEPS))
     coef, gain, moves = call(
         functools.partial(base_kernel, size, order), "base",
         (f32(rows, ratio, groups, nz), f32(rows, ratio, groups, nz), f32(moved, 3 * ratio, groups, nz)),
-        [smem] * 3 + [vmem] * len(blocks),
+        [smem] + [vmem] * (1 + len(blocks)),
         [pltpu.VMEM((rows, 3 * ratio, groups, nz), F32)] * 2 + [pltpu.VMEM((rows, ratio, groups, nz), F32)],
-        10**7, (parity, eps_levels, region_gain, own, *blocks[1:]), 10**7,
+        5.0, (parity, tables, own, *blocks[1:]),
     )
     deps = with_core(*gather(deps_packed))
     out_e, out_h = call(
         functools.partial(tangent_kernel, size, order), "tangent",
         (f32(3 * plane, nz), f32(3 * plane, nz)),
-        [smem, vmem, vmem, anywhere] + [vmem] * len(deps),
-        [pltpu.VMEM((rows, 3 * ratio, groups, nz), F32)] * 2
-        + [
-            pltpu.VMEM((rows, ratio, groups, nz), F32),
-            pltpu.VMEM((moved, 3 * ratio, groups, nz), F32),
-            pltpu.SemaphoreType.DMA((STEPS,)),
-        ],
-        10**7, (parity, coef, gain, moves, deps_own, *deps[1:]), 10**7,
+        [smem] + [vmem] * (3 + len(deps)),
+        [pltpu.VMEM((rows, 3 * ratio, groups, nz), F32)] * 2 + [pltpu.VMEM((rows, ratio, groups, nz), F32)],
+        4.0, (parity, coef, gain, moves, deps_own, *deps[1:]),
     )
     shape = (1, 3, nx, ny, nz)
     return out_e.reshape(shape), out_h.reshape(shape)

time: 76.9 us -> 34.8 us (0.45)
  Pallas kernels: 36.8 us -> 10 us
  waiting for transfers between devices: 18.7 us -> 7.03 us
  local copies, waits for them, and re-layouts: 7.06 us -> 0.05 us
  starting transfers between devices: 13.3 us -> 16.7 us
    pallas_call x4, Pallas kernels: 36.8 us -> 10 us  [call(): pl.pallas_call(kernel, out_shape=outs, in_specs=specs, out_specs=tuple((p...]
    ppermute x10, waiting for transfers between devices: 13.1 us -> 4.67 us  [over_xy(): return lax.ppermute(block, ('gx', 'gy'), route)]
    unnamed x16 -> x0, local copies, waits for them, and re-layouts: 7.01 us -> none
    ppermute x3, starting transfers between devices: 4.45 us -> 7.92 us  [over_mode(): return lax.ppermute(block, 'mode', [(i, i ^ flip) for i in range(n_mode)])]
    ppermute x3, waiting for transfers between devices: 5.59 us -> 2.37 us  [over_mode(): return lax.ppermute(block, 'mode', [(i, i ^ flip) for i in range(n_mode)])]
  transfers between devices with their start and end apart: 13 -> 13, of which waited for: 10 -> 6; matrix products, arithmetic and copies ran while one was open for 0% -> 0% of each run, Pallas kernels for 27% -> 14%
where the time goes in v2:
time: 34.8 us; the launch traced here: 34.6 us
  starting transfers between devices  16.7 us (48%)
  Pallas kernels  10 us (29%)
  waiting for transfers between devices  7.03 us (20%)
  between operations  0.75 us (2%)
    pallas_call x4, Pallas kernels, call(): pl.pallas_call(kernel, out_shape=outs, in_specs=specs, out_specs=tuple((p...  10 us
    ppermute x10, starting transfers between devices, over_xy(): return lax.ppermute(block, ('gx', 'gy'), route)  8.81 us
    ppermute x3, starting transfers between devices, over_mode(): return lax.ppermute(block, 'mode', [(i, i ^ flip) for i in range(n_mode)])  7.92 us
    ppermute x10, waiting for transfers between devices, over_xy(): return lax.ppermute(block, ('gx', 'gy'), route)  4.67 us
    ppermute x3, waiting for transfers between devices, over_mode(): return lax.ppermute(block, 'mode', [(i, i ^ flip) for i in range(n_mode)])  2.37 us
  transfers between devices with their start and end apart: 13, of which 6 were waited for; matrix products, arithmetic and copies ran while one was open for 0% of the time, Pallas kernels for 14%

profile of v2, /device:TPU:0, one launch (start us, length us, event | category | flops | bytes accessed | tf_op | source)
XLA Modules:
  0.0 34.6 jit_solution(17574070097790669306)
XLA Ops:
  0.6 1.6 %pack.1 = (s16[768,128]{1,0:T(8,128)(2,1)S(1)}, f32[768,128]{1,0:T(8,128)S(1)}, f32[96,128]{1,0:T(8,128)S(1)}, f32[8,128]{1,0:T(8,128)S(1)}, s16[112,128]{1,0:T(...) custom-call(s32[1]{0:T(128)} %bitcast.1.me, s32[16]{0:T(128)} %modes_at.1, f32[3]{0:T(128)} %levels_at.1, ...), custom_call_target="tpu_custom_call" | custom-call | bytes 5550000 | tf_op jit(solution)/shard_map/pack/pallas_call | solution.py:457
  2.2 3.0 %collective-permute-start = (s16[768,128]{1,0:T(8,128)(2,1)S(1)}, s16[768,128]{1,0:T(8,128)(2,1)S(1)}, u32[]{:S(2)}, u32[]{:S(2)}) collective-permute-start(s16[768,128]{1,0:T(8,128)(2,1)S(1)} %get-tuple-element.29), channel_id=1, source_target_pairs={{0,16},{4,20},{8,24},{12,28},{16,0},{20,4},{24,8},{28,12},{1,17},{... | collective-permute-start | bytes 589832 | tf_op jit(solution)/shard_map/ppermute | solution.py:485
  5.2 1.5 %collective-permute-start.1 = (s16[768,128]{1,0:T(8,128)(2,1)S(1)}, s16[768,128]{1,0:T(8,128)(2,1)S(1)}, u32[]{:S(2)}, u32[]{:S(2)}) collective-permute-start(s16[768,128]{1,0:T(8,128)(2,1)S(1)} %get-tuple-element.29), channel_id=1, source_target_pairs={{0,8},{4,12},{8,0},{12,4},{16,24},{20,28},{24,16},{28,20},{1,9},{5... | collective-permute-start | bytes 589832 | tf_op jit(solution)/shard_map/ppermute | solution.py:485
  6.7 0.0 collective-permute-start.2
  6.8 2.0 %collective-permute-start.3 = (s16[112,128]{1,0:T(8,128)(2,1)S(1)}, s16[112,128]{1,0:T(8,128)(2,1)S(1)}, u32[]{:S(2)}, u32[]{:S(2)}) collective-permute-start(s16[112,128]{1,0:T(8,128)(2,1)S(1)} %get-tuple-element.25), channel_id=1, source_target_pairs={{0,1},{1,0},{2,3},{3,2},{4,5},{5,4},{6,7},{7,6},{8,9},{9,8},{10,11... | collective-permute-start | bytes 86024 | tf_op jit(solution)/shard_map/ppermute | solution.py:488
  8.8 2.6 %collective-permute-start.4 = (s16[112,128]{1,0:T(8,128)(2,1)S(1)}, s16[112,128]{1,0:T(8,128)(2,1)S(1)}, u32[]{:S(2)}, u32[]{:S(2)}) collective-permute-start(s16[112,128]{1,0:T(8,128)(2,1)S(1)} %get-tuple-element.26), channel_id=1, source_target_pairs={{0,2},{1,3},{2,0},{3,1},{4,6},{5,7},{6,4},{7,5},{8,10},{9,11},{10,... | collective-permute-start | bytes 86024 | tf_op jit(solution)/shard_map/ppermute | solution.py:488
  11.4 0.0 collective-permute-done.3.rest_0_
  11.4 3.3 %collective-permute-start.5 = (s16[112,128]{1,0:T(8,128)(2,1)S(1)}, s16[112,128]{1,0:T(8,128)(2,1)S(1)}, u32[]{:S(2)}, u32[]{:S(2)}) collective-permute-start(s16[112,128]{1,0:T(8,128)(2,1)S(1)} %get-tuple-element.27), channel_id=1, source_target_pairs={{0,3},{1,2},{2,1},{3,0},{4,7},{5,6},{6,5},{7,4},{8,11},{9,10},{10,... | collective-permute-start | bytes 86024 | tf_op jit(solution)/shard_map/ppermute | solution.py:488
  14.7 2.4 %collective-permute-done.5.rest_2_ = s16[112,128]{1,0:T(8,128)(2,1)S(1)} collective-permute-done((s16[112,128]{1,0:T(8,128)(2,1)S(1)}, s16[112,128]{1,0:T(8,128)(2,1)S(1)}, u32[]{:S(2)}, u32[]{:S(2)}) %collective-permute-start.5) | collective-permute-done | bytes 28704 | tf_op jit(solution)/shard_map/ppermute | solution.py:488
  17.1 0.2 sum.1
  17.3 0.1 collective-permute-start.7
  17.4 1.6 %collective-permute-start.10 = (s16[112,128]{1,0:T(8,128)(2,1)S(1)}, s16[112,128]{1,0:T(8,128)(2,1)S(1)}, u32[]{:S(2)}, u32[]{:S(2)}) collective-permute-start(s16[112,128]{1,0:T(8,128)(2,1)S(1)} %get-tuple-element.37), channel_id=1, source_target_pairs={{0,16},{4,20},{8,24},{12,28},{16,0},{20,4},{24,8},{28,12},{1,17},{... | collective-permute-start | bytes 86024 | tf_op jit(solution)/shard_map/ppermute | solution.py:485
  19.0 1.5 %collective-permute-start.11 = (s16[112,128]{1,0:T(8,128)(2,1)S(1)}, s16[112,128]{1,0:T(8,128)(2,1)S(1)}, u32[]{:S(2)}, u32[]{:S(2)}) collective-permute-start(s16[112,128]{1,0:T(8,128)(2,1)S(1)} %get-tuple-element.37), channel_id=1, source_target_pairs={{0,24},{4,28},{8,16},{12,20},{16,8},{20,12},{24,0},{28,4},{1,25},{... | collective-permute-start | bytes 86024 | tf_op jit(solution)/shard_map/ppermute | solution.py:485
  20.5 0.5 %collective-permute-start.9 = (s16[112,128]{1,0:T(8,128)(2,1)S(1)}, s16[112,128]{1,0:T(8,128)(2,1)S(1)}, u32[]{:S(2)}, u32[]{:S(2)}) collective-permute-start(s16[112,128]{1,0:T(8,128)(2,1)S(1)} %get-tuple-element.37), channel_id=1, source_target_pairs={{0,8},{4,12},{8,0},{12,4},{16,24},{20,28},{24,16},{28,20},{1,9},{5... | collective-permute-start | bytes 86024 | tf_op jit(solution)/shard_map/ppermute | solution.py:485
  21.0 0.4 %collective-permute-done.10.rest_3_ = s16[112,128]{1,0:T(8,128)(2,1)S(1)} collective-permute-done((s16[112,128]{1,0:T(8,128)(2,1)S(1)}, s16[112,128]{1,0:T(8,128)(2,1)S(1)}, u32[]{:S(2)}, u32[]{:S(2)}) %collective-permute-start.10) | collective-permute-done | bytes 28704 | tf_op jit(solution)/shard_map/ppermute | solution.py:485
  21.4 2.4 %collective-permute-done.11.rest_5_ = s16[112,128]{1,0:T(8,128)(2,1)S(1)} collective-permute-done((s16[112,128]{1,0:T(8,128)(2,1)S(1)}, s16[112,128]{1,0:T(8,128)(2,1)S(1)}, u32[]{:S(2)}, u32[]{:S(2)}) %collective-permute-start.11) | collective-permute-done | bytes 28704 | tf_op jit(solution)/shard_map/ppermute | solution.py:485
  23.7 0.6 %collective-permute-done.9.rest_1_ = s16[112,128]{1,0:T(8,128)(2,1)S(1)} collective-permute-done((s16[112,128]{1,0:T(8,128)(2,1)S(1)}, s16[112,128]{1,0:T(8,128)(2,1)S(1)}, u32[]{:S(2)}, u32[]{:S(2)}) %collective-permute-start.9) | collective-permute-done | bytes 28704 | tf_op jit(solution)/shard_map/ppermute | solution.py:485
  24.3 0.1 collective-permute-start.12
  24.4 0.5 %collective-permute-start.8 = (s16[112,128]{1,0:T(8,128)(2,1)S(1)}, s16[112,128]{1,0:T(8,128)(2,1)S(1)}, u32[]{:S(2)}, u32[]{:S(2)}) collective-permute-start(s16[112,128]{1,0:T(8,128)(2,1)S(1)} %get-tuple-element.37), channel_id=1, source_target_pairs={{0,4},{4,0},{8,12},{12,8},{16,20},{20,16},{24,28},{28,24},{1,5},{5... | collective-permute-start | bytes 86024 | tf_op jit(solution)/shard_map/ppermute | solution.py:485
  24.9 0.1 collective-permute-start.6
  25.0 0.7 %collective-permute-done.12 = s16[336,128]{1,0:T(8,128)(2,1)S(1)} collective-permute-done((s16[336,128]{1,0:T(8,128)(2,1)S(1)}, s16[336,128]{1,0:T(8,128)(2,1)S(1)}, u32[]{:S(2)}, u32[]{:S(2)}) %collective-permute-start.12) | collective-permute-done | bytes 86048 | tf_op jit(solution)/shard_map/ppermute | solution.py:485
  25.8 0.6 %collective-permute-done.6.rest_0_ = s16[768,128]{1,0:T(8,128)(2,1)S(1)} collective-permute-done((s16[768,128]{1,0:T(8,128)(2,1)S(1)}, s16[768,128]{1,0:T(8,128)(2,1)S(1)}, u32[]{:S(2)}, u32[]{:S(2)}) %collective-permute-start.6) | collective-permute-done | bytes 196640 | tf_op jit(solution)/shard_map/ppermute | solution.py:485
  26.4 4.7 %base.1 = (f32[28,3,8,128]{3,2,1,0:T(8,128)S(1)}, f32[28,3,8,128]{3,2,1,0:T(8,128)S(1)}, f32[170,9,8,128]{3,2,1,0:T(8,128)S(1)}) custom-call(s32[1]{0:T(128)} %bitcast.parity, f32[8,128]{1,0:T(8,128)S(1)} %get-tuple-element.21.tables, f32[768,128]{1,0:T(8,128)S(1)} %get-tuple-element.22.own, s16[768,128]{1,0:T(8,128)(2,1)S(1)} %collective-permute-done.6.rest_0_, ...), custom_call_target="tpu_custom_call" | custom-call | bytes 18500000 | tf_op jit(solution)/shard_map/base/pallas_call | solution.py:457
  31.1 3.6 %tangent.1 = (f32[288,128]{1,0:T(8,128)}, f32[288,128]{1,0:T(8,128)}) custom-call(s32[1]{0:T(128)} %bitcast.parity, f32[28,3,8,128]{3,2,1,0:T(8,128)S(1)} %get-tuple-element.33.coef, f32[28,3,8,128]{3,2,1,0:T(8,128)S(1)} %get-tuple-element.34.gain, f32[170,9,8,128]{3,2,1,0:T(8,128)S(1)} %get-tuple-element.35.moves, f32[96,128]{1,0:T(8,128)S(1)} %get-tuple-element.36.own, ...), custom_call_target="tpu_custom_call" | custom-call | bytes 14800000 | tf_op jit(solution)/shard_map/tangent/pallas_call | solution.py:457
  (10 shorter events, 0.1 us)
Async XLA Ops:
  2.2 15.0 %collective-permute-start = (s16[768,128]{1,0:T(8,128)(2,1)S(1)}, s16[768,128]{1,0:T(8,128)(2,1)S(1)}, u32[]{:S(2)}, u32[]{:S(2)}) collective-permute-start(s16[768,128]{1,0:T(8,128)(2,1)S(1)} %get-tuple-element.29), channel_id=1, source_target_pairs={{0,16},{4,20},{8,24},{12,28},{16,0},{20,4},{24,8},{28,12},{1,17},{... | collective-permute-start | bytes 589832 | tf_op jit(solution)/shard_map/ppermute | solution.py:485
  5.2 12.1 %collective-permute-start.1 = (s16[768,128]{1,0:T(8,128)(2,1)S(1)}, s16[768,128]{1,0:T(8,128)(2,1)S(1)}, u32[]{:S(2)}, u32[]{:S(2)}) collective-permute-start(s16[768,128]{1,0:T(8,128)(2,1)S(1)} %get-tuple-element.29), channel_id=1, source_target_pairs={{0,8},{4,12},{8,0},{12,4},{16,24},{20,28},{24,16},{28,20},{1,9},{5... | collective-permute-start | bytes 589832 | tf_op jit(solution)/shard_map/ppermute | solution.py:485
  6.7 10.5 %collective-permute-start.2 = (s16[768,128]{1,0:T(8,128)(2,1)S(1)}, s16[768,128]{1,0:T(8,128)(2,1)S(1)}, u32[]{:S(2)}, u32[]{:S(2)}) collective-permute-start(s16[768,128]{1,0:T(8,128)(2,1)S(1)} %get-tuple-element.29), channel_id=1, source_target_pairs={{0,24},{4,28},{8,16},{12,20},{16,8},{20,12},{24,0},{28,4},{1,25},{... | collective-permute-start | bytes 589832 | tf_op jit(solution)/shard_map/ppermute | solution.py:485
  6.8 4.6 %collective-permute-start.3 = (s16[112,128]{1,0:T(8,128)(2,1)S(1)}, s16[112,128]{1,0:T(8,128)(2,1)S(1)}, u32[]{:S(2)}, u32[]{:S(2)}) collective-permute-start(s16[112,128]{1,0:T(8,128)(2,1)S(1)} %get-tuple-element.25), channel_id=1, source_target_pairs={{0,1},{1,0},{2,3},{3,2},{4,5},{5,4},{6,7},{7,6},{8,9},{9,8},{10,11... | collective-permute-start | bytes 86024 | tf_op jit(solution)/shard_map/ppermute | solution.py:488
  8.8 5.9 %collective-permute-start.4 = (s16[112,128]{1,0:T(8,128)(2,1)S(1)}, s16[112,128]{1,0:T(8,128)(2,1)S(1)}, u32[]{:S(2)}, u32[]{:S(2)}) collective-permute-start(s16[112,128]{1,0:T(8,128)(2,1)S(1)} %get-tuple-element.26), channel_id=1, source_target_pairs={{0,2},{1,3},{2,0},{3,1},{4,6},{5,7},{6,4},{7,5},{8,10},{9,11},{10,... | collective-permute-start | bytes 86024 | tf_op jit(solution)/shard_map/ppermute | solution.py:488
  11.4 5.7 %collective-permute-start.5 = (s16[112,128]{1,0:T(8,128)(2,1)S(1)}, s16[112,128]{1,0:T(8,128)(2,1)S(1)}, u32[]{:S(2)}, u32[]{:S(2)}) collective-permute-start(s16[112,128]{1,0:T(8,128)(2,1)S(1)} %get-tuple-element.27), channel_id=1, source_target_pairs={{0,3},{1,2},{2,1},{3,0},{4,7},{5,6},{6,5},{7,4},{8,11},{9,10},{10,... | collective-permute-start | bytes 86024 | tf_op jit(solution)/shard_map/ppermute | solution.py:488
  17.3 8.4 %collective-permute-start.7 = (s16[2304,128]{1,0:T(8,128)(2,1)S(1)}, s16[2304,128]{1,0:T(8,128)(2,1)S(1)}, u32[]{:S(2)}, u32[]{:S(2)}) collective-permute-start(s16[2304,128]{1,0:T(8,128)(2,1)S(1)} %pad_add_fusion), channel_id=1, source_target_pairs={{0,4},{4,0},{8,12},{12,8},{16,20},{20,16},{24,28},{28,24},{1,5},{5... | collective-permute-start | bytes 1769480 | tf_op jit(solution)/shard_map/ppermute | solution.py:485
  17.4 3.9 %collective-permute-start.10 = (s16[112,128]{1,0:T(8,128)(2,1)S(1)}, s16[112,128]{1,0:T(8,128)(2,1)S(1)}, u32[]{:S(2)}, u32[]{:S(2)}) collective-permute-start(s16[112,128]{1,0:T(8,128)(2,1)S(1)} %get-tuple-element.37), channel_id=1, source_target_pairs={{0,16},{4,20},{8,24},{12,28},{16,0},{20,4},{24,8},{28,12},{1,17},{... | collective-permute-start | bytes 86024 | tf_op jit(solution)/shard_map/ppermute | solution.py:485
  19.0 4.8 %collective-permute-start.11 = (s16[112,128]{1,0:T(8,128)(2,1)S(1)}, s16[112,128]{1,0:T(8,128)(2,1)S(1)}, u32[]{:S(2)}, u32[]{:S(2)}) collective-permute-start(s16[112,128]{1,0:T(8,128)(2,1)S(1)} %get-tuple-element.37), channel_id=1, source_target_pairs={{0,24},{4,28},{8,16},{12,20},{16,8},{20,12},{24,0},{28,4},{1,25},{... | collective-permute-start | bytes 86024 | tf_op jit(solution)/shard_map/ppermute | solution.py:485
  20.5 3.9 %collective-permute-start.9 = (s16[112,128]{1,0:T(8,128)(2,1)S(1)}, s16[112,128]{1,0:T(8,128)(2,1)S(1)}, u32[]{:S(2)}, u32[]{:S(2)}) collective-permute-start(s16[112,128]{1,0:T(8,128)(2,1)S(1)} %get-tuple-element.37), channel_id=1, source_target_pairs={{0,8},{4,12},{8,0},{12,4},{16,24},{20,28},{24,16},{28,20},{1,9},{5... | collective-permute-start | bytes 86024 | tf_op jit(solution)/shard_map/ppermute | solution.py:485
  24.3 1.3 %collective-permute-start.12 = (s16[336,128]{1,0:T(8,128)(2,1)S(1)}, s16[336,128]{1,0:T(8,128)(2,1)S(1)}, u32[]{:S(2)}, u32[]{:S(2)}) collective-permute-start(s16[336,128]{1,0:T(8,128)(2,1)S(1)} %pad_add_fusion.1), channel_id=1, source_target_pairs={{0,4},{4,0},{8,12},{12,8},{16,20},{20,16},{24,28},{28,24},{1,5},{5... | collective-permute-start | bytes 258056 | tf_op jit(solution)/shard_map/ppermute | solution.py:485
  24.4 6.6 %collective-permute-start.8 = (s16[112,128]{1,0:T(8,128)(2,1)S(1)}, s16[112,128]{1,0:T(8,128)(2,1)S(1)}, u32[]{:S(2)}, u32[]{:S(2)}) collective-permute-start(s16[112,128]{1,0:T(8,128)(2,1)S(1)} %get-tuple-element.37), channel_id=1, source_target_pairs={{0,4},{4,0},{8,12},{12,8},{16,20},{20,16},{24,28},{28,24},{1,5},{5... | collective-permute-start | bytes 86024 | tf_op jit(solution)/shard_map/ppermute | solution.py:485
  24.9 1.4 %collective-permute-start.6 = (s16[768,128]{1,0:T(8,128)(2,1)S(1)}, s16[768,128]{1,0:T(8,128)(2,1)S(1)}, u32[]{:S(2)}, u32[]{:S(2)}) collective-permute-start(s16[768,128]{1,0:T(8,128)(2,1)S(1)} %get-tuple-element.29), channel_id=1, source_target_pairs={{0,4},{4,0},{8,12},{12,8},{16,20},{20,16},{24,28},{28,24},{1,5},{5... | collective-permute-start | bytes 589832 | tf_op jit(solution)/shard_map/ppermute | solution.py:485

commit v3 on v2

--- a/solution.py
+++ b/solution.py
@@ -16,6 +16,7 @@
 TILE = 8
 FULL = 32000.0
 FINE = 256.0
+FIRST_STEPS = 5
 CHUNK = 13
 F32 = jnp.float32
 VMEM_LIMIT = 24 * 1024 * 1024
@@ -331,14 +332,27 @@
 
             lax.fori_loop(0, count // each, some, 0)
 
+    base_steps(size, range(FIRST_STEPS), coef, profile, moves, (electric, magnetic), (electric, magnetic))
+
+
+def later_kernel(size, coef, profile, electric, magnetic, moves, electric_held, magnetic_held):
+    base_steps(
+        size, range(FIRST_STEPS, STEPS), coef, profile, moves, (electric, magnetic), (electric_held, magnetic_held)
+    )
+
+
+def base_steps(size, steps, coef, profile, moves, fields, held):
+    nx, ny = size
+    ratio = nx // GROUP
+    to_electric, to_magnetic = held
     moved = 0
-    for step in range(STEPS):
+    for step in steps:
+        electric, magnetic = fields if step == steps[0] else held
         wave = math.cos(OMEGA_FREQ * (step + 0.5) * DT_STEP)
         first, end = rows_of(step, ny)
         now = load_row(electric, first - 1, ratio)
         above = load_row(electric, first, ratio)
         new = add_curl_forward(load_row(magnetic, first - 1, ratio), now, above)
-
         below_x, below_z = new[0], new[2]
         for run in chunks(first, end):
             field = [above] + [load_row(electric, at + 1, ratio) for at in run]
@@ -354,15 +368,15 @@
                 change = [[coef[at, r] * drive[c][r] for r in range(ratio)] for c in range(3)]
                 store_row(moves, at - first + moved, change)
                 if step < STEPS - 1:
-                    store_row(magnetic, at, new[i])
+                    store_row(to_magnetic, at, new[i])
                     store_row(
-                        electric, at,
+                        to_electric, at,
                         [[p + q for p, q in zip(field[i][c], change[c])] for c in range(3)],
                     )
         moved += end - first
 
 
-def tangent_kernel(size, order, parity, coef, gain, moves, own, *rest):
+def tangent_kernel(size, order, parity, coef, gain, moves_first, moves_later, own, *rest):
     nx, ny = size
     ratio, plane = nx // GROUP, nx * ny
     n_blocks = 4 * len(set(order)) - 1
@@ -406,6 +420,9 @@
     moved = 0
     for step in range(STEPS):
         first, end = rows_of(step, ny)
+        if step == FIRST_STEPS:
+            moved = 0
+        moves = moves_first if step < FIRST_STEPS else moves_later
         shift = moved - first
         if step == 0:
 
@@ -521,15 +538,14 @@
         far = [over_xy(block, dx, 2) for dx in moves_x]
         return near, far
 
+    parts = [over_mode(parts[d], d + 1) for d in reversed(range(len(parts)))]
     near, far = gather(packed)
-    parts = [over_mode(part, d + 1) for d, part in enumerate(parts)]
 
     def with_core(near, far):
-        got = near[1:] + far
+        got = near + far
         sent = over_xy(jnp.concatenate(got, 0), 0, 1)
         rows = got[0].shape[0]
-        first = over_xy(near[0], 0, 1)
-        other = [first] + [sent[rows * i : rows * i + rows] for i in range(len(got))]
+        other = [sent[rows * i : rows * i + rows] for i in range(len(got))]
         other_near, other_far = other[: len(near)], other[len(near) :]
         return [b for four in zip(near, other_near, far, other_far) for b in four]
 
@@ -541,21 +557,31 @@
     near, far, deps_packed = lax.optimization_barrier((near, far, deps_packed))
     blocks = with_core(near, far)
     rows = ny + 2 * STEPS
-    moved = sum(rows_of(step, ny)[1] - rows_of(step, ny)[0] for step in range(STEPS))
-    coef, gain, moves = call(
+    counts = [rows_of(step, ny)[1] - rows_of(step, ny)[0] for step in range(STEPS)]
+    moved = [sum(counts[:FIRST_STEPS]), sum(counts[FIRST_STEPS:])]
+    plane_shape, field_shape = (rows, ratio, groups, nz), (rows, 3 * ratio, groups, nz)
+    deps_near, deps_far = gather(deps_packed)
+    coef, gain, moves_first, electric, magnetic, profile = call(
         functools.partial(base_kernel, size, order), "base",
-        (f32(rows, ratio, groups, nz), f32(rows, ratio, groups, nz), f32(moved, 3 * ratio, groups, nz)),
+        (f32(*plane_shape), f32(*plane_shape), f32(moved[0], *field_shape[1:]), f32(*field_shape), f32(*field_shape), f32(*plane_shape)),
         [smem] + [vmem] * (1 + len(blocks)),
-        [pltpu.VMEM((rows, 3 * ratio, groups, nz), F32)] * 2 + [pltpu.VMEM((rows, ratio, groups, nz), F32)],
-        5.0, (parity, tables, own, *blocks[1:]),
-    )
-    deps = with_core(*gather(deps_packed))
+        [], 3.5, (parity, tables, own, *blocks[1:]),
+    )
+    deps_near, deps_far, coef, gain, moves_first = lax.optimization_barrier(
+        (deps_near, deps_far, coef, gain, moves_first)
+    )
+    deps = with_core(deps_near, deps_far)
+    (moves_later,) = call(
+        functools.partial(later_kernel, size), "later",
+        (f32(moved[1], *field_shape[1:]),), [vmem] * 4, [pltpu.VMEM(field_shape, F32)] * 2,
+        1.5, (coef, profile, electric, magnetic),
+    )
     out_e, out_h = call(
         functools.partial(tangent_kernel, size, order), "tangent",
         (f32(3 * plane, nz), f32(3 * plane, nz)),
-        [smem] + [vmem] * (3 + len(deps)),
-        [pltpu.VMEM((rows, 3 * ratio, groups, nz), F32)] * 2 + [pltpu.VMEM((rows, ratio, groups, nz), F32)],
-        4.0, (parity, coef, gain, moves, deps_own, *deps[1:]),
+        [smem] + [vmem] * (4 + len(deps)),
+        [pltpu.VMEM(field_shape, F32)] * 2 + [pltpu.VMEM(plane_shape, F32)],
+        4.0, (parity, coef, gain, moves_first, moves_later, deps_own, *deps[1:]),
     )
     shape = (1, 3, nx, ny, nz)
     return out_e.reshape(shape), out_h.reshape(shape)

time: 34.8 us -> 29.7 us (0.85)
  starting transfers between devices: 16.7 us -> 12.3 us
  waiting for transfers between devices: 7.03 us -> 5.94 us
  Pallas kernels: 10 us -> 10.4 us
    ppermute x10 -> x8, waiting for transfers between devices: 4.67 us -> 0.19 us  [over_xy(): return lax.ppermute(block, ('gx', 'gy'), route)]
    ppermute x3, starting transfers between devices: 7.92 us -> 4.01 us  [over_mode(): return lax.ppermute(block, 'mode', [(i, i ^ flip) for i in range(n_mode)])]
    ppermute x3, waiting for transfers between devices: 2.37 us -> 5.76 us  [over_mode(): return lax.ppermute(block, 'mode', [(i, i ^ flip) for i in range(n_mode)])]
    ppermute x10 -> x8, starting transfers between devices: 8.81 us -> 8.3 us  [over_xy(): return lax.ppermute(block, ('gx', 'gy'), route)]
    pallas_call x4 -> x5, Pallas kernels: 10 us -> 10.4 us  [call(): pl.pallas_call(kernel, out_shape=outs, in_specs=specs, out_specs=tuple((p...]
  transfers between devices with their start and end apart: 13 -> 11, of which waited for: 6 -> 4; matrix products, arithmetic and copies ran while one was open for 0% -> 0% of each run, Pallas kernels for 14% -> 18%
where the time goes in v3:
time: 29.7 us; the launch traced here: 29.5 us
  starting transfers between devices  12.3 us (41%)
  Pallas kernels  10.4 us (35%)
  waiting for transfers between devices  5.94 us (20%)
  between operations  0.77 us (3%)
    pallas_call x5, Pallas kernels, call(): pl.pallas_call(kernel, out_shape=outs, in_specs=specs, out_specs=tuple((p...  10.4 us
    ppermute x8, starting transfers between devices, over_xy(): return lax.ppermute(block, ('gx', 'gy'), route)  8.3 us
    ppermute x3, waiting for transfers between devices, over_mode(): return lax.ppermute(block, 'mode', [(i, i ^ flip) for i in range(n_mode)])  5.76 us
    ppermute x3, starting transfers between devices, over_mode(): return lax.ppermute(block, 'mode', [(i, i ^ flip) for i in range(n_mode)])  4.01 us
  transfers between devices with their start and end apart: 11, of which 4 were waited for; matrix products, arithmetic and copies ran while one was open for 0% of the time, Pallas kernels for 18%

profile of v3, /device:TPU:0, one launch (start us, length us, event | category | flops | bytes accessed | tf_op | source)
XLA Modules:
  0.0 29.5 jit_solution(12351803465941128370)
XLA Ops:
  0.6 1.6 %pack.1 = (s16[768,128]{1,0:T(8,128)(2,1)S(1)}, f32[768,128]{1,0:T(8,128)S(1)}, f32[96,128]{1,0:T(8,128)S(1)}, f32[8,128]{1,0:T(8,128)S(1)}, s16[112,128]{1,0:T(...) custom-call(s32[1]{0:T(128)} %bitcast.1.me, s32[16]{0:T(128)} %modes_at.1, f32[3]{0:T(128)} %levels_at.1, ...), custom_call_target="tpu_custom_call" | custom-call | bytes 5550000 | tf_op jit(solution)/shard_map/pack/pallas_call | solution.py:474
  2.2 4.0 %collective-permute-start.2 = (s16[768,128]{1,0:T(8,128)(2,1)S(1)}, s16[768,128]{1,0:T(8,128)(2,1)S(1)}, u32[]{:S(2)}, u32[]{:S(2)}) collective-permute-start(s16[768,128]{1,0:T(8,128)(2,1)S(1)} %get-tuple-element.40), channel_id=1, source_target_pairs={{0,24},{4,28},{8,16},{12,20},{16,8},{20,12},{24,0},{28,4},{1,25},{... | collective-permute-start | bytes 589832 | tf_op jit(solution)/shard_map/ppermute | solution.py:502
  6.2 0.5 %collective-permute-start.1 = (s16[768,128]{1,0:T(8,128)(2,1)S(1)}, s16[768,128]{1,0:T(8,128)(2,1)S(1)}, u32[]{:S(2)}, u32[]{:S(2)}) collective-permute-start(s16[768,128]{1,0:T(8,128)(2,1)S(1)} %get-tuple-element.40), channel_id=1, source_target_pairs={{0,8},{4,12},{8,0},{12,4},{16,24},{20,28},{24,16},{28,20},{1,9},{5... | collective-permute-start | bytes 589832 | tf_op jit(solution)/shard_map/ppermute | solution.py:502
  6.7 0.1 collective-permute-start
  6.8 4.0 %collective-permute-start.3 = (s16[112,128]{1,0:T(8,128)(2,1)S(1)}, s16[112,128]{1,0:T(8,128)(2,1)S(1)}, u32[]{:S(2)}, u32[]{:S(2)}) collective-permute-start(s16[112,128]{1,0:T(8,128)(2,1)S(1)} %get-tuple-element.33), channel_id=1, source_target_pairs={{0,3},{1,2},{2,1},{3,0},{4,7},{5,6},{6,5},{7,4},{8,11},{9,10},{10,... | collective-permute-start | bytes 86024 | tf_op jit(solution)/shard_map/ppermute | solution.py:505
  10.8 1.9 %collective-permute-done.3.rest_0_ = s16[112,128]{1,0:T(8,128)(2,1)S(1)} collective-permute-done((s16[112,128]{1,0:T(8,128)(2,1)S(1)}, s16[112,128]{1,0:T(8,128)(2,1)S(1)}, u32[]{:S(2)}, u32[]{:S(2)}) %collective-permute-start.3) | collective-permute-done | bytes 28704 | tf_op jit(solution)/shard_map/ppermute | solution.py:505
  12.7 0.0 collective-permute-start.5
  12.7 2.9 %collective-permute-done.4.rest_1_ = s16[112,128]{1,0:T(8,128)(2,1)S(1)} collective-permute-done((s16[112,128]{1,0:T(8,128)(2,1)S(1)}, s16[112,128]{1,0:T(8,128)(2,1)S(1)}, u32[]{:S(2)}, u32[]{:S(2)}) %collective-permute-start.4) | collective-permute-done | bytes 28704 | tf_op jit(solution)/shard_map/ppermute | solution.py:505
  15.6 1.0 %collective-permute-done.5.rest_2_ = s16[112,128]{1,0:T(8,128)(2,1)S(1)} collective-permute-done((s16[112,128]{1,0:T(8,128)(2,1)S(1)}, s16[112,128]{1,0:T(8,128)(2,1)S(1)}, u32[]{:S(2)}, u32[]{:S(2)}) %collective-permute-start.5) | collective-permute-done | bytes 28704 | tf_op jit(solution)/shard_map/ppermute | solution.py:505
  16.6 0.2 sum.1
  16.8 0.0 collective-permute-done.2.rest_5_
  16.8 0.0 collective-permute-done.1.rest_1_
  16.8 0.1 pad_add_fusion
  16.9 0.1 collective-permute-start.9
  17.0 2.7 %collective-permute-start.8 = (s16[112,128]{1,0:T(8,128)(2,1)S(1)}, s16[112,128]{1,0:T(8,128)(2,1)S(1)}, u32[]{:S(2)}, u32[]{:S(2)}) collective-permute-start(s16[112,128]{1,0:T(8,128)(2,1)S(1)} %get-tuple-element.54), channel_id=1, source_target_pairs={{0,24},{4,28},{8,16},{12,20},{16,8},{20,12},{24,0},{28,4},{1,25},{... | collective-permute-start | bytes 86024 | tf_op jit(solution)/shard_map/ppermute | solution.py:502
  19.7 0.5 %collective-permute-start.7 = (s16[112,128]{1,0:T(8,128)(2,1)S(1)}, s16[112,128]{1,0:T(8,128)(2,1)S(1)}, u32[]{:S(2)}, u32[]{:S(2)}) collective-permute-start(s16[112,128]{1,0:T(8,128)(2,1)S(1)} %get-tuple-element.54), channel_id=1, source_target_pairs={{0,8},{4,12},{8,0},{12,4},{16,24},{20,28},{24,16},{28,20},{1,9},{5... | collective-permute-start | bytes 86024 | tf_op jit(solution)/shard_map/ppermute | solution.py:502
  20.2 0.4 %collective-permute-start.6 = (s16[112,128]{1,0:T(8,128)(2,1)S(1)}, s16[112,128]{1,0:T(8,128)(2,1)S(1)}, u32[]{:S(2)}, u32[]{:S(2)}) collective-permute-start(s16[112,128]{1,0:T(8,128)(2,1)S(1)} %get-tuple-element.54), channel_id=1, source_target_pairs={{0,16},{4,20},{8,24},{12,28},{16,0},{20,4},{24,8},{28,12},{1,17},{... | collective-permute-start | bytes 86024 | tf_op jit(solution)/shard_map/ppermute | solution.py:502
  20.5 0.0 collective-permute-done.9
  20.5 0.1 fusion
  20.6 3.9 %base.1 = (f32[28,3,8,128]{3,2,1,0:T(8,128)S(1)}, f32[28,3,8,128]{3,2,1,0:T(8,128)S(1)}, f32[110,9,8,128]{3,2,1,0:T(8,128)S(1)}, f32[28,9,8,128]{3,2,1,0:T(8,128...) custom-call(s32[1]{0:T(128)} %bitcast.parity, f32[8,128]{1,0:T(8,128)S(1)} %get-tuple-element.38.tables, ...), custom_call_target="tpu_custom_call" | custom-call | bytes 12950000 | tf_op jit(solution)/shard_map/base/pallas_call | solution.py:474
  24.6 0.1 collective-permute-start.10
  24.6 1.1 %later.1.moves_later = f32[60,9,8,128]{3,2,1,0:T(8,128)S(1)} custom-call(f32[28,3,8,128]{3,2,1,0:T(8,128)S(1)} %get-tuple-element.47.coef, f32[28,3,8,128]{3,2,1,0:T(8,128)S(1)} %get-tuple-element.50.profile, f32[28,9,8,128]{3,2,1,0:T(8,128)S(1)} %get-tuple-element.51.electric, f32[28,9,8,128]{3,2,1,0:T(8,128)S(1)} %get-tuple-element.52.magnetic), custom_call_target="tpu_custom_call" | custom-call | bytes 5550000 | tf_op jit(solution)/shard_map/later/pallas_call | solution.py:474
  25.8 0.2 collective-permute-done.10
  26.0 3.5 %tangent.1 = (f32[288,128]{1,0:T(8,128)}, f32[288,128]{1,0:T(8,128)}) custom-call(s32[1]{0:T(128)} %bitcast.parity, f32[28,3,8,128]{3,2,1,0:T(8,128)S(1)} %get-tuple-element.47.coef, f32[28,3,8,128]{3,2,1,0:T(8,128)S(1)} %get-tuple-element.48.gain, f32[110,9,8,128]{3,2,1,0:T(8,128)S(1)} %get-tuple-element.49.moves_first, ...), custom_call_target="tpu_custom_call" | custom-call | bytes 14800000 | tf_op jit(solution)/shard_map/tangent/pallas_call | solution.py:474
  (7 shorter events, 0.0 us)
Async XLA Ops:
  2.2 14.6 %collective-permute-start.2 = (s16[768,128]{1,0:T(8,128)(2,1)S(1)}, s16[768,128]{1,0:T(8,128)(2,1)S(1)}, u32[]{:S(2)}, u32[]{:S(2)}) collective-permute-start(s16[768,128]{1,0:T(8,128)(2,1)S(1)} %get-tuple-element.40), channel_id=1, source_target_pairs={{0,24},{4,28},{8,16},{12,20},{16,8},{20,12},{24,0},{28,4},{1,25},{... | collective-permute-start | bytes 589832 | tf_op jit(solution)/shard_map/ppermute | solution.py:502
  6.2 10.6 %collective-permute-start.1 = (s16[768,128]{1,0:T(8,128)(2,1)S(1)}, s16[768,128]{1,0:T(8,128)(2,1)S(1)}, u32[]{:S(2)}, u32[]{:S(2)}) collective-permute-start(s16[768,128]{1,0:T(8,128)(2,1)S(1)} %get-tuple-element.40), channel_id=1, source_target_pairs={{0,8},{4,12},{8,0},{12,4},{16,24},{20,28},{24,16},{28,20},{1,9},{5... | collective-permute-start | bytes 589832 | tf_op jit(solution)/shard_map/ppermute | solution.py:502
  6.7 10.1 %collective-permute-start = (s16[768,128]{1,0:T(8,128)(2,1)S(1)}, s16[768,128]{1,0:T(8,128)(2,1)S(1)}, u32[]{:S(2)}, u32[]{:S(2)}) collective-permute-start(s16[768,128]{1,0:T(8,128)(2,1)S(1)} %get-tuple-element.40), channel_id=1, source_target_pairs={{0,16},{4,20},{8,24},{12,28},{16,0},{20,4},{24,8},{28,12},{1,17},{... | collective-permute-start | bytes 589832 | tf_op jit(solution)/shard_map/ppermute | solution.py:502
  6.8 5.9 %collective-permute-start.3 = (s16[112,128]{1,0:T(8,128)(2,1)S(1)}, s16[112,128]{1,0:T(8,128)(2,1)S(1)}, u32[]{:S(2)}, u32[]{:S(2)}) collective-permute-start(s16[112,128]{1,0:T(8,128)(2,1)S(1)} %get-tuple-element.33), channel_id=1, source_target_pairs={{0,3},{1,2},{2,1},{3,0},{4,7},{5,6},{6,5},{7,4},{8,11},{9,10},{10,... | collective-permute-start | bytes 86024 | tf_op jit(solution)/shard_map/ppermute | solution.py:505
  10.8 4.8 %collective-permute-start.4 = (s16[112,128]{1,0:T(8,128)(2,1)S(1)}, s16[112,128]{1,0:T(8,128)(2,1)S(1)}, u32[]{:S(2)}, u32[]{:S(2)}) collective-permute-start(s16[112,128]{1,0:T(8,128)(2,1)S(1)} %get-tuple-element.34), channel_id=1, source_target_pairs={{0,2},{1,3},{2,0},{3,1},{4,6},{5,7},{6,4},{7,5},{8,10},{9,11},{10,... | collective-permute-start | bytes 86024 | tf_op jit(solution)/shard_map/ppermute | solution.py:505
  12.7 3.9 %collective-permute-start.5 = (s16[112,128]{1,0:T(8,128)(2,1)S(1)}, s16[112,128]{1,0:T(8,128)(2,1)S(1)}, u32[]{:S(2)}, u32[]{:S(2)}) collective-permute-start(s16[112,128]{1,0:T(8,128)(2,1)S(1)} %get-tuple-element.35), channel_id=1, source_target_pairs={{0,1},{1,0},{2,3},{3,2},{4,5},{5,4},{6,7},{7,6},{8,9},{9,8},{10,11... | collective-permute-start | bytes 86024 | tf_op jit(solution)/shard_map/ppermute | solution.py:505
  16.9 3.6 %collective-permute-start.9 = (s16[3072,128]{1,0:T(8,128)(2,1)S(1)}, s16[3072,128]{1,0:T(8,128)(2,1)S(1)}, u32[]{:S(2)}, u32[]{:S(2)}) collective-permute-start(s16[3072,128]{1,0:T(8,128)(2,1)S(1)} %pad_add_fusion), channel_id=1, source_target_pairs={{0,4},{4,0},{8,12},{12,8},{16,20},{20,16},{24,28},{28,24},{1,5},{5... | collective-permute-start | bytes 2359304 | tf_op jit(solution)/shard_map/ppermute | solution.py:502
  17.0 7.5 %collective-permute-start.8 = (s16[112,128]{1,0:T(8,128)(2,1)S(1)}, s16[112,128]{1,0:T(8,128)(2,1)S(1)}, u32[]{:S(2)}, u32[]{:S(2)}) collective-permute-start(s16[112,128]{1,0:T(8,128)(2,1)S(1)} %get-tuple-element.54), channel_id=1, source_target_pairs={{0,24},{4,28},{8,16},{12,20},{16,8},{20,12},{24,0},{28,4},{1,25},{... | collective-permute-start | bytes 86024 | tf_op jit(solution)/shard_map/ppermute | solution.py:502
  19.7 4.9 %collective-permute-start.7 = (s16[112,128]{1,0:T(8,128)(2,1)S(1)}, s16[112,128]{1,0:T(8,128)(2,1)S(1)}, u32[]{:S(2)}, u32[]{:S(2)}) collective-permute-start(s16[112,128]{1,0:T(8,128)(2,1)S(1)} %get-tuple-element.54), channel_id=1, source_target_pairs={{0,8},{4,12},{8,0},{12,4},{16,24},{20,28},{24,16},{28,20},{1,9},{5... | collective-permute-start | bytes 86024 | tf_op jit(solution)/shard_map/ppermute | solution.py:502
  20.2 4.4 %collective-permute-start.6 = (s16[112,128]{1,0:T(8,128)(2,1)S(1)}, s16[112,128]{1,0:T(8,128)(2,1)S(1)}, u32[]{:S(2)}, u32[]{:S(2)}) collective-permute-start(s16[112,128]{1,0:T(8,128)(2,1)S(1)} %get-tuple-element.54), channel_id=1, source_target_pairs={{0,16},{4,20},{8,24},{12,28},{16,0},{20,4},{24,8},{28,12},{1,17},{... | collective-permute-start | bytes 86024 | tf_op jit(solution)/shard_map/ppermute | solution.py:502
  24.6 1.4 %collective-permute-start.10 = (s16[448,128]{1,0:T(8,128)(2,1)S(1)}, s16[448,128]{1,0:T(8,128)(2,1)S(1)}, u32[]{:S(2)}, u32[]{:S(2)}) collective-permute-start(s16[448,128]{1,0:T(8,128)(2,1)S(1)} %pad_add_fusion.1), channel_id=1, source_target_pairs={{0,4},{4,0},{8,12},{12,8},{16,20},{20,16},{24,28},{28,24},{1,5},{5... | collective-permute-start | bytes 344072 | tf_op jit(solution)/shard_map/ppermute | solution.py:502

commit v4 on v3

--- a/solution.py
+++ b/solution.py
@@ -16,7 +16,8 @@
 TILE = 8
 FULL = 32000.0
 FINE = 256.0
-FIRST_STEPS = 5
+FIRST_STEPS = 4
+SCALE_AT = 4 * 8
 CHUNK = 13
 F32 = jnp.float32
 VMEM_LIMIT = 24 * 1024 * 1024
@@ -50,12 +51,52 @@
     return jnp.broadcast_to(tile[:, at : at + 1], tile.shape)
 
 
+def code_tiles(total, k, codes):
+    rows, coded = iota(0, 16), []
+    for i in range(2):
+        tile = total[TILE * i : TILE * i + TILE]
+        code = scale_code(jnp.max(jnp.abs(tile), axis=(0, 1), keepdims=True))
+        coded.append(to_codes(tile, code))
+        codes = jnp.where(rows == 2 * k + i, code, codes)
+    return narrow(coded), codes
+
+
+def decoded(part, at, plane, k):
+    scales = scale_of(wide(part[at + plane : at + plane + 16]))
+    coded = wide(part[at + 16 * k : at + 16 * k + 16])
+    return [coded[TILE * i : TILE * i + TILE] * scales[2 * k + i : 2 * k + i + 1] for i in range(2)]
+
+
+def half_kernel(size, near_part, far_parts, part):
+    plane = size[0] * size[1]
+    codes = jnp.zeros((16, 128), F32)
+    for k in range(plane // 16):
+        total = near_part[16 * k : 16 * k + 16] + jnp.concatenate(decoded(far_parts, plane + 16, plane, k), 0)
+        part[16 * k : 16 * k + 16], codes = code_tiles(total, k, codes)
+    part[plane:] = narrow([codes])
+
+
+def field_rows(size, y, r):
+    nx, ny = size
+    ratio = nx // GROUP
+    second, third = 16 * ny * ratio, 24 * ny * ratio
+    return (
+        (y * ratio + r) * 16,
+        second + (y // 2 * ratio + r) * 16 + y % 2 * TILE,
+        third + (y // 4 * ratio + r) * 16 + y % 4 * GROUP,
+    )
+
+
+def info_row(size):
+    nx, ny = size
+    return 28 * ny * (nx // GROUP)
+
+
 def pack_kernel(
     size, me, modes_at, levels_at, gains_at, e_at, h_at, labels_at, kl_at, z_at, amp_at,
-    packed, own, own_part, tables, *rest,
+    packed, own, own_part, near_part, tables, far_parts, *rest,
 ):
     nx, ny = size
-    parts, rest = rest[:-11], rest[-11:]
     modes, levels, gains, e, h, labels, kl, source_z, source_amp, label_rows, sems = rest
     ratio, plane, stride = nx // GROUP, nx * ny, nx // GROUP * ny
     ends = zip(
@@ -76,84 +117,79 @@
     tables[6:8] = jnp.zeros((2, 128), F32)
     heights_of = source_z[...].astype(F32)
     amps_of = source_amp[...]
-    wide_lanes = lax.broadcasted_iota(jnp.int32, (TILE, nx), 1)
-    turned = lax.broadcasted_iota(jnp.int32, (TILE, nx), 0)
-
-    def column(values, y, r):
-        wanted = wide_lanes == (turned - GROUP) * ratio + r
-        picked = jnp.where(wanted, jnp.broadcast_to(values[y : y + 1], wanted.shape), 0.0)
-        return jnp.broadcast_to(jnp.sum(picked, axis=1, keepdims=True), (TILE, 128))
-
     low, lanes = iota(0) < GROUP, iota(1)
 
     blocks = kl.shape[0] // plane
-    rows16 = iota(0, 16)
     weights = [
-        [(modes[me[0] * blocks + j] == (me[0] ^ d)).astype(F32) for j in range(blocks)]
-        for d in range(len(parts) + 1)
+        [(modes[me[0] * blocks + j] == (me[0] ^ d)).astype(F32) for j in range(blocks)] for d in (0, 2, 1, 3)
     ]
-    codes = [jnp.zeros((16, 128), F32) for _ in parts]
+    codes = [jnp.zeros((16, 128), F32) for _ in range(2)]
     for k in range(plane // 16):
         tiles = [kl[j * plane + 16 * k : j * plane + 16 * k + 16].astype(F32) for j in range(blocks)]
-        for d in range(len(parts) + 1):
+        for d in range(4):
             total = sum(weights[d][j] * tiles[j] for j in range(blocks))
-            if d == 0:
-                own_part[16 * k : 16 * k + 16] = total
-                continue
-            halves = []
-            for i in range(2):
-                half = total[TILE * i : TILE * i + TILE]
-                code = scale_code(jnp.max(jnp.abs(half), axis=(0, 1), keepdims=True))
-                halves.append(to_codes(half, code))
-                codes[d - 1] = jnp.where(rows16 == 2 * k + i, code, codes[d - 1])
-            parts[d - 1][16 * k : 16 * k + 16] = narrow(halves)
-    for d, part in enumerate(parts):
-        part[plane:] = narrow([codes[d]])
-
-    for y in range(ny):
-        for r in range(ratio):
+            if d < 2:
+                (own_part, near_part)[d][16 * k : 16 * k + 16] = total
+            else:
+                first = (plane + 16) * (d - 2) + 16 * k
+                far_parts[first : first + 16], codes[d - 2] = code_tiles(total, k, codes[d - 2])
+    for i in range(2):
+        first = (plane + 16) * i + plane
+        far_parts[first : first + 16] = narrow([codes[i]])
+
+    info = jnp.zeros((TILE, 128), F32)
+    rows = iota(0)
+    for r in range(ratio):
+        labels_held = []
+        for y in range(ny):
             at = r * ny + y
             tiles = [e[pl.ds(at, TILE, stride=stride)], h[pl.ds(at, TILE, stride=stride)]]
             e_last = e[pl.ds(at + plane, TILE, stride=stride)]
             h_last = h[pl.ds(at + plane, TILE, stride=stride)]
             tiles.append(jnp.where(low, pltpu.roll(e_last, GROUP, 0), h_last))
-            label = label_rows[pl.ds(at, TILE, stride=stride)]
-            height, amp = column(heights_of, y, r), column(amps_of, y, r)
-            coded, meta = [], jnp.zeros((TILE, 128), F32)
+            coded = []
             for i, tile in enumerate(tiles):
-                code = scale_code(jnp.broadcast_to(jnp.max(jnp.abs(tile), axis=1, keepdims=True), tile.shape))
+                code = scale_code(jnp.max(jnp.abs(tile), axis=(0, 1), keepdims=True))
                 coded.append(to_codes(tile, code))
-                meta = jnp.where(lanes == 2 * i, pltpu.roll(code, GROUP, 0), meta)
-                meta = jnp.where(lanes == 2 * i + 1, code, meta)
-            meta = jnp.where(lanes == 6, height, meta)
-            amp_code = scale_code(jnp.abs(amp))
-            meta = jnp.where(lanes == 7, to_codes(amp, amp_code), meta)
-            meta = jnp.where(lanes == 8, amp_code, meta)
-            own_meta = jnp.where(lanes == 6, height, jnp.where(lanes == 7, amp, 0.0))
-            coded.append(jnp.where(low, label, meta))
-            tiles.append(jnp.where(low, label, own_meta))
-            base = (y * ratio + r) * 32
-            packed[base : base + 16] = narrow(coded[:2])
-            packed[base + 16 : base + 32] = narrow(coded[2:])
-            for i, tile in enumerate(tiles):
-                own[base + TILE * i : base + TILE * i + TILE] = tile
-
-
-def sum_kernel(size, own_part, *rest):
+                info = jnp.where((rows == y) & (lanes == SCALE_AT + i * ratio + r), code, info)
+            first, second, third = field_rows(size, y, r)
+            packed[first : first + 16] = narrow(coded[:2])
+            own[first : first + TILE] = tiles[0]
+            own[first + TILE : first + 16] = tiles[1]
+            own[second : second + TILE] = tiles[2]
+            labels_held.append(label_rows[pl.ds(at, TILE, stride=stride)])
+            if y % 2 == 0:
+                last_even = coded[2]
+                continue
+            packed[second - TILE : second + TILE] = narrow([last_even, coded[2]])
+            pair = jnp.where(low, labels_held[-2], pltpu.roll(labels_held[-1], GROUP, 0))
+            labels_held[-2:] = [pair]
+            third = third // TILE * TILE
+            own[third : third + TILE] = pair
+            if len(labels_held) == 2:
+                packed[third - TILE : third + TILE] = narrow(labels_held)
+                labels_held = []
+    amp_codes = scale_code(jnp.abs(amps_of))
+    sources = [heights_of, to_codes(amps_of, amp_codes), amp_codes, amps_of]
+    sources = jnp.concatenate([jnp.concatenate(sources, 0), jnp.zeros((4 * ny, 128 - nx), F32)], 1)
+    sources = jnp.concatenate([sources, jnp.zeros((128 - 4 * ny, 128), F32)], 0).T[:16]
+    lanes16 = iota(1, 16)
+    last = info_row(size)
+    info = jnp.concatenate([info, jnp.zeros((TILE, 128), F32)], 0)
+    packed[last : last + 16] = jnp.where(lanes16 < 3 * ny, sources, info).astype(jnp.int32).astype(jnp.int16)
+    own[last : last + 16] = jnp.where(lanes16 < ny, sources, pltpu.roll(sources, 128 - 2 * ny, 1))
+
+
+def sum_kernel(size, own_part, far_parts, near_part, packed, own, total):
     nx, ny = size
-    parts, (packed, own, total) = rest[:-3], rest[-3:]
     ratio, plane, stride = nx // GROUP, nx * ny, nx // GROUP * ny
-    scales = [scale_of(wide(part[plane : plane + 16])) for part in parts]
     total[:plane] = jnp.zeros((plane, 128), F32)
     total[2 * plane :] = jnp.zeros((plane, 128), F32)
     for k in range(plane // 16):
-        coded = [wide(part[16 * k : 16 * k + 16]) for part in parts]
-        for i in range(2):
+        both = zip(decoded(far_parts, 0, plane, k), decoded(near_part, 0, plane, k))
+        for i, (far, near) in enumerate(both):
             at = 16 * k + TILE * i
-            tile = own_part[at : at + TILE]
-            for c, s in zip(coded, scales):
-                tile = tile + c[TILE * i : TILE * i + TILE] * s[2 * k + i : 2 * k + i + 1]
-            total[plane + at : plane + at + TILE] = tile
+            total[plane + at : plane + at + TILE] = own_part[at : at + TILE] + far + near
     low, rows16 = iota(0) < GROUP, iota(0, 16)
     codes = jnp.zeros((16, 128), F32)
     held = []
@@ -269,7 +305,8 @@
 def base_kernel(size, order, parity, tables, own, *rest):
     nx, ny = size
     ratio = nx // GROUP
-    blocks, (coef, gain_out, moves, electric, magnetic, profile) = rest[:-6], rest[-6:]
+    blocks, rest = rest[:-8], rest[-8:]
+    coef, gain_out, moves, electric, magnetic, profile, scales, sources = rest
     blocks = (own,) + blocks
     low, lanes = iota(0) < GROUP, iota(1)
     table = [jnp.broadcast_to(tables[i : i + 1], (TILE, 128)) for i in range(6)]
@@ -277,60 +314,78 @@
     def pick(label, first):
         return jnp.where(label < 0.5, table[first], jnp.where(label < 1.5, table[first + 1], table[first + 2]))
 
-    def unpack(y_block, y, to):
+    last = info_row(size)
+    def prepare(y_block):
+        found = {}
+        for x_block in set(order):
+            block = 4 * x_block + y_block
+            if block == 0:
+                found[x_block] = own[last : last + 16]
+                continue
+            info = wide(blocks[block][last : last + 16])
+            scale = scale_of(info)
+            for i in range(3 * ratio):
+                at = (3 * ratio * block + i) * TILE
+                scales[at : at + TILE] = lane(scale[:TILE], SCALE_AT + i)
+            amps = info * pltpu.roll(scale, 128 - ny, 1)
+            found[x_block] = jnp.where(iota(1, 16) < ny, info, amps)
+        for i, x_block in enumerate(order):
+            at = (y_block * len(order) + i) * nx
+            sources[at : at + nx] = found[x_block][:nx]
+
+    def load_pair(block, pair, r):
+        out = []
+        for y in (2 * pair, 2 * pair + 1):
+            first, second, third = field_rows(size, y, r)
+            if block == 0:
+                tiles = [own[first : first + TILE], own[first + TILE : first + 16], own[second : second + TILE]]
+            else:
+                both = wide(blocks[block][first : first + 16])
+                at = second // 16 * 16
+                ends = wide(blocks[block][at : at + 16])[second - at : second - at + TILE]
+                tiles = [both[:TILE], both[TILE:], ends]
+                rows = [((3 * block + i) * ratio + r) * TILE + y for i in range(3)]
+                tiles = [t * scales[row : row + 1] for t, row in zip(tiles, rows)]
+            out.append(tiles)
+        third = field_rows(size, 2 * pair, r)[2]
+        if block == 0:
+            return out, own[third : third + TILE]
+        at = third // 16 * 16
+        return out, wide(blocks[block][at : at + 16])[third - at : third - at + TILE]
+
+    def unpack(y_block, pair, to):
         for r in range(ratio):
-            base = pl.multiple_of((y * ratio + r) * 32, 32)
-            outs = []
-            for first in range(0, len(order), 2):
-                pair, owned = [], []
-                for x_block in order[first : first + 2]:
-                    ref = blocks[4 * x_block + y_block]
-                    owned.append(x_block == 0 and y_block == 0)
-                    if owned[-1]:
-                        pair.append([ref[pl.ds(base + TILE * i, TILE)] for i in range(4)])
+            held = {x: load_pair(4 * x + y_block, pair, r) for x in set(order)}
+            for i, y in enumerate((2 * pair, 2 * pair + 1)):
+                outs = []
+                for k in range(0, len(order), 2):
+                    one, two = order[k], order[k + 1]
+                    tiles = [halves((held[one][0][i][j], held[two][0][i][j]), low) for j in range(3)]
+                    (ex, ey), (hx, hy), (ez, hz) = tiles
+                    label = halves((held[one][1], held[two][1]), low)[i]
+                    at = (y_block * len(order) + k) * nx
+                    source = sources[pl.ds(at + r, TILE, stride=ratio)]
+                    height, amp = lane(source, y), lane(source, ny + y)
+                    outs.append(
+                        [
+                            ex * DT_STEP, ey * DT_STEP, ez * DT_STEP, hx, hy, hz, pick(label, 0), pick(label, 3),
+                            jnp.where(lanes.astype(F32) == height, amp, 0.0),
+                        ]
+                    )
+                for j in range(9):
+                    tile = jnp.concatenate([o[j] for o in outs], 0) if len(outs) > 1 else outs[0][j]
+                    if j < 3:
+                        electric[to + i, j * ratio + r] = tile
+                    elif j < 6:
+                        magnetic[to + i, (j - 3) * ratio + r] = tile
                     else:
-                        both = [wide(ref[pl.ds(base + 16 * i, 16)]) for i in range(2)]
-                        pair.append([b[TILE * i : TILE * i + TILE] for b in both for i in range(2)])
-                planes = [p for i in range(4) for p in halves((pair[0][i], pair[1][i]), low)]
-                meta = planes[7]
-                scale = scale_of(meta)
-                mine = low if owned[0] else jnp.logical_not(low)
-
-                def scaled(value, at):
-                    factor = lane(scale, at)
-                    return value * (jnp.where(mine, 1.0, factor) if any(owned) else factor)
-
-                fields = [scaled(planes[i], i) for i in range(6)]
-                amp = scaled(lane(meta, 7), 8)
-                outs.append(
-                    [fields[i] * DT_STEP for i in (0, 1, 4)]
-                    + [fields[i] for i in (2, 3, 5)]
-                    + [
-                        pick(planes[6], 0),
-                        pick(planes[6], 3),
-                        jnp.where(lanes.astype(F32) == lane(meta, 6), amp, 0.0),
-                    ]
-                )
-            for i in range(9):
-                tile = jnp.concatenate([o[i] for o in outs], 0) if len(outs) > 1 else outs[0][i]
-                if i < 3:
-                    electric[to, i * ratio + r] = tile
-                elif i < 6:
-                    magnetic[to, (i - 3) * ratio + r] = tile
-                else:
-                    (coef, gain_out, profile)[i - 6][to, r] = tile
+                        (coef, gain_out, profile)[j - 6][to + i, r] = tile
 
     for y_block, pieces in enumerate(places(parity[0], ny)):
+        prepare(y_block)
         for first, count, to in pieces:
-
-            each = min(count, 4)
-
-            def some(j, _, y_block=y_block, first=first, to=to, each=each):
-                for i in range(each):
-                    unpack(y_block, first + each * j + i, to + each * j + i)
-                return 0
-
-            lax.fori_loop(0, count // each, some, 0)
+            for j in range(0, count, 2):
+                unpack(y_block, (first + j) // 2, to + j)
 
     base_steps(size, range(FIRST_STEPS), coef, profile, moves, (electric, magnetic), (electric, magnetic))
 
@@ -478,7 +533,7 @@
         out_specs=tuple(pl.BlockSpec(memory_space=pltpu.VMEM) for _ in outs),
         scratch_shapes=scratch,
         compiler_params=pltpu.CompilerParams(vmem_limit_bytes=vmem),
-        cost_estimate=pl.CostEstimate(flops=0, bytes_accessed=int(about_us * 3.7e6), transcendentals=0),
+        cost_estimate=pl.CostEstimate(flops=int(about_us * 1e9), bytes_accessed=0, transcendentals=0),
         name=name,
     )(*args)
 
@@ -486,7 +541,7 @@
 def body(sizes, e_init, h_init, eps_levels, region_gain, region_labels, kl_blocks, kl_modes, source_z, source_amp):
     n_gx, n_gy, n_mode = sizes
     _, nx, ny, nz = e_init.shape
-    assert n_gy == 4 and nx % GROUP == 0 and nx >= STEPS and ny < STEPS < 2 * ny
+    assert n_gy == 4 and n_mode == 4 and ny == TILE and nx <= 16 and nx % GROUP == 0 and nx >= STEPS and ny < STEPS < 2 * ny
     ratio, plane = nx // GROUP, nx * ny
     size = (nx, ny)
     vmem, smem, hbm = (pl.BlockSpec(memory_space=s) for s in (pltpu.VMEM, pltpu.SMEM, pltpu.HBM))
@@ -506,10 +561,12 @@
 
     me = lax.axis_index("mode").astype(jnp.int32).reshape(1)
     parity = (lax.axis_index("gy") % 2).astype(jnp.int32).reshape(1)
-    packed, own, own_part, tables, *parts = call(
+    packed, own, own_part, near_part, tables, far_parts = call(
         functools.partial(pack_kernel, size), "pack",
-        (i16(ny * ratio * 32, nz), f32(ny * ratio * 32, nz), f32(plane, nz), f32(TILE, nz))
-        + (i16(plane + 16, nz),) * (n_mode - 1),
+        (
+            i16(info_row(size) + 16, nz), f32(info_row(size) + 16, nz), f32(plane, nz), f32(plane, nz), f32(TILE, nz),
+            i16(2 * (plane + 16), nz),
+        ),
         [smem] + [hbm] * 9,
         [pltpu.SMEM(a.shape, a.dtype) for a in (kl_modes, eps_levels, region_gain)]
         + [pltpu.VMEM((3 * plane, nz), F32)] * 2
@@ -538,7 +595,12 @@
         far = [over_xy(block, dx, 2) for dx in moves_x]
         return near, far
 
-    parts = [over_mode(parts[d], d + 1) for d in reversed(range(len(parts)))]
+    far_parts = over_mode(far_parts, 1)
+    (near_part,) = call(
+        functools.partial(half_kernel, size), "half",
+        (i16(plane + 16, nz),), [vmem] * 2, [], 0.2, (near_part, far_parts),
+    )
+    near_part = over_mode(near_part, 2)
     near, far = gather(packed)
 
     def with_core(near, far):
@@ -551,10 +613,11 @@
 
     deps_packed, deps_own = call(
         functools.partial(sum_kernel, size), "sum",
-        (i16(plane + 16, nz), f32(plane, nz)), [vmem] * n_mode, [pltpu.VMEM((3 * plane, nz), F32)],
-        0.3, (own_part, *parts),
-    )
-    near, far, deps_packed = lax.optimization_barrier((near, far, deps_packed))
+        (i16(plane + 16, nz), f32(plane, nz)), [vmem] * 3, [pltpu.VMEM((3 * plane, nz), F32)],
+        1.2, (own_part, far_parts, near_part),
+    )
+    far, near, deps_packed = lax.optimization_barrier((far[::-1], near, deps_packed))
+    far = far[::-1]
     blocks = with_core(near, far)
     rows = ny + 2 * STEPS
     counts = [rows_of(step, ny)[1] - rows_of(step, ny)[0] for step in range(STEPS)]
@@ -565,12 +628,13 @@
         functools.partial(base_kernel, size, order), "base",
         (f32(*plane_shape), f32(*plane_shape), f32(moved[0], *field_shape[1:]), f32(*field_shape), f32(*field_shape), f32(*plane_shape)),
         [smem] + [vmem] * (1 + len(blocks)),
-        [], 3.5, (parity, tables, own, *blocks[1:]),
-    )
-    deps_near, deps_far, coef, gain, moves_first = lax.optimization_barrier(
-        (deps_near, deps_far, coef, gain, moves_first)
-    )
-    deps = with_core(deps_near, deps_far)
+        [pltpu.VMEM((12 * ratio * len(set(order)) * TILE, nz), F32), pltpu.VMEM((4 * len(order) * nx, nz), F32)],
+        3.5, (parity, tables, own, *blocks[1:]),
+    )
+    deps_far, deps_near, coef, gain, moves_first = lax.optimization_barrier(
+        (deps_far[::-1], deps_near, coef, gain, moves_first)
+    )
+    deps = with_core(deps_near, deps_far[::-1])
     (moves_later,) = call(
         functools.partial(later_kernel, size), "later",
         (f32(moved[1], *field_shape[1:]),), [vmem] * 4, [pltpu.VMEM(field_shape, F32)] * 2,

time: 29.7 us -> 28.5 us (0.960)
  waiting for transfers between devices: 5.94 us -> 4.72 us
  starting transfers between devices: 12.3 us -> 12.9 us
  Pallas kernels: 10.4 us -> 9.83 us
    ppermute x3 -> x2, waiting for transfers between devices: 5.76 us -> 2.49 us  [over_mode(): return lax.ppermute(block, 'mode', [(i, i ^ flip) for i in range(n_mode)])]
    ppermute x8, waiting for transfers between devices: 0.19 us -> 2.23 us  [over_xy(): return lax.ppermute(block, ('gx', 'gy'), route)]
    ppermute x3 -> x2, starting transfers between devices: 4.01 us -> 5.74 us  [over_mode(): return lax.ppermute(block, 'mode', [(i, i ^ flip) for i in range(n_mode)])]
    ppermute x8, starting transfers between devices: 8.3 us -> 7.18 us  [over_xy(): return lax.ppermute(block, ('gx', 'gy'), route)]
    pallas_call x5 -> x6, Pallas kernels: 10.4 us -> 9.83 us  [call(): pl.pallas_call(kernel, out_shape=outs, in_specs=specs, out_specs=tuple((p...]
  transfers between devices with their start and end apart: 11 -> 10, of which waited for: 4 -> 4; matrix products, arithmetic and copies ran while one was open for 0% -> 0% of each run, Pallas kernels for 18% -> 16%
where the time goes in v4:
time: 28.5 us; the launch traced here: 28.4 us
  starting transfers between devices  12.9 us (45%)
  Pallas kernels  9.83 us (34%)
  waiting for transfers between devices  4.72 us (17%)
  between operations  0.76 us (3%)
    pallas_call x6, Pallas kernels, call(): pl.pallas_call(kernel, out_shape=outs, in_specs=specs, out_specs=tuple((p...  9.83 us
    ppermute x8, starting transfers between devices, over_xy(): return lax.ppermute(block, ('gx', 'gy'), route)  7.18 us
    ppermute x2, starting transfers between devices, over_mode(): return lax.ppermute(block, 'mode', [(i, i ^ flip) for i in range(n_mode)])  5.74 us
    ppermute x2, waiting for transfers between devices, over_mode(): return lax.ppermute(block, 'mode', [(i, i ^ flip) for i in range(n_mode)])  2.49 us
    ppermute x8, waiting for transfers between devices, over_xy(): return lax.ppermute(block, ('gx', 'gy'), route)  2.23 us
  transfers between devices with their start and end apart: 10, of which 4 were waited for; matrix products, arithmetic and copies ran while one was open for 0% of the time, Pallas kernels for 16%

profile of v4, /device:TPU:0, one launch (start us, length us, event | category | flops | bytes accessed | tf_op | source)
XLA Modules:
  0.0 28.4 jit_solution(8223340051931609106)
XLA Ops:
  0.6 1.6 %pack.1 = (s16[688,128]{1,0:T(8,128)(2,1)S(1)}, f32[688,128]{1,0:T(8,128)S(1)}, f32[96,128]{1,0:T(8,128)S(1)}, f32[96,128]{1,0:T(8,128)S(1)}, f32[8,128]{1,0:T(8,128)S(1)}, /*index=5*/s16[224,128]{1,0:T(8,128)(2,1)S(1)}) custom-call(s32[1]{0:T(128)} %bitcast.1.me, s32[16]{0:T(128)} %modes_at.1, f32[3]{0:T(128)} %levels_at.1, f32[3]{0:T(128)} %gains_at.1, ...), custom_call_target="tpu_custom_call" | custom-call | flops 1500000000 | tf_op jit(solution)/shard_map/pack/pallas_call | solution.py:529
  2.2 3.1 %collective-permute-start.3 = (s16[224,128]{1,0:T(8,128)(2,1)S(1)}, s16[224,128]{1,0:T(8,128)(2,1)S(1)}, u32[]{:S(2)}, u32[]{:S(2)}) collective-permute-start(s16[224,128]{1,0:T(8,128)(2,1)S(1)} %get-tuple-element.32), channel_id=1, source_target_pairs={{0,1},{1,0},{2,3},{3,2},{4,5},{5,4},{6,7},{7,6},{8,9},{9,8},{10,11... | collective-permute-start | bytes 172040 | tf_op jit(solution)/shard_map/ppermute | solution.py:560
  5.3 2.4 %collective-permute-start = (s16[688,128]{1,0:T(8,128)(2,1)S(1)}, s16[688,128]{1,0:T(8,128)(2,1)S(1)}, u32[]{:S(2)}, u32[]{:S(2)}) collective-permute-start(s16[688,128]{1,0:T(8,128)(2,1)S(1)} %get-tuple-element.38), channel_id=1, source_target_pairs={{0,24},{4,28},{8,16},{12,20},{16,8},{20,12},{24,0},{28,4},{1,25},{... | collective-permute-start | bytes 528392 | tf_op jit(solution)/shard_map/ppermute | solution.py:557
  7.8 0.5 %collective-permute-start.1 = (s16[688,128]{1,0:T(8,128)(2,1)S(1)}, s16[688,128]{1,0:T(8,128)(2,1)S(1)}, u32[]{:S(2)}, u32[]{:S(2)}) collective-permute-start(s16[688,128]{1,0:T(8,128)(2,1)S(1)} %get-tuple-element.38), channel_id=1, source_target_pairs={{0,8},{4,12},{8,0},{12,4},{16,24},{20,28},{24,16},{28,20},{1,9},{5... | collective-permute-start | bytes 528392 | tf_op jit(solution)/shard_map/ppermute | solution.py:557
  8.3 0.5 %collective-permute-start.2 = (s16[688,128]{1,0:T(8,128)(2,1)S(1)}, s16[688,128]{1,0:T(8,128)(2,1)S(1)}, u32[]{:S(2)}, u32[]{:S(2)}) collective-permute-start(s16[688,128]{1,0:T(8,128)(2,1)S(1)} %get-tuple-element.38), channel_id=1, source_target_pairs={{0,16},{4,20},{8,24},{12,28},{16,0},{20,4},{24,8},{28,12},{1,17},{... | collective-permute-start | bytes 528392 | tf_op jit(solution)/shard_map/ppermute | solution.py:557
  8.8 0.0 collective-permute-done.3.far_parts
  8.8 0.2 half.1
  9.0 2.7 %collective-permute-start.4 = (s16[112,128]{1,0:T(8,128)(2,1)S(1)}, s16[112,128]{1,0:T(8,128)(2,1)S(1)}, u32[]{:S(2)}, u32[]{:S(2)}) collective-permute-start(s16[112,128]{1,0:T(8,128)(2,1)S(1)} %half.1), channel_id=1, source_target_pairs={{0,2},{1,3},{2,0},{3,1},{4,6},{5,7},{6,4},{7,5},{8,10},{9,11},{10,... | collective-permute-start | bytes 86024 | tf_op jit(solution)/shard_map/ppermute | solution.py:560
  11.6 2.5 %collective-permute-done.4.near_part = s16[112,128]{1,0:T(8,128)(2,1)S(1)} collective-permute-done((s16[112,128]{1,0:T(8,128)(2,1)S(1)}, s16[112,128]{1,0:T(8,128)(2,1)S(1)}, u32[]{:S(2)}, u32[]{:S(2)}) %collective-permute-start.4) | collective-permute-done | bytes 28704 | tf_op jit(solution)/shard_map/ppermute | solution.py:560
  14.1 0.2 sum.1
  14.3 0.0 collective-permute-done.rest_5_
  14.3 1.6 %collective-permute-done.1.rest_1_ = s16[688,128]{1,0:T(8,128)(2,1)S(1)} collective-permute-done((s16[688,128]{1,0:T(8,128)(2,1)S(1)}, s16[688,128]{1,0:T(8,128)(2,1)S(1)}, u32[]{:S(2)}, u32[]{:S(2)}) %collective-permute-start.1) | collective-permute-done | bytes 176160 | tf_op jit(solution)/shard_map/ppermute | solution.py:557
  15.9 0.1 collective-permute-done.2.rest_3_
  16.1 0.1 collective-permute-start.8
  16.1 1.7 %collective-permute-start.5 = (s16[112,128]{1,0:T(8,128)(2,1)S(1)}, s16[112,128]{1,0:T(8,128)(2,1)S(1)}, u32[]{:S(2)}, u32[]{:S(2)}) collective-permute-start(s16[112,128]{1,0:T(8,128)(2,1)S(1)} %get-tuple-element.52), channel_id=1, source_target_pairs={{0,24},{4,28},{8,16},{12,20},{16,8},{20,12},{24,0},{28,4},{1,25},{... | collective-permute-start | bytes 86024 | tf_op jit(solution)/shard_map/ppermute | solution.py:557
  17.9 1.3 %collective-permute-start.6 = (s16[112,128]{1,0:T(8,128)(2,1)S(1)}, s16[112,128]{1,0:T(8,128)(2,1)S(1)}, u32[]{:S(2)}, u32[]{:S(2)}) collective-permute-start(s16[112,128]{1,0:T(8,128)(2,1)S(1)} %get-tuple-element.52), channel_id=1, source_target_pairs={{0,8},{4,12},{8,0},{12,4},{16,24},{20,28},{24,16},{28,20},{1,9},{5... | collective-permute-start | bytes 86024 | tf_op jit(solution)/shard_map/ppermute | solution.py:557
  19.2 0.5 %collective-permute-start.7 = (s16[112,128]{1,0:T(8,128)(2,1)S(1)}, s16[112,128]{1,0:T(8,128)(2,1)S(1)}, u32[]{:S(2)}, u32[]{:S(2)}) collective-permute-start(s16[112,128]{1,0:T(8,128)(2,1)S(1)} %get-tuple-element.52), channel_id=1, source_target_pairs={{0,16},{4,20},{8,24},{12,28},{16,0},{20,4},{24,8},{28,12},{1,17},{... | collective-permute-start | bytes 86024 | tf_op jit(solution)/shard_map/ppermute | solution.py:557
  19.7 2.7 %base.1 = (f32[28,3,8,128]{3,2,1,0:T(8,128)S(1)}, f32[28,3,8,128]{3,2,1,0:T(8,128)S(1)}, f32[92,9,8,128]{3,2,1,0:T(8,128)S(1)}, f32[28,9,8,128]{3,2,1,0:T(8,128)...) custom-call(s32[1]{0:T(128)} %bitcast.parity, f32[8,128]{1,0:T(8,128)S(1)} %get-tuple-element.36.tables, ...), custom_call_target="tpu_custom_call" | custom-call | flops 3500000000 | tf_op jit(solution)/shard_map/base/pallas_call | solution.py:529
  22.5 0.0 collective-permute-done.5.rest_5_
  22.5 0.0 collective-permute-done.6.rest_1_
  22.5 0.5 %collective-permute-done.7.rest_3_ = s16[112,128]{1,0:T(8,128)(2,1)S(1)} collective-permute-done((s16[112,128]{1,0:T(8,128)(2,1)S(1)}, s16[112,128]{1,0:T(8,128)(2,1)S(1)}, u32[]{:S(2)}, u32[]{:S(2)}) %collective-permute-start.7) | collective-permute-done | bytes 28704 | tf_op jit(solution)/shard_map/ppermute | solution.py:557
  23.0 0.1 collective-permute-start.9
  23.1 1.5 %later.1.moves_later = f32[78,9,8,128]{3,2,1,0:T(8,128)S(1)} custom-call(f32[28,3,8,128]{3,2,1,0:T(8,128)S(1)} %get-tuple-element.45.coef, f32[28,3,8,128]{3,2,1,0:T(8,128)S(1)} %get-tuple-element.48.profile, f32[28,9,8,128]{3,2,1,0:T(8,128)S(1)} %get-tuple-element.49.electric, f32[28,9,8,128]{3,2,1,0:T(8,128)S(1)} %get-tuple-element.50.magnetic), custom_call_target="tpu_custom_call" | custom-call | flops 1500000000 | tf_op jit(solution)/shard_map/later/pallas_call | solution.py:529
  24.6 3.7 %tangent.1 = (f32[288,128]{1,0:T(8,128)}, f32[288,128]{1,0:T(8,128)}) custom-call(s32[1]{0:T(128)} %bitcast.parity, f32[28,3,8,128]{3,2,1,0:T(8,128)S(1)} %get-tuple-element.45.coef, f32[28,3,8,128]{3,2,1,0:T(8,128)S(1)} %get-tuple-element.46.gain, f32[92,9,8,128]{3,2,1,0:T(8,128)S(1)} %get-tuple-element.47.moves_first, ...), custom_call_target="tpu_custom_call" | custom-call | flops 4000000000 | tf_op jit(solution)/shard_map/tangent/pallas_call | solution.py:529
  (6 shorter events, 0.1 us)
Async XLA Ops:
  2.2 6.6 %collective-permute-start.3 = (s16[224,128]{1,0:T(8,128)(2,1)S(1)}, s16[224,128]{1,0:T(8,128)(2,1)S(1)}, u32[]{:S(2)}, u32[]{:S(2)}) collective-permute-start(s16[224,128]{1,0:T(8,128)(2,1)S(1)} %get-tuple-element.32), channel_id=1, source_target_pairs={{0,1},{1,0},{2,3},{3,2},{4,5},{5,4},{6,7},{7,6},{8,9},{9,8},{10,11... | collective-permute-start | bytes 172040 | tf_op jit(solution)/shard_map/ppermute | solution.py:560
  5.3 9.0 %collective-permute-start = (s16[688,128]{1,0:T(8,128)(2,1)S(1)}, s16[688,128]{1,0:T(8,128)(2,1)S(1)}, u32[]{:S(2)}, u32[]{:S(2)}) collective-permute-start(s16[688,128]{1,0:T(8,128)(2,1)S(1)} %get-tuple-element.38), channel_id=1, source_target_pairs={{0,24},{4,28},{8,16},{12,20},{16,8},{20,12},{24,0},{28,4},{1,25},{... | collective-permute-start | bytes 528392 | tf_op jit(solution)/shard_map/ppermute | solution.py:557
  7.8 8.1 %collective-permute-start.1 = (s16[688,128]{1,0:T(8,128)(2,1)S(1)}, s16[688,128]{1,0:T(8,128)(2,1)S(1)}, u32[]{:S(2)}, u32[]{:S(2)}) collective-permute-start(s16[688,128]{1,0:T(8,128)(2,1)S(1)} %get-tuple-element.38), channel_id=1, source_target_pairs={{0,8},{4,12},{8,0},{12,4},{16,24},{20,28},{24,16},{28,20},{1,9},{5... | collective-permute-start | bytes 528392 | tf_op jit(solution)/shard_map/ppermute | solution.py:557
  8.3 7.7 %collective-permute-start.2 = (s16[688,128]{1,0:T(8,128)(2,1)S(1)}, s16[688,128]{1,0:T(8,128)(2,1)S(1)}, u32[]{:S(2)}, u32[]{:S(2)}) collective-permute-start(s16[688,128]{1,0:T(8,128)(2,1)S(1)} %get-tuple-element.38), channel_id=1, source_target_pairs={{0,16},{4,20},{8,24},{12,28},{16,0},{20,4},{24,8},{28,12},{1,17},{... | collective-permute-start | bytes 528392 | tf_op jit(solution)/shard_map/ppermute | solution.py:557
  9.0 5.1 %collective-permute-start.4 = (s16[112,128]{1,0:T(8,128)(2,1)S(1)}, s16[112,128]{1,0:T(8,128)(2,1)S(1)}, u32[]{:S(2)}, u32[]{:S(2)}) collective-permute-start(s16[112,128]{1,0:T(8,128)(2,1)S(1)} %half.1), channel_id=1, source_target_pairs={{0,2},{1,3},{2,0},{3,1},{4,6},{5,7},{6,4},{7,5},{8,10},{9,11},{10,... | collective-permute-start | bytes 86024 | tf_op jit(solution)/shard_map/ppermute | solution.py:560
  16.1 3.6 %collective-permute-start.8 = (s16[2752,128]{1,0:T(8,128)(2,1)S(1)}, s16[2752,128]{1,0:T(8,128)(2,1)S(1)}, u32[]{:S(2)}, u32[]{:S(2)}) collective-permute-start(s16[2752,128]{1,0:T(8,128)(2,1)S(1)} %pad_add_fusion), channel_id=1, source_target_pairs={{0,4},{4,0},{8,12},{12,8},{16,20},{20,16},{24,28},{28,24},{1,5},{5... | collective-permute-start | bytes 2113544 | tf_op jit(solution)/shard_map/ppermute | solution.py:557
  16.1 6.3 %collective-permute-start.5 = (s16[112,128]{1,0:T(8,128)(2,1)S(1)}, s16[112,128]{1,0:T(8,128)(2,1)S(1)}, u32[]{:S(2)}, u32[]{:S(2)}) collective-permute-start(s16[112,128]{1,0:T(8,128)(2,1)S(1)} %get-tuple-element.52), channel_id=1, source_target_pairs={{0,24},{4,28},{8,16},{12,20},{16,8},{20,12},{24,0},{28,4},{1,25},{... | collective-permute-start | bytes 86024 | tf_op jit(solution)/shard_map/ppermute | solution.py:557
  17.9 4.6 %collective-permute-start.6 = (s16[112,128]{1,0:T(8,128)(2,1)S(1)}, s16[112,128]{1,0:T(8,128)(2,1)S(1)}, u32[]{:S(2)}, u32[]{:S(2)}) collective-permute-start(s16[112,128]{1,0:T(8,128)(2,1)S(1)} %get-tuple-element.52), channel_id=1, source_target_pairs={{0,8},{4,12},{8,0},{12,4},{16,24},{20,28},{24,16},{28,20},{1,9},{5... | collective-permute-start | bytes 86024 | tf_op jit(solution)/shard_map/ppermute | solution.py:557
  19.2 3.9 %collective-permute-start.7 = (s16[112,128]{1,0:T(8,128)(2,1)S(1)}, s16[112,128]{1,0:T(8,128)(2,1)S(1)}, u32[]{:S(2)}, u32[]{:S(2)}) collective-permute-start(s16[112,128]{1,0:T(8,128)(2,1)S(1)} %get-tuple-element.52), channel_id=1, source_target_pairs={{0,16},{4,20},{8,24},{12,28},{16,0},{20,4},{24,8},{28,12},{1,17},{... | collective-permute-start | bytes 86024 | tf_op jit(solution)/shard_map/ppermute | solution.py:557
  23.0 1.6 %collective-permute-start.9 = (s16[448,128]{1,0:T(8,128)(2,1)S(1)}, s16[448,128]{1,0:T(8,128)(2,1)S(1)}, u32[]{:S(2)}, u32[]{:S(2)}) collective-permute-start(s16[448,128]{1,0:T(8,128)(2,1)S(1)} %pad_add_fusion.1), channel_id=1, source_target_pairs={{0,4},{4,0},{8,12},{12,8},{16,20},{20,16},{24,28},{28,24},{1,5},{5... | collective-permute-start | bytes 344072 | tf_op jit(solution)/shard_map/ppermute | solution.py:557

commit v5 on v4

--- a/solution.py
+++ b/solution.py
@@ -107,16 +107,13 @@
     for copy in copies:
         copy.start()
     label_rows[plane:] = jnp.zeros((plane, 128), F32)
-    for copy in copies:
+    for copy in copies[:4]:
         copy.wait()
-    label_rows[:plane] = labels[...].astype(F32)
     for i in range(3):
         at = slice(i, i + 1)
         tables[at] = jnp.full((1, 128), DT_STEP * DT_STEP) / jnp.full((1, 128), levels[i])
         tables[slice(i + 3, i + 4)] = jnp.full((1, 128), gains[i]) / jnp.full((1, 128), levels[i])
     tables[6:8] = jnp.zeros((2, 128), F32)
-    heights_of = source_z[...].astype(F32)
-    amps_of = source_amp[...]
     low, lanes = iota(0) < GROUP, iota(1)
 
     blocks = kl.shape[0] // plane
@@ -137,6 +134,11 @@
         first = (plane + 16) * i + plane
         far_parts[first : first + 16] = narrow([codes[i]])
 
+    for copy in copies[4:]:
+        copy.wait()
+    label_rows[:plane] = labels[...].astype(F32)
+    heights_of = source_z[...].astype(F32)
+    amps_of = source_amp[...]
     info = jnp.zeros((TILE, 128), F32)
     rows = iota(0)
     for r in range(ratio):
@@ -600,8 +602,9 @@
         functools.partial(half_kernel, size), "half",
         (i16(plane + 16, nz),), [vmem] * 2, [], 0.2, (near_part, far_parts),
     )
+    near, far = gather(packed)
     near_part = over_mode(near_part, 2)
-    near, far = gather(packed)
+    *corners, near_part = lax.optimization_barrier((*far[1:], near_part))
 
     def with_core(near, far):
         got = near + far
@@ -616,8 +619,8 @@
         (i16(plane + 16, nz), f32(plane, nz)), [vmem] * 3, [pltpu.VMEM((3 * plane, nz), F32)],
         1.2, (own_part, far_parts, near_part),
     )
-    far, near, deps_packed = lax.optimization_barrier((far[::-1], near, deps_packed))
-    far = far[::-1]
+    *sides, middle, deps_packed = lax.optimization_barrier((*near[1:], far[0], deps_packed))
+    near, far = [packed, *sides], [middle, *corners]
     blocks = with_core(near, far)
     rows = ny + 2 * STEPS
     counts = [rows_of(step, ny)[1] - rows_of(step, ny)[0] for step in range(STEPS)]

time: 28.5 us -> 27.6 us (0.968)
  waiting for transfers between devices: 4.72 us -> 3.76 us
    ppermute x8, waiting for transfers between devices: 2.23 us -> 0.02 us  [over_xy(): return lax.ppermute(block, ('gx', 'gy'), route)]
    ppermute x2, starting transfers between devices: 5.74 us -> 4.23 us  [over_mode(): return lax.ppermute(block, 'mode', [(i, i ^ flip) for i in range(n_mode)])]
    ppermute x8, starting transfers between devices: 7.18 us -> 8.7 us  [over_xy(): return lax.ppermute(block, ('gx', 'gy'), route)]
    ppermute x2, waiting for transfers between devices: 2.49 us -> 3.74 us  [over_mode(): return lax.ppermute(block, 'mode', [(i, i ^ flip) for i in range(n_mode)])]
  transfers between devices with their start and end apart: 10 -> 10, of which waited for: 4 -> 2; matrix products, arithmetic and copies ran while one was open for 0% -> 0% of each run, Pallas kernels for 16% -> 17%
where the time goes in v5:
time: 27.6 us; the launch traced here: 27.4 us
  starting transfers between devices  12.9 us (47%)
  Pallas kernels  9.8 us (36%)
  waiting for transfers between devices  3.76 us (14%)
  between operations  0.78 us (3%)
    pallas_call x6, Pallas kernels, call(): pl.pallas_call(kernel, out_shape=outs, in_specs=specs, out_specs=tuple((p...  9.8 us
    ppermute x8, starting transfers between devices, over_xy(): return lax.ppermute(block, ('gx', 'gy'), route)  8.7 us
    ppermute x2, starting transfers between devices, over_mode(): return lax.ppermute(block, 'mode', [(i, i ^ flip) for i in range(n_mode)])  4.23 us
    ppermute x2, waiting for transfers between devices, over_mode(): return lax.ppermute(block, 'mode', [(i, i ^ flip) for i in range(n_mode)])  3.74 us
  transfers between devices with their start and end apart: 10, of which 2 were waited for; matrix products, arithmetic and copies ran while one was open for 0% of the time, Pallas kernels for 17%

profile of v5, /device:TPU:0, one launch (start us, length us, event | category | flops | bytes accessed | tf_op | source)
XLA Modules:
  0.0 27.4 jit_solution(16086572957982299074)
XLA Ops:
  0.6 1.5 %pack.1 = (s16[688,128]{1,0:T(8,128)(2,1)S(1)}, f32[688,128]{1,0:T(8,128)S(1)}, f32[96,128]{1,0:T(8,128)S(1)}, f32[96,128]{1,0:T(8,128)S(1)}, f32[8,128]{1,0:T(8,128)S(1)}, /*index=5*/s16[224,128]{1,0:T(8,128)(2,1)S(1)}) custom-call(s32[1]{0:T(128)} %bitcast.1.me, s32[16]{0:T(128)} %modes_at.1, f32[3]{0:T(128)} %levels_at.1, f32[3]{0:T(128)} %gains_at.1, ...), custom_call_target="tpu_custom_call" | custom-call | flops 1500000000 | tf_op jit(solution)/shard_map/pack/pallas_call | solution.py:531
  2.2 4.0 %collective-permute-start.3 = (s16[688,128]{1,0:T(8,128)(2,1)S(1)}, s16[688,128]{1,0:T(8,128)(2,1)S(1)}, u32[]{:S(2)}, u32[]{:S(2)}) collective-permute-start(s16[688,128]{1,0:T(8,128)(2,1)S(1)} %get-tuple-element.30), channel_id=1, source_target_pairs={{0,24},{4,28},{8,16},{12,20},{16,8},{20,12},{24,0},{28,4},{1,25},{... | collective-permute-start | bytes 528392 | tf_op jit(solution)/shard_map/ppermute | solution.py:559
  6.1 1.6 %collective-permute-start.2 = (s16[224,128]{1,0:T(8,128)(2,1)S(1)}, s16[224,128]{1,0:T(8,128)(2,1)S(1)}, u32[]{:S(2)}, u32[]{:S(2)}) collective-permute-start(s16[224,128]{1,0:T(8,128)(2,1)S(1)} %get-tuple-element.32), channel_id=1, source_target_pairs={{0,1},{1,0},{2,3},{3,2},{4,5},{5,4},{6,7},{7,6},{8,9},{9,8},{10,11... | collective-permute-start | bytes 172040 | tf_op jit(solution)/shard_map/ppermute | solution.py:562
  7.7 0.5 %collective-permute-start = (s16[688,128]{1,0:T(8,128)(2,1)S(1)}, s16[688,128]{1,0:T(8,128)(2,1)S(1)}, u32[]{:S(2)}, u32[]{:S(2)}) collective-permute-start(s16[688,128]{1,0:T(8,128)(2,1)S(1)} %get-tuple-element.30), channel_id=1, source_target_pairs={{0,16},{4,20},{8,24},{12,28},{16,0},{20,4},{24,8},{28,12},{1,17},{... | collective-permute-start | bytes 528392 | tf_op jit(solution)/shard_map/ppermute | solution.py:559
  8.2 0.5 %collective-permute-start.1 = (s16[688,128]{1,0:T(8,128)(2,1)S(1)}, s16[688,128]{1,0:T(8,128)(2,1)S(1)}, u32[]{:S(2)}, u32[]{:S(2)}) collective-permute-start(s16[688,128]{1,0:T(8,128)(2,1)S(1)} %get-tuple-element.30), channel_id=1, source_target_pairs={{0,8},{4,12},{8,0},{12,4},{16,24},{20,28},{24,16},{28,20},{1,9},{5... | collective-permute-start | bytes 528392 | tf_op jit(solution)/shard_map/ppermute | solution.py:559
  8.8 1.6 %collective-permute-done.2.far_parts = s16[224,128]{1,0:T(8,128)(2,1)S(1)} collective-permute-done((s16[224,128]{1,0:T(8,128)(2,1)S(1)}, s16[224,128]{1,0:T(8,128)(2,1)S(1)}, u32[]{:S(2)}, u32[]{:S(2)}) %collective-permute-start.2) | collective-permute-done | bytes 57376 | tf_op jit(solution)/shard_map/ppermute | solution.py:562
  10.3 0.2 half.1
  10.5 2.7 %collective-permute-start.4 = (s16[112,128]{1,0:T(8,128)(2,1)S(1)}, s16[112,128]{1,0:T(8,128)(2,1)S(1)}, u32[]{:S(2)}, u32[]{:S(2)}) collective-permute-start(s16[112,128]{1,0:T(8,128)(2,1)S(1)} %half.1), channel_id=1, source_target_pairs={{0,2},{1,3},{2,0},{3,1},{4,6},{5,7},{6,4},{7,5},{8,10},{9,11},{10,... | collective-permute-start | bytes 86024 | tf_op jit(solution)/shard_map/ppermute | solution.py:562
  13.1 2.2 %collective-permute-done.4.near_part = s16[112,128]{1,0:T(8,128)(2,1)S(1)} collective-permute-done((s16[112,128]{1,0:T(8,128)(2,1)S(1)}, s16[112,128]{1,0:T(8,128)(2,1)S(1)}, u32[]{:S(2)}, u32[]{:S(2)}) %collective-permute-start.4) | collective-permute-done | bytes 28704 | tf_op jit(solution)/shard_map/ppermute | solution.py:562
  15.3 0.0 collective-permute-done.3.rest_5_
  15.3 0.2 sum.1
  15.5 0.0 collective-permute-done.rest_3_
  15.6 0.1 collective-permute-start.8
  15.7 1.5 %collective-permute-start.5 = (s16[112,128]{1,0:T(8,128)(2,1)S(1)}, s16[112,128]{1,0:T(8,128)(2,1)S(1)}, u32[]{:S(2)}, u32[]{:S(2)}) collective-permute-start(s16[112,128]{1,0:T(8,128)(2,1)S(1)} %get-tuple-element.52), channel_id=1, source_target_pairs={{0,24},{4,28},{8,16},{12,20},{16,8},{20,12},{24,0},{28,4},{1,25},{... | collective-permute-start | bytes 86024 | tf_op jit(solution)/shard_map/ppermute | solution.py:559
  17.2 0.6 %collective-permute-start.6 = (s16[112,128]{1,0:T(8,128)(2,1)S(1)}, s16[112,128]{1,0:T(8,128)(2,1)S(1)}, u32[]{:S(2)}, u32[]{:S(2)}) collective-permute-start(s16[112,128]{1,0:T(8,128)(2,1)S(1)} %get-tuple-element.52), channel_id=1, source_target_pairs={{0,8},{4,12},{8,0},{12,4},{16,24},{20,28},{24,16},{28,20},{1,9},{5... | collective-permute-start | bytes 86024 | tf_op jit(solution)/shard_map/ppermute | solution.py:559
  17.8 1.4 %collective-permute-start.7 = (s16[112,128]{1,0:T(8,128)(2,1)S(1)}, s16[112,128]{1,0:T(8,128)(2,1)S(1)}, u32[]{:S(2)}, u32[]{:S(2)}) collective-permute-start(s16[112,128]{1,0:T(8,128)(2,1)S(1)} %get-tuple-element.52), channel_id=1, source_target_pairs={{0,16},{4,20},{8,24},{12,28},{16,0},{20,4},{24,8},{28,12},{1,17},{... | collective-permute-start | bytes 86024 | tf_op jit(solution)/shard_map/ppermute | solution.py:559
  19.2 0.0 collective-permute-done.8
  19.3 2.7 %base.1 = (f32[28,3,8,128]{3,2,1,0:T(8,128)S(1)}, f32[28,3,8,128]{3,2,1,0:T(8,128)S(1)}, f32[92,9,8,128]{3,2,1,0:T(8,128)S(1)}, f32[28,9,8,128]{3,2,1,0:T(8,128)...) custom-call(s32[1]{0:T(128)} %bitcast.parity, f32[8,128]{1,0:T(8,128)S(1)} %get-tuple-element.37.tables, ...), custom_call_target="tpu_custom_call" | custom-call | flops 3500000000 | tf_op jit(solution)/shard_map/base/pallas_call | solution.py:531
  22.0 0.0 collective-permute-done.6.rest_1_
  22.0 0.0 collective-permute-done.7.rest_3_
  22.1 0.1 collective-permute-start.9
  22.2 1.5 %later.1.moves_later = f32[78,9,8,128]{3,2,1,0:T(8,128)S(1)} custom-call(f32[28,3,8,128]{3,2,1,0:T(8,128)S(1)} %get-tuple-element.45.coef, f32[28,3,8,128]{3,2,1,0:T(8,128)S(1)} %get-tuple-element.48.profile, f32[28,9,8,128]{3,2,1,0:T(8,128)S(1)} %get-tuple-element.49.electric, f32[28,9,8,128]{3,2,1,0:T(8,128)S(1)} %get-tuple-element.50.magnetic), custom_call_target="tpu_custom_call" | custom-call | flops 1500000000 | tf_op jit(solution)/shard_map/later/pallas_call | solution.py:531
  23.6 0.0 collective-permute-done.9
  23.7 3.7 %tangent.1 = (f32[288,128]{1,0:T(8,128)}, f32[288,128]{1,0:T(8,128)}) custom-call(s32[1]{0:T(128)} %bitcast.parity, f32[28,3,8,128]{3,2,1,0:T(8,128)S(1)} %get-tuple-element.45.coef, f32[28,3,8,128]{3,2,1,0:T(8,128)S(1)} %get-tuple-element.46.gain, f32[92,9,8,128]{3,2,1,0:T(8,128)S(1)} %get-tuple-element.47.moves_first, ...), custom_call_target="tpu_custom_call" | custom-call | flops 4000000000 | tf_op jit(solution)/shard_map/tangent/pallas_call | solution.py:531
  (6 shorter events, 0.1 us)
Async XLA Ops:
  2.2 13.1 %collective-permute-start.3 = (s16[688,128]{1,0:T(8,128)(2,1)S(1)}, s16[688,128]{1,0:T(8,128)(2,1)S(1)}, u32[]{:S(2)}, u32[]{:S(2)}) collective-permute-start(s16[688,128]{1,0:T(8,128)(2,1)S(1)} %get-tuple-element.30), channel_id=1, source_target_pairs={{0,24},{4,28},{8,16},{12,20},{16,8},{20,12},{24,0},{28,4},{1,25},{... | collective-permute-start | bytes 528392 | tf_op jit(solution)/shard_map/ppermute | solution.py:559
  6.1 4.2 %collective-permute-start.2 = (s16[224,128]{1,0:T(8,128)(2,1)S(1)}, s16[224,128]{1,0:T(8,128)(2,1)S(1)}, u32[]{:S(2)}, u32[]{:S(2)}) collective-permute-start(s16[224,128]{1,0:T(8,128)(2,1)S(1)} %get-tuple-element.32), channel_id=1, source_target_pairs={{0,1},{1,0},{2,3},{3,2},{4,5},{5,4},{6,7},{7,6},{8,9},{9,8},{10,11... | collective-permute-start | bytes 172040 | tf_op jit(solution)/shard_map/ppermute | solution.py:562
  7.7 7.8 %collective-permute-start = (s16[688,128]{1,0:T(8,128)(2,1)S(1)}, s16[688,128]{1,0:T(8,128)(2,1)S(1)}, u32[]{:S(2)}, u32[]{:S(2)}) collective-permute-start(s16[688,128]{1,0:T(8,128)(2,1)S(1)} %get-tuple-element.30), channel_id=1, source_target_pairs={{0,16},{4,20},{8,24},{12,28},{16,0},{20,4},{24,8},{28,12},{1,17},{... | collective-permute-start | bytes 528392 | tf_op jit(solution)/shard_map/ppermute | solution.py:559
  8.2 7.3 %collective-permute-start.1 = (s16[688,128]{1,0:T(8,128)(2,1)S(1)}, s16[688,128]{1,0:T(8,128)(2,1)S(1)}, u32[]{:S(2)}, u32[]{:S(2)}) collective-permute-start(s16[688,128]{1,0:T(8,128)(2,1)S(1)} %get-tuple-element.30), channel_id=1, source_target_pairs={{0,8},{4,12},{8,0},{12,4},{16,24},{20,28},{24,16},{28,20},{1,9},{5... | collective-permute-start | bytes 528392 | tf_op jit(solution)/shard_map/ppermute | solution.py:559
  10.5 4.8 %collective-permute-start.4 = (s16[112,128]{1,0:T(8,128)(2,1)S(1)}, s16[112,128]{1,0:T(8,128)(2,1)S(1)}, u32[]{:S(2)}, u32[]{:S(2)}) collective-permute-start(s16[112,128]{1,0:T(8,128)(2,1)S(1)} %half.1), channel_id=1, source_target_pairs={{0,2},{1,3},{2,0},{3,1},{4,6},{5,7},{6,4},{7,5},{8,10},{9,11},{10,... | collective-permute-start | bytes 86024 | tf_op jit(solution)/shard_map/ppermute | solution.py:562
  15.6 3.6 %collective-permute-start.8 = (s16[2752,128]{1,0:T(8,128)(2,1)S(1)}, s16[2752,128]{1,0:T(8,128)(2,1)S(1)}, u32[]{:S(2)}, u32[]{:S(2)}) collective-permute-start(s16[2752,128]{1,0:T(8,128)(2,1)S(1)} %pad_add_fusion), channel_id=1, source_target_pairs={{0,4},{4,0},{8,12},{12,8},{16,20},{20,16},{24,28},{28,24},{1,5},{5... | collective-permute-start | bytes 2113544 | tf_op jit(solution)/shard_map/ppermute | solution.py:559
  15.7 6.3 %collective-permute-start.5 = (s16[112,128]{1,0:T(8,128)(2,1)S(1)}, s16[112,128]{1,0:T(8,128)(2,1)S(1)}, u32[]{:S(2)}, u32[]{:S(2)}) collective-permute-start(s16[112,128]{1,0:T(8,128)(2,1)S(1)} %get-tuple-element.52), channel_id=1, source_target_pairs={{0,24},{4,28},{8,16},{12,20},{16,8},{20,12},{24,0},{28,4},{1,25},{... | collective-permute-start | bytes 86024 | tf_op jit(solution)/shard_map/ppermute | solution.py:559
  17.2 4.8 %collective-permute-start.6 = (s16[112,128]{1,0:T(8,128)(2,1)S(1)}, s16[112,128]{1,0:T(8,128)(2,1)S(1)}, u32[]{:S(2)}, u32[]{:S(2)}) collective-permute-start(s16[112,128]{1,0:T(8,128)(2,1)S(1)} %get-tuple-element.52), channel_id=1, source_target_pairs={{0,8},{4,12},{8,0},{12,4},{16,24},{20,28},{24,16},{28,20},{1,9},{5... | collective-permute-start | bytes 86024 | tf_op jit(solution)/shard_map/ppermute | solution.py:559
  17.8 4.2 %collective-permute-start.7 = (s16[112,128]{1,0:T(8,128)(2,1)S(1)}, s16[112,128]{1,0:T(8,128)(2,1)S(1)}, u32[]{:S(2)}, u32[]{:S(2)}) collective-permute-start(s16[112,128]{1,0:T(8,128)(2,1)S(1)} %get-tuple-element.52), channel_id=1, source_target_pairs={{0,16},{4,20},{8,24},{12,28},{16,0},{20,4},{24,8},{28,12},{1,17},{... | collective-permute-start | bytes 86024 | tf_op jit(solution)/shard_map/ppermute | solution.py:559
  22.1 1.6 %collective-permute-start.9 = (s16[448,128]{1,0:T(8,128)(2,1)S(1)}, s16[448,128]{1,0:T(8,128)(2,1)S(1)}, u32[]{:S(2)}, u32[]{:S(2)}) collective-permute-start(s16[448,128]{1,0:T(8,128)(2,1)S(1)} %pad_add_fusion.1), channel_id=1, source_target_pairs={{0,4},{4,0},{8,12},{12,8},{16,20},{20,16},{24,28},{28,24},{1,5},{5... | collective-permute-start | bytes 344072 | tf_op jit(solution)/shard_map/ppermute | solution.py:559

commit v6 on v5

--- a/solution.py
+++ b/solution.py
@@ -61,17 +61,17 @@
     return narrow(coded), codes
 
 
-def decoded(part, at, plane, k):
-    scales = scale_of(wide(part[at + plane : at + plane + 16]))
+def decoded(part, at, scales, k):
     coded = wide(part[at + 16 * k : at + 16 * k + 16])
     return [coded[TILE * i : TILE * i + TILE] * scales[2 * k + i : 2 * k + i + 1] for i in range(2)]
 
 
-def half_kernel(size, near_part, far_parts, part):
+def half_kernel(size, near_part, far_parts, part, scales):
     plane = size[0] * size[1]
     codes = jnp.zeros((16, 128), F32)
+    scales[...] = scale_of(wide(far_parts[2 * plane + 16 :]))
     for k in range(plane // 16):
-        total = near_part[16 * k : 16 * k + 16] + jnp.concatenate(decoded(far_parts, plane + 16, plane, k), 0)
+        total = near_part[16 * k : 16 * k + 16] + jnp.concatenate(decoded(far_parts, plane + 16, scales, k), 0)
         part[16 * k : 16 * k + 16], codes = code_tiles(total, k, codes)
     part[plane:] = narrow([codes])
 
@@ -182,13 +182,15 @@
     own[last : last + 16] = jnp.where(lanes16 < ny, sources, pltpu.roll(sources, 128 - 2 * ny, 1))
 
 
-def sum_kernel(size, own_part, far_parts, near_part, packed, own, total):
+def sum_kernel(size, own_part, far_parts, near_part, packed, own, total, far_scales, near_scales):
     nx, ny = size
     ratio, plane, stride = nx // GROUP, nx * ny, nx // GROUP * ny
+    far_scales[...] = scale_of(wide(far_parts[plane : plane + 16]))
+    near_scales[...] = scale_of(wide(near_part[plane:]))
     total[:plane] = jnp.zeros((plane, 128), F32)
     total[2 * plane :] = jnp.zeros((plane, 128), F32)
     for k in range(plane // 16):
-        both = zip(decoded(far_parts, 0, plane, k), decoded(near_part, 0, plane, k))
+        both = zip(decoded(far_parts, 0, far_scales, k), decoded(near_part, 0, near_scales, k))
         for i, (far, near) in enumerate(both):
             at = 16 * k + TILE * i
             total[plane + at : plane + at + TILE] = own_part[at : at + TILE] + far + near
@@ -438,10 +440,11 @@
     ratio, plane = nx // GROUP, nx * ny
     n_blocks = 4 * len(set(order)) - 1
     blocks, rest = (own,) + rest[:n_blocks], rest[n_blocks:]
-    out_e, out_h, electric, magnetic, weight = rest
+    out_e, out_h, electric, magnetic, weight, scales = rest
     low = iota(0) < GROUP
 
-    scales = [None if i == 0 else scale_of(wide(b[plane : plane + 16])) for i, b in enumerate(blocks)]
+    for i, block in enumerate(blocks[1:]):
+        scales[16 * i : 16 * i + 16] = scale_of(wide(block[plane : plane + 16]))
 
     def unpack(y_block, pair, to, wanted):
         loaded = {}
@@ -458,7 +461,8 @@
                     at = TILE * unit // 16 * 16
                     both = wide(blocks[i][at : at + 16])
                     half = TILE * unit - at
-                    tiles.append(both[half : half + TILE] * scales[i][unit : unit + 1])
+                    row = 16 * (i - 1) + unit
+                    tiles.append(both[half : half + TILE] * scales[row : row + 1])
             loaded[x_block] = tiles
         for r in range(ratio):
             outs = [
@@ -600,7 +604,7 @@
     far_parts = over_mode(far_parts, 1)
     (near_part,) = call(
         functools.partial(half_kernel, size), "half",
-        (i16(plane + 16, nz),), [vmem] * 2, [], 0.2, (near_part, far_parts),
+        (i16(plane + 16, nz),), [vmem] * 2, [pltpu.VMEM((16, nz), F32)], 0.2, (near_part, far_parts),
     )
     near, far = gather(packed)
     near_part = over_mode(near_part, 2)
@@ -616,7 +620,8 @@
 
     deps_packed, deps_own = call(
         functools.partial(sum_kernel, size), "sum",
-        (i16(plane + 16, nz), f32(plane, nz)), [vmem] * 3, [pltpu.VMEM((3 * plane, nz), F32)],
+        (i16(plane + 16, nz), f32(plane, nz)), [vmem] * 3,
+        [pltpu.VMEM((3 * plane, nz), F32)] + [pltpu.VMEM((16, nz), F32)] * 2,
         1.2, (own_part, far_parts, near_part),
     )
     *sides, middle, deps_packed = lax.optimization_barrier((*near[1:], far[0], deps_packed))
@@ -647,7 +652,8 @@
         functools.partial(tangent_kernel, size, order), "tangent",
         (f32(3 * plane, nz), f32(3 * plane, nz)),
         [smem] + [vmem] * (4 + len(deps)),
-        [pltpu.VMEM(field_shape, F32)] * 2 + [pltpu.VMEM(plane_shape, F32)],
+        [pltpu.VMEM(field_shape, F32)] * 2
+        + [pltpu.VMEM(plane_shape, F32), pltpu.VMEM((16 * (len(deps) - 1), nz), F32)],
         4.0, (parity, coef, gain, moves_first, moves_later, deps_own, *deps[1:]),
     )
     shape = (1, 3, nx, ny, nz)

time: 27.6 us -> 27.6 us (level)
  no operation moved by 1% of the time
where the time goes in v6:
time: 27.6 us; the launch traced here: 27.4 us
  starting transfers between devices  12.9 us (47%)
  Pallas kernels  9.86 us (36%)
  waiting for transfers between devices  3.76 us (14%)
  between operations  0.78 us (3%)
    pallas_call x6, Pallas kernels, call(): pl.pallas_call(kernel, out_shape=outs, in_specs=specs, out_specs=tuple((p...  9.86 us
    ppermute x8, starting transfers between devices, over_xy(): return lax.ppermute(block, ('gx', 'gy'), route)  8.7 us
    ppermute x2, starting transfers between devices, over_mode(): return lax.ppermute(block, 'mode', [(i, i ^ flip) for i in range(n_mode)])  4.23 us
    ppermute x2, waiting for transfers between devices, over_mode(): return lax.ppermute(block, 'mode', [(i, i ^ flip) for i in range(n_mode)])  3.74 us
  transfers between devices with their start and end apart: 10, of which 2 were waited for; matrix products, arithmetic and copies ran while one was open for 0% of the time, Pallas kernels for 17%

profile of v6, /device:TPU:0, one launch (start us, length us, event | category | flops | bytes accessed | tf_op | source)
XLA Modules:
  0.0 27.4 jit_solution(7929505914758179290)
XLA Ops:
  0.6 1.5 %pack.1 = (s16[688,128]{1,0:T(8,128)(2,1)S(1)}, f32[688,128]{1,0:T(8,128)S(1)}, f32[96,128]{1,0:T(8,128)S(1)}, f32[96,128]{1,0:T(8,128)S(1)}, f32[8,128]{1,0:T(8,128)S(1)}, /*index=5*/s16[224,128]{1,0:T(8,128)(2,1)S(1)}) custom-call(s32[1]{0:T(128)} %bitcast.1.me, s32[16]{0:T(128)} %modes_at.1, f32[3]{0:T(128)} %levels_at.1, f32[3]{0:T(128)} %gains_at.1, ...), custom_call_target="tpu_custom_call" | custom-call | flops 1500000000 | tf_op jit(solution)/shard_map/pack/pallas_call | solution.py:535
  2.2 4.0 %collective-permute-start.3 = (s16[688,128]{1,0:T(8,128)(2,1)S(1)}, s16[688,128]{1,0:T(8,128)(2,1)S(1)}, u32[]{:S(2)}, u32[]{:S(2)}) collective-permute-start(s16[688,128]{1,0:T(8,128)(2,1)S(1)} %get-tuple-element.30), channel_id=1, source_target_pairs={{0,24},{4,28},{8,16},{12,20},{16,8},{20,12},{24,0},{28,4},{1,25},{... | collective-permute-start | bytes 528392 | tf_op jit(solution)/shard_map/ppermute | solution.py:563
  6.1 1.6 %collective-permute-start.2 = (s16[224,128]{1,0:T(8,128)(2,1)S(1)}, s16[224,128]{1,0:T(8,128)(2,1)S(1)}, u32[]{:S(2)}, u32[]{:S(2)}) collective-permute-start(s16[224,128]{1,0:T(8,128)(2,1)S(1)} %get-tuple-element.32), channel_id=1, source_target_pairs={{0,1},{1,0},{2,3},{3,2},{4,5},{5,4},{6,7},{7,6},{8,9},{9,8},{10,11... | collective-permute-start | bytes 172040 | tf_op jit(solution)/shard_map/ppermute | solution.py:566
  7.7 0.5 %collective-permute-start = (s16[688,128]{1,0:T(8,128)(2,1)S(1)}, s16[688,128]{1,0:T(8,128)(2,1)S(1)}, u32[]{:S(2)}, u32[]{:S(2)}) collective-permute-start(s16[688,128]{1,0:T(8,128)(2,1)S(1)} %get-tuple-element.30), channel_id=1, source_target_pairs={{0,16},{4,20},{8,24},{12,28},{16,0},{20,4},{24,8},{28,12},{1,17},{... | collective-permute-start | bytes 528392 | tf_op jit(solution)/shard_map/ppermute | solution.py:563
  8.2 0.5 %collective-permute-start.1 = (s16[688,128]{1,0:T(8,128)(2,1)S(1)}, s16[688,128]{1,0:T(8,128)(2,1)S(1)}, u32[]{:S(2)}, u32[]{:S(2)}) collective-permute-start(s16[688,128]{1,0:T(8,128)(2,1)S(1)} %get-tuple-element.30), channel_id=1, source_target_pairs={{0,8},{4,12},{8,0},{12,4},{16,24},{20,28},{24,16},{28,20},{1,9},{5... | collective-permute-start | bytes 528392 | tf_op jit(solution)/shard_map/ppermute | solution.py:563
  8.8 1.6 %collective-permute-done.2.far_parts = s16[224,128]{1,0:T(8,128)(2,1)S(1)} collective-permute-done((s16[224,128]{1,0:T(8,128)(2,1)S(1)}, s16[224,128]{1,0:T(8,128)(2,1)S(1)}, u32[]{:S(2)}, u32[]{:S(2)}) %collective-permute-start.2) | collective-permute-done | bytes 57376 | tf_op jit(solution)/shard_map/ppermute | solution.py:566
  10.3 0.2 half.1
  10.5 2.7 %collective-permute-start.4 = (s16[112,128]{1,0:T(8,128)(2,1)S(1)}, s16[112,128]{1,0:T(8,128)(2,1)S(1)}, u32[]{:S(2)}, u32[]{:S(2)}) collective-permute-start(s16[112,128]{1,0:T(8,128)(2,1)S(1)} %half.1), channel_id=1, source_target_pairs={{0,2},{1,3},{2,0},{3,1},{4,6},{5,7},{6,4},{7,5},{8,10},{9,11},{10,... | collective-permute-start | bytes 86024 | tf_op jit(solution)/shard_map/ppermute | solution.py:566
  13.1 2.2 %collective-permute-done.4.near_part = s16[112,128]{1,0:T(8,128)(2,1)S(1)} collective-permute-done((s16[112,128]{1,0:T(8,128)(2,1)S(1)}, s16[112,128]{1,0:T(8,128)(2,1)S(1)}, u32[]{:S(2)}, u32[]{:S(2)}) %collective-permute-start.4) | collective-permute-done | bytes 28704 | tf_op jit(solution)/shard_map/ppermute | solution.py:566
  15.3 0.0 collective-permute-done.3.rest_5_
  15.3 0.2 sum.1
  15.5 0.0 collective-permute-done.rest_3_
  15.6 0.1 collective-permute-start.8
  15.7 1.5 %collective-permute-start.5 = (s16[112,128]{1,0:T(8,128)(2,1)S(1)}, s16[112,128]{1,0:T(8,128)(2,1)S(1)}, u32[]{:S(2)}, u32[]{:S(2)}) collective-permute-start(s16[112,128]{1,0:T(8,128)(2,1)S(1)} %get-tuple-element.52), channel_id=1, source_target_pairs={{0,24},{4,28},{8,16},{12,20},{16,8},{20,12},{24,0},{28,4},{1,25},{... | collective-permute-start | bytes 86024 | tf_op jit(solution)/shard_map/ppermute | solution.py:563
  17.2 0.6 %collective-permute-start.6 = (s16[112,128]{1,0:T(8,128)(2,1)S(1)}, s16[112,128]{1,0:T(8,128)(2,1)S(1)}, u32[]{:S(2)}, u32[]{:S(2)}) collective-permute-start(s16[112,128]{1,0:T(8,128)(2,1)S(1)} %get-tuple-element.52), channel_id=1, source_target_pairs={{0,8},{4,12},{8,0},{12,4},{16,24},{20,28},{24,16},{28,20},{1,9},{5... | collective-permute-start | bytes 86024 | tf_op jit(solution)/shard_map/ppermute | solution.py:563
  17.8 1.4 %collective-permute-start.7 = (s16[112,128]{1,0:T(8,128)(2,1)S(1)}, s16[112,128]{1,0:T(8,128)(2,1)S(1)}, u32[]{:S(2)}, u32[]{:S(2)}) collective-permute-start(s16[112,128]{1,0:T(8,128)(2,1)S(1)} %get-tuple-element.52), channel_id=1, source_target_pairs={{0,16},{4,20},{8,24},{12,28},{16,0},{20,4},{24,8},{28,12},{1,17},{... | collective-permute-start | bytes 86024 | tf_op jit(solution)/shard_map/ppermute | solution.py:563
  19.3 0.0 collective-permute-done.8
  19.3 2.7 %base.1 = (f32[28,3,8,128]{3,2,1,0:T(8,128)S(1)}, f32[28,3,8,128]{3,2,1,0:T(8,128)S(1)}, f32[92,9,8,128]{3,2,1,0:T(8,128)S(1)}, f32[28,9,8,128]{3,2,1,0:T(8,128)...) custom-call(s32[1]{0:T(128)} %bitcast.parity, f32[8,128]{1,0:T(8,128)S(1)} %get-tuple-element.37.tables, ...), custom_call_target="tpu_custom_call" | custom-call | flops 3500000000 | tf_op jit(solution)/shard_map/base/pallas_call | solution.py:535
  22.1 0.0 collective-permute-done.6.rest_1_
  22.1 0.0 collective-permute-done.7.rest_3_
  22.1 0.1 collective-permute-start.9
  22.2 1.5 %later.1.moves_later = f32[78,9,8,128]{3,2,1,0:T(8,128)S(1)} custom-call(f32[28,3,8,128]{3,2,1,0:T(8,128)S(1)} %get-tuple-element.45.coef, f32[28,3,8,128]{3,2,1,0:T(8,128)S(1)} %get-tuple-element.48.profile, f32[28,9,8,128]{3,2,1,0:T(8,128)S(1)} %get-tuple-element.49.electric, f32[28,9,8,128]{3,2,1,0:T(8,128)S(1)} %get-tuple-element.50.magnetic), custom_call_target="tpu_custom_call" | custom-call | flops 1500000000 | tf_op jit(solution)/shard_map/later/pallas_call | solution.py:535
  23.6 0.0 collective-permute-done.9
  23.7 3.8 %tangent.1 = (f32[288,128]{1,0:T(8,128)}, f32[288,128]{1,0:T(8,128)}) custom-call(s32[1]{0:T(128)} %bitcast.parity, f32[28,3,8,128]{3,2,1,0:T(8,128)S(1)} %get-tuple-element.45.coef, f32[28,3,8,128]{3,2,1,0:T(8,128)S(1)} %get-tuple-element.46.gain, f32[92,9,8,128]{3,2,1,0:T(8,128)S(1)} %get-tuple-element.47.moves_first, ...), custom_call_target="tpu_custom_call" | custom-call | flops 4000000000 | tf_op jit(solution)/shard_map/tangent/pallas_call | solution.py:535
  (6 shorter events, 0.1 us)
Async XLA Ops:
  2.2 13.2 %collective-permute-start.3 = (s16[688,128]{1,0:T(8,128)(2,1)S(1)}, s16[688,128]{1,0:T(8,128)(2,1)S(1)}, u32[]{:S(2)}, u32[]{:S(2)}) collective-permute-start(s16[688,128]{1,0:T(8,128)(2,1)S(1)} %get-tuple-element.30), channel_id=1, source_target_pairs={{0,24},{4,28},{8,16},{12,20},{16,8},{20,12},{24,0},{28,4},{1,25},{... | collective-permute-start | bytes 528392 | tf_op jit(solution)/shard_map/ppermute | solution.py:563
  6.1 4.2 %collective-permute-start.2 = (s16[224,128]{1,0:T(8,128)(2,1)S(1)}, s16[224,128]{1,0:T(8,128)(2,1)S(1)}, u32[]{:S(2)}, u32[]{:S(2)}) collective-permute-start(s16[224,128]{1,0:T(8,128)(2,1)S(1)} %get-tuple-element.32), channel_id=1, source_target_pairs={{0,1},{1,0},{2,3},{3,2},{4,5},{5,4},{6,7},{7,6},{8,9},{9,8},{10,11... | collective-permute-start | bytes 172040 | tf_op jit(solution)/shard_map/ppermute | solution.py:566
  7.7 7.8 %collective-permute-start = (s16[688,128]{1,0:T(8,128)(2,1)S(1)}, s16[688,128]{1,0:T(8,128)(2,1)S(1)}, u32[]{:S(2)}, u32[]{:S(2)}) collective-permute-start(s16[688,128]{1,0:T(8,128)(2,1)S(1)} %get-tuple-element.30), channel_id=1, source_target_pairs={{0,16},{4,20},{8,24},{12,28},{16,0},{20,4},{24,8},{28,12},{1,17},{... | collective-permute-start | bytes 528392 | tf_op jit(solution)/shard_map/ppermute | solution.py:563
  8.2 7.3 %collective-permute-start.1 = (s16[688,128]{1,0:T(8,128)(2,1)S(1)}, s16[688,128]{1,0:T(8,128)(2,1)S(1)}, u32[]{:S(2)}, u32[]{:S(2)}) collective-permute-start(s16[688,128]{1,0:T(8,128)(2,1)S(1)} %get-tuple-element.30), channel_id=1, source_target_pairs={{0,8},{4,12},{8,0},{12,4},{16,24},{20,28},{24,16},{28,20},{1,9},{5... | collective-permute-start | bytes 528392 | tf_op jit(solution)/shard_map/ppermute | solution.py:563
  10.5 4.8 %collective-permute-start.4 = (s16[112,128]{1,0:T(8,128)(2,1)S(1)}, s16[112,128]{1,0:T(8,128)(2,1)S(1)}, u32[]{:S(2)}, u32[]{:S(2)}) collective-permute-start(s16[112,128]{1,0:T(8,128)(2,1)S(1)} %half.1), channel_id=1, source_target_pairs={{0,2},{1,3},{2,0},{3,1},{4,6},{5,7},{6,4},{7,5},{8,10},{9,11},{10,... | collective-permute-start | bytes 86024 | tf_op jit(solution)/shard_map/ppermute | solution.py:566
  15.6 3.6 %collective-permute-start.8 = (s16[2752,128]{1,0:T(8,128)(2,1)S(1)}, s16[2752,128]{1,0:T(8,128)(2,1)S(1)}, u32[]{:S(2)}, u32[]{:S(2)}) collective-permute-start(s16[2752,128]{1,0:T(8,128)(2,1)S(1)} %pad_add_fusion), channel_id=1, source_target_pairs={{0,4},{4,0},{8,12},{12,8},{16,20},{20,16},{24,28},{28,24},{1,5},{5... | collective-permute-start | bytes 2113544 | tf_op jit(solution)/shard_map/ppermute | solution.py:563
  15.7 6.3 %collective-permute-start.5 = (s16[112,128]{1,0:T(8,128)(2,1)S(1)}, s16[112,128]{1,0:T(8,128)(2,1)S(1)}, u32[]{:S(2)}, u32[]{:S(2)}) collective-permute-start(s16[112,128]{1,0:T(8,128)(2,1)S(1)} %get-tuple-element.52), channel_id=1, source_target_pairs={{0,24},{4,28},{8,16},{12,20},{16,8},{20,12},{24,0},{28,4},{1,25},{... | collective-permute-start | bytes 86024 | tf_op jit(solution)/shard_map/ppermute | solution.py:563
  17.2 4.8 %collective-permute-start.6 = (s16[112,128]{1,0:T(8,128)(2,1)S(1)}, s16[112,128]{1,0:T(8,128)(2,1)S(1)}, u32[]{:S(2)}, u32[]{:S(2)}) collective-permute-start(s16[112,128]{1,0:T(8,128)(2,1)S(1)} %get-tuple-element.52), channel_id=1, source_target_pairs={{0,8},{4,12},{8,0},{12,4},{16,24},{20,28},{24,16},{28,20},{1,9},{5... | collective-permute-start | bytes 86024 | tf_op jit(solution)/shard_map/ppermute | solution.py:563
  17.8 4.2 %collective-permute-start.7 = (s16[112,128]{1,0:T(8,128)(2,1)S(1)}, s16[112,128]{1,0:T(8,128)(2,1)S(1)}, u32[]{:S(2)}, u32[]{:S(2)}) collective-permute-start(s16[112,128]{1,0:T(8,128)(2,1)S(1)} %get-tuple-element.52), channel_id=1, source_target_pairs={{0,16},{4,20},{8,24},{12,28},{16,0},{20,4},{24,8},{28,12},{1,17},{... | collective-permute-start | bytes 86024 | tf_op jit(solution)/shard_map/ppermute | solution.py:563
  22.1 1.6 %collective-permute-start.9 = (s16[448,128]{1,0:T(8,128)(2,1)S(1)}, s16[448,128]{1,0:T(8,128)(2,1)S(1)}, u32[]{:S(2)}, u32[]{:S(2)}) collective-permute-start(s16[448,128]{1,0:T(8,128)(2,1)S(1)} %pad_add_fusion.1), channel_id=1, source_target_pairs={{0,4},{4,0},{8,12},{12,8},{16,20},{20,16},{24,28},{28,24},{1,5},{5... | collective-permute-start | bytes 344072 | tf_op jit(solution)/shard_map/ppermute | solution.py:563

commit v7 on v6

--- a/solution.py
+++ b/solution.py
@@ -18,7 +18,7 @@
 FINE = 256.0
 FIRST_STEPS = 4
 SCALE_AT = 4 * 8
-CHUNK = 13
+CHUNK = 26
 F32 = jnp.float32
 VMEM_LIMIT = 24 * 1024 * 1024
 

time: 27.6 us -> 27.8 us (level)
  no operation moved by 1% of the time
where the time goes in v7:
time: 27.8 us; the launch traced here: 27.6 us
  starting transfers between devices  12.9 us (46%)
  Pallas kernels  9.98 us (36%)
  waiting for transfers between devices  3.76 us (14%)
  between operations  0.78 us (3%)
    pallas_call x6, Pallas kernels, call(): pl.pallas_call(kernel, out_shape=outs, in_specs=specs, out_specs=tuple((p...  9.98 us
    ppermute x8, starting transfers between devices, over_xy(): return lax.ppermute(block, ('gx', 'gy'), route)  8.7 us
    ppermute x2, starting transfers between devices, over_mode(): return lax.ppermute(block, 'mode', [(i, i ^ flip) for i in range(n_mode)])  4.23 us
    ppermute x2, waiting for transfers between devices, over_mode(): return lax.ppermute(block, 'mode', [(i, i ^ flip) for i in range(n_mode)])  3.74 us
  transfers between devices with their start and end apart: 10, of which 2 were waited for; matrix products, arithmetic and copies ran while one was open for 0% of the time, Pallas kernels for 17%

profile of v7, /device:TPU:0, one launch (start us, length us, event | category | flops | bytes accessed | tf_op | source)
XLA Modules:
  0.0 27.6 jit_solution(8993310951292809374)
XLA Ops:
  0.6 1.5 %pack.1 = (s16[688,128]{1,0:T(8,128)(2,1)S(1)}, f32[688,128]{1,0:T(8,128)S(1)}, f32[96,128]{1,0:T(8,128)S(1)}, f32[96,128]{1,0:T(8,128)S(1)}, f32[8,128]{1,0:T(8,128)S(1)}, /*index=5*/s16[224,128]{1,0:T(8,128)(2,1)S(1)}) custom-call(s32[1]{0:T(128)} %bitcast.1.me, s32[16]{0:T(128)} %modes_at.1, f32[3]{0:T(128)} %levels_at.1, f32[3]{0:T(128)} %gains_at.1, ...), custom_call_target="tpu_custom_call" | custom-call | flops 1500000000 | tf_op jit(solution)/shard_map/pack/pallas_call | solution.py:535
  2.2 4.0 %collective-permute-start.3 = (s16[688,128]{1,0:T(8,128)(2,1)S(1)}, s16[688,128]{1,0:T(8,128)(2,1)S(1)}, u32[]{:S(2)}, u32[]{:S(2)}) collective-permute-start(s16[688,128]{1,0:T(8,128)(2,1)S(1)} %get-tuple-element.30), channel_id=1, source_target_pairs={{0,24},{4,28},{8,16},{12,20},{16,8},{20,12},{24,0},{28,4},{1,25},{... | collective-permute-start | bytes 528392 | tf_op jit(solution)/shard_map/ppermute | solution.py:563
  6.1 1.6 %collective-permute-start.2 = (s16[224,128]{1,0:T(8,128)(2,1)S(1)}, s16[224,128]{1,0:T(8,128)(2,1)S(1)}, u32[]{:S(2)}, u32[]{:S(2)}) collective-permute-start(s16[224,128]{1,0:T(8,128)(2,1)S(1)} %get-tuple-element.32), channel_id=1, source_target_pairs={{0,1},{1,0},{2,3},{3,2},{4,5},{5,4},{6,7},{7,6},{8,9},{9,8},{10,11... | collective-permute-start | bytes 172040 | tf_op jit(solution)/shard_map/ppermute | solution.py:566
  7.7 0.5 %collective-permute-start = (s16[688,128]{1,0:T(8,128)(2,1)S(1)}, s16[688,128]{1,0:T(8,128)(2,1)S(1)}, u32[]{:S(2)}, u32[]{:S(2)}) collective-permute-start(s16[688,128]{1,0:T(8,128)(2,1)S(1)} %get-tuple-element.30), channel_id=1, source_target_pairs={{0,16},{4,20},{8,24},{12,28},{16,0},{20,4},{24,8},{28,12},{1,17},{... | collective-permute-start | bytes 528392 | tf_op jit(solution)/shard_map/ppermute | solution.py:563
  8.2 0.5 %collective-permute-start.1 = (s16[688,128]{1,0:T(8,128)(2,1)S(1)}, s16[688,128]{1,0:T(8,128)(2,1)S(1)}, u32[]{:S(2)}, u32[]{:S(2)}) collective-permute-start(s16[688,128]{1,0:T(8,128)(2,1)S(1)} %get-tuple-element.30), channel_id=1, source_target_pairs={{0,8},{4,12},{8,0},{12,4},{16,24},{20,28},{24,16},{28,20},{1,9},{5... | collective-permute-start | bytes 528392 | tf_op jit(solution)/shard_map/ppermute | solution.py:563
  8.8 1.6 %collective-permute-done.2.far_parts = s16[224,128]{1,0:T(8,128)(2,1)S(1)} collective-permute-done((s16[224,128]{1,0:T(8,128)(2,1)S(1)}, s16[224,128]{1,0:T(8,128)(2,1)S(1)}, u32[]{:S(2)}, u32[]{:S(2)}) %collective-permute-start.2) | collective-permute-done | bytes 57376 | tf_op jit(solution)/shard_map/ppermute | solution.py:566
  10.3 0.2 half.1
  10.5 2.7 %collective-permute-start.4 = (s16[112,128]{1,0:T(8,128)(2,1)S(1)}, s16[112,128]{1,0:T(8,128)(2,1)S(1)}, u32[]{:S(2)}, u32[]{:S(2)}) collective-permute-start(s16[112,128]{1,0:T(8,128)(2,1)S(1)} %half.1), channel_id=1, source_target_pairs={{0,2},{1,3},{2,0},{3,1},{4,6},{5,7},{6,4},{7,5},{8,10},{9,11},{10,... | collective-permute-start | bytes 86024 | tf_op jit(solution)/shard_map/ppermute | solution.py:566
  13.1 2.2 %collective-permute-done.4.near_part = s16[112,128]{1,0:T(8,128)(2,1)S(1)} collective-permute-done((s16[112,128]{1,0:T(8,128)(2,1)S(1)}, s16[112,128]{1,0:T(8,128)(2,1)S(1)}, u32[]{:S(2)}, u32[]{:S(2)}) %collective-permute-start.4) | collective-permute-done | bytes 28704 | tf_op jit(solution)/shard_map/ppermute | solution.py:566
  15.3 0.0 collective-permute-done.3.rest_5_
  15.3 0.2 sum.1
  15.5 0.0 collective-permute-done.1.rest_1_
  15.6 0.1 collective-permute-start.8
  15.7 1.5 %collective-permute-start.5 = (s16[112,128]{1,0:T(8,128)(2,1)S(1)}, s16[112,128]{1,0:T(8,128)(2,1)S(1)}, u32[]{:S(2)}, u32[]{:S(2)}) collective-permute-start(s16[112,128]{1,0:T(8,128)(2,1)S(1)} %get-tuple-element.52), channel_id=1, source_target_pairs={{0,24},{4,28},{8,16},{12,20},{16,8},{20,12},{24,0},{28,4},{1,25},{... | collective-permute-start | bytes 86024 | tf_op jit(solution)/shard_map/ppermute | solution.py:563
  17.2 0.6 %collective-permute-start.6 = (s16[112,128]{1,0:T(8,128)(2,1)S(1)}, s16[112,128]{1,0:T(8,128)(2,1)S(1)}, u32[]{:S(2)}, u32[]{:S(2)}) collective-permute-start(s16[112,128]{1,0:T(8,128)(2,1)S(1)} %get-tuple-element.52), channel_id=1, source_target_pairs={{0,8},{4,12},{8,0},{12,4},{16,24},{20,28},{24,16},{28,20},{1,9},{5... | collective-permute-start | bytes 86024 | tf_op jit(solution)/shard_map/ppermute | solution.py:563
  17.8 1.4 %collective-permute-start.7 = (s16[112,128]{1,0:T(8,128)(2,1)S(1)}, s16[112,128]{1,0:T(8,128)(2,1)S(1)}, u32[]{:S(2)}, u32[]{:S(2)}) collective-permute-start(s16[112,128]{1,0:T(8,128)(2,1)S(1)} %get-tuple-element.52), channel_id=1, source_target_pairs={{0,16},{4,20},{8,24},{12,28},{16,0},{20,4},{24,8},{28,12},{1,17},{... | collective-permute-start | bytes 86024 | tf_op jit(solution)/shard_map/ppermute | solution.py:563
  19.3 0.0 collective-permute-done.8
  19.3 3.0 %base.1 = (f32[28,3,8,128]{3,2,1,0:T(8,128)S(1)}, f32[28,3,8,128]{3,2,1,0:T(8,128)S(1)}, f32[92,9,8,128]{3,2,1,0:T(8,128)S(1)}, f32[28,9,8,128]{3,2,1,0:T(8,128)...) custom-call(s32[1]{0:T(128)} %bitcast.parity, f32[8,128]{1,0:T(8,128)S(1)} %get-tuple-element.37.tables, ...), custom_call_target="tpu_custom_call" | custom-call | flops 3500000000 | tf_op jit(solution)/shard_map/base/pallas_call | solution.py:535
  22.3 0.0 collective-permute-done.5.rest_5_
  22.3 0.0 collective-permute-done.6.rest_1_
  22.3 0.1 collective-permute-start.9
  22.4 1.4 %later.1.moves_later = f32[78,9,8,128]{3,2,1,0:T(8,128)S(1)} custom-call(f32[28,3,8,128]{3,2,1,0:T(8,128)S(1)} %get-tuple-element.45.coef, f32[28,3,8,128]{3,2,1,0:T(8,128)S(1)} %get-tuple-element.48.profile, f32[28,9,8,128]{3,2,1,0:T(8,128)S(1)} %get-tuple-element.49.electric, f32[28,9,8,128]{3,2,1,0:T(8,128)S(1)} %get-tuple-element.50.magnetic), custom_call_target="tpu_custom_call" | custom-call | flops 1500000000 | tf_op jit(solution)/shard_map/later/pallas_call | solution.py:535
  23.8 0.0 collective-permute-done.9
  23.8 3.7 %tangent.1 = (f32[288,128]{1,0:T(8,128)}, f32[288,128]{1,0:T(8,128)}) custom-call(s32[1]{0:T(128)} %bitcast.parity, f32[28,3,8,128]{3,2,1,0:T(8,128)S(1)} %get-tuple-element.45.coef, f32[28,3,8,128]{3,2,1,0:T(8,128)S(1)} %get-tuple-element.46.gain, f32[92,9,8,128]{3,2,1,0:T(8,128)S(1)} %get-tuple-element.47.moves_first, ...), custom_call_target="tpu_custom_call" | custom-call | flops 4000000000 | tf_op jit(solution)/shard_map/tangent/pallas_call | solution.py:535
  (6 shorter events, 0.1 us)
Async XLA Ops:
  2.2 13.2 %collective-permute-start.3 = (s16[688,128]{1,0:T(8,128)(2,1)S(1)}, s16[688,128]{1,0:T(8,128)(2,1)S(1)}, u32[]{:S(2)}, u32[]{:S(2)}) collective-permute-start(s16[688,128]{1,0:T(8,128)(2,1)S(1)} %get-tuple-element.30), channel_id=1, source_target_pairs={{0,24},{4,28},{8,16},{12,20},{16,8},{20,12},{24,0},{28,4},{1,25},{... | collective-permute-start | bytes 528392 | tf_op jit(solution)/shard_map/ppermute | solution.py:563
  6.1 4.2 %collective-permute-start.2 = (s16[224,128]{1,0:T(8,128)(2,1)S(1)}, s16[224,128]{1,0:T(8,128)(2,1)S(1)}, u32[]{:S(2)}, u32[]{:S(2)}) collective-permute-start(s16[224,128]{1,0:T(8,128)(2,1)S(1)} %get-tuple-element.32), channel_id=1, source_target_pairs={{0,1},{1,0},{2,3},{3,2},{4,5},{5,4},{6,7},{7,6},{8,9},{9,8},{10,11... | collective-permute-start | bytes 172040 | tf_op jit(solution)/shard_map/ppermute | solution.py:566
  7.7 7.8 %collective-permute-start = (s16[688,128]{1,0:T(8,128)(2,1)S(1)}, s16[688,128]{1,0:T(8,128)(2,1)S(1)}, u32[]{:S(2)}, u32[]{:S(2)}) collective-permute-start(s16[688,128]{1,0:T(8,128)(2,1)S(1)} %get-tuple-element.30), channel_id=1, source_target_pairs={{0,16},{4,20},{8,24},{12,28},{16,0},{20,4},{24,8},{28,12},{1,17},{... | collective-permute-start | bytes 528392 | tf_op jit(solution)/shard_map/ppermute | solution.py:563
  8.2 7.3 %collective-permute-start.1 = (s16[688,128]{1,0:T(8,128)(2,1)S(1)}, s16[688,128]{1,0:T(8,128)(2,1)S(1)}, u32[]{:S(2)}, u32[]{:S(2)}) collective-permute-start(s16[688,128]{1,0:T(8,128)(2,1)S(1)} %get-tuple-element.30), channel_id=1, source_target_pairs={{0,8},{4,12},{8,0},{12,4},{16,24},{20,28},{24,16},{28,20},{1,9},{5... | collective-permute-start | bytes 528392 | tf_op jit(solution)/shard_map/ppermute | solution.py:563
  10.5 4.8 %collective-permute-start.4 = (s16[112,128]{1,0:T(8,128)(2,1)S(1)}, s16[112,128]{1,0:T(8,128)(2,1)S(1)}, u32[]{:S(2)}, u32[]{:S(2)}) collective-permute-start(s16[112,128]{1,0:T(8,128)(2,1)S(1)} %half.1), channel_id=1, source_target_pairs={{0,2},{1,3},{2,0},{3,1},{4,6},{5,7},{6,4},{7,5},{8,10},{9,11},{10,... | collective-permute-start | bytes 86024 | tf_op jit(solution)/shard_map/ppermute | solution.py:566
  15.6 3.6 %collective-permute-start.8 = (s16[2752,128]{1,0:T(8,128)(2,1)S(1)}, s16[2752,128]{1,0:T(8,128)(2,1)S(1)}, u32[]{:S(2)}, u32[]{:S(2)}) collective-permute-start(s16[2752,128]{1,0:T(8,128)(2,1)S(1)} %pad_add_fusion), channel_id=1, source_target_pairs={{0,4},{4,0},{8,12},{12,8},{16,20},{20,16},{24,28},{28,24},{1,5},{5... | collective-permute-start | bytes 2113544 | tf_op jit(solution)/shard_map/ppermute | solution.py:563
  15.7 6.6 %collective-permute-start.5 = (s16[112,128]{1,0:T(8,128)(2,1)S(1)}, s16[112,128]{1,0:T(8,128)(2,1)S(1)}, u32[]{:S(2)}, u32[]{:S(2)}) collective-permute-start(s16[112,128]{1,0:T(8,128)(2,1)S(1)} %get-tuple-element.52), channel_id=1, source_target_pairs={{0,24},{4,28},{8,16},{12,20},{16,8},{20,12},{24,0},{28,4},{1,25},{... | collective-permute-start | bytes 86024 | tf_op jit(solution)/shard_map/ppermute | solution.py:563
  17.2 5.1 %collective-permute-start.6 = (s16[112,128]{1,0:T(8,128)(2,1)S(1)}, s16[112,128]{1,0:T(8,128)(2,1)S(1)}, u32[]{:S(2)}, u32[]{:S(2)}) collective-permute-start(s16[112,128]{1,0:T(8,128)(2,1)S(1)} %get-tuple-element.52), channel_id=1, source_target_pairs={{0,8},{4,12},{8,0},{12,4},{16,24},{20,28},{24,16},{28,20},{1,9},{5... | collective-permute-start | bytes 86024 | tf_op jit(solution)/shard_map/ppermute | solution.py:563
  17.8 4.5 %collective-permute-start.7 = (s16[112,128]{1,0:T(8,128)(2,1)S(1)}, s16[112,128]{1,0:T(8,128)(2,1)S(1)}, u32[]{:S(2)}, u32[]{:S(2)}) collective-permute-start(s16[112,128]{1,0:T(8,128)(2,1)S(1)} %get-tuple-element.52), channel_id=1, source_target_pairs={{0,16},{4,20},{8,24},{12,28},{16,0},{20,4},{24,8},{28,12},{1,17},{... | collective-permute-start | bytes 86024 | tf_op jit(solution)/shard_map/ppermute | solution.py:563
  22.3 1.5 %collective-permute-start.9 = (s16[448,128]{1,0:T(8,128)(2,1)S(1)}, s16[448,128]{1,0:T(8,128)(2,1)S(1)}, u32[]{:S(2)}, u32[]{:S(2)}) collective-permute-start(s16[448,128]{1,0:T(8,128)(2,1)S(1)} %pad_add_fusion.1), channel_id=1, source_target_pairs={{0,4},{4,0},{8,12},{12,8},{16,20},{20,16},{24,28},{28,24},{1,5},{5... | collective-permute-start | bytes 344072 | tf_op jit(solution)/shard_map/ppermute | solution.py:563
